TPU v7x, 32 devices: a whole 2x2x4 slice. The times are simulated.
32 devices in a mesh: parts: 2 (over y), pool: 4 (over z), tp: 2 (over x), sp: 2 (over core).
Axes of the slice: x: 2, y: 2, z: 4, core: 2. Of those that a mesh axis runs over, the one named last changes fastest.
Arguments:
- queries: bfloat16 [8, 256, 36864], P(('parts', 'pool'), 'sp', 'tp'), parts along dimension 0, may hold values from -32 to 32
- block_latent: bfloat16 [8, 256, 576], P(('parts', 'pool'), ('tp', 'sp')), parts along dimension 0, may hold values from -6 to 6
- prefix_cache: bfloat16 [8, 128, 576], P('parts', 'pool'), parts along dimension 0, may hold values from -6 to 6
- queue_list: int32 [8], P('parts'), parts along dimension 0, may hold values from 0 to 3, each once
- prefix_len: int32 [8], P('parts'), parts along dimension 0, may hold values from 32 to 128, as said below
- block_len: int32 [8], P('parts'), parts along dimension 0, may hold values from 64 to 256, as said below
- decode_dest: int32 [8], P('parts'), parts along dimension 0, may hold values from 0 to 3, as said below
Outputs:
- latent_out: bfloat16 [8, 256, 32768], P(('parts', 'pool'), 'sp', 'tp'), parts along dimension 0
- decode_pages: bfloat16 [8, 2, 6, 64, 576], P(('parts', 'pool'), None, None, ('tp', 'sp')), parts along dimension 0
There are 2 independent parts, one for each index of `parts`. A program takes and returns all parts, laid end to end along the dimension named above; each array names one. Nothing has to cross between parts.
Inputs may be any that keep to these rules, and one draw needn't show every extreme that they name: `queue_list`: each request appears once. `prefix_len`: some request has exactly 128. `block_len`: some group has exactly 256. `decode_dest`: no decode group is named by more than 2 prefill groups, and some is named by exactly 2.
All inputs are finite; a program needn't handle non-finite values.
Results may differ from a plain program's by a relative error of at most 0.0034.
Values may be sent and summed in bfloat16 or wider, within the bound.
No kernel may reach another device: no remote copies, remote signals or barrier semaphores. Data moves between devices by JAX's collectives and lax.ppermute only.
A program may use at most 128 MiB of HBM per device.

v0:
```python
import jax
import jax.numpy as jnp
from jax import lax
from jax.sharding import PartitionSpec as P

LAT = 512
ROPE = 64
QK = 192
PG = 64
MOST = 2


def build_rows(pre_keys, new_keys, pre_length, blk_length, lane_index, lane_count):
    prefix_count = pre_keys.shape[0]
    key_width = pre_keys.shape[1]
    block_count = new_keys.shape[0]
    cache_len = prefix_count + block_count
    rows_lane = PG // lane_count
    padding = jnp.zeros((prefix_count, key_width), new_keys.dtype)
    padded = jnp.concatenate([padding, new_keys, padding], axis=0)
    shifted = lax.dynamic_slice_in_dim(padded, prefix_count - pre_length, cache_len, 0)
    shifted = shifted.reshape(cache_len // PG, lane_count, rows_lane, key_width)
    new_rows = lax.dynamic_index_in_dim(shifted, lane_index, 1, keepdims=False)
    pre_pages = pre_keys.reshape(prefix_count // PG, lane_count, rows_lane, key_width)
    pre_part = lax.dynamic_index_in_dim(pre_pages, lane_index, 1, keepdims=False)
    tail_zeros = jnp.zeros((block_count // PG, rows_lane, key_width), pre_keys.dtype)
    pre_rows = jnp.concatenate([pre_part, tail_zeros], axis=0)
    position = (
        jnp.arange(cache_len // PG, dtype=jnp.int32)[:, None] * PG
        + lane_index * rows_lane
        + jnp.arange(rows_lane, dtype=jnp.int32)[None, :]
    )
    offset = position - pre_length
    in_prefix = (position < pre_length)[:, :, None]
    in_new = ((offset >= 0) & (offset < blk_length))[:, :, None]
    blank_rows = jnp.zeros_like(new_rows)
    merged = jnp.where(in_prefix, pre_rows, jnp.where(in_new, new_rows, blank_rows))
    return merged.reshape(-1, key_width)


def attend(queries, pre_keys, new_keys, pre_length, blk_length, first_query):
    query_count = queries.shape[1]
    key_width = pre_keys.shape[1]
    heads_here = queries.shape[2] // key_width
    query_rows = queries.reshape(query_count * heads_here, key_width)
    contract = (((1,), (1,)), ((), ()))
    pre_scores = lax.dot_general(query_rows, pre_keys, contract, preferred_element_type=jnp.float32)
    new_scores = lax.dot_general(query_rows, new_keys, contract, preferred_element_type=jnp.float32)
    pre_scores = (pre_scores * QK ** (-0.5)).reshape(query_count, heads_here, pre_keys.shape[0])
    new_scores = (new_scores * QK ** (-0.5)).reshape(query_count, heads_here, new_keys.shape[0])
    pre_index = jnp.arange(pre_keys.shape[0], dtype=jnp.int32)
    new_index = jnp.arange(new_keys.shape[0], dtype=jnp.int32)
    query_index = first_query + jnp.arange(query_count, dtype=jnp.int32)
    pre_visible = (pre_index < pre_length)[None, None, :]
    new_visible = (
        (new_index[None, :] <= query_index[:, None]) & (new_index < blk_length)[None, :]
    )[:, None, :]
    pre_top = jnp.max(jnp.where(pre_visible, pre_scores, -jnp.inf), axis=2, keepdims=True)
    new_top = jnp.max(jnp.where(new_visible, new_scores, -jnp.inf), axis=2, keepdims=True)
    row_top = jnp.maximum(pre_top, new_top)
    pre_weights = jnp.where(pre_visible, jnp.exp(pre_scores - row_top), 0.0)
    new_weights = jnp.where(new_visible, jnp.exp(new_scores - row_top), 0.0)
    row_total = jnp.sum(pre_weights, axis=2, keepdims=True) + jnp.sum(
        new_weights, axis=2, keepdims=True
    )
    pre_probs = pre_weights.astype(jnp.bfloat16).reshape(query_count * heads_here, -1)
    new_probs = new_weights.astype(jnp.bfloat16).reshape(query_count * heads_here, -1)
    mixture = jnp.dot(pre_probs, pre_keys[:, :LAT], preferred_element_type=jnp.float32)
    mixture = mixture + jnp.dot(new_probs, new_keys[:, :LAT], preferred_element_type=jnp.float32)
    mixture = mixture.reshape(query_count, heads_here, LAT) / row_total
    live_rows = (query_index < blk_length)[:, None, None]
    return (
        jnp.where(live_rows, mixture, 0.0)
        .astype(jnp.bfloat16)
        .reshape(1, query_count, heads_here * LAT)
    )


def body(queries, block_latent, prefix_cache, queue_list, prefix_len, block_len, decode_dest):
    group_count = lax.axis_size("pool")
    lane_count = lax.axis_size("tp") * lax.axis_size("sp")
    group_index = lax.axis_index("pool")
    lane_index = lax.axis_index("tp") * lax.axis_size("sp") + lax.axis_index("sp")
    key_width = LAT + ROPE
    request = queue_list[group_index]
    pre_length = prefix_len[request]
    blk_length = block_len[group_index]
    chosen = jnp.take(prefix_cache, queue_list, axis=0)
    prefix_rows = lax.all_to_all(chosen, "pool", split_axis=0, concat_axis=1, tiled=True)
    new_rows = lax.all_gather(block_latent, ("tp", "sp"), axis=1, tiled=True)
    pre_keys = prefix_rows.reshape(-1, key_width)
    new_keys = new_rows.reshape(-1, key_width)
    cache_len = pre_keys.shape[0] + new_keys.shape[0]
    page_count = cache_len // PG
    rows_lane = PG // lane_count
    hit_table = (decode_dest[:, None] == jnp.arange(group_count, dtype=jnp.int32)[None, :]).astype(
        jnp.int32
    )
    rank_table = jnp.cumsum(hit_table, axis=0) - hit_table
    rank = jnp.sum(rank_table * hit_table, axis=1)
    first_query = lax.axis_index("sp") * queries.shape[1]
    latent_out = attend(queries, pre_keys, new_keys, pre_length, blk_length, first_query)
    lane_rows = build_rows(pre_keys, new_keys, pre_length, blk_length, lane_index, lane_count)
    flat = lane_rows.reshape(1, -1)
    picker = (
        (decode_dest == group_index)[None, :]
        & (rank[None, :] == jnp.arange(MOST, dtype=jnp.int32)[:, None])
    ).astype(jnp.bfloat16)
    landed = jnp.dot(
        picker, lax.all_gather(flat, "pool", axis=0, tiled=True), preferred_element_type=jnp.float32
    ).astype(jnp.bfloat16)
    decode_pages = landed.reshape(1, MOST, page_count, rows_lane, key_width)
    return (latent_out, decode_pages)


def solution(mesh):
    in_specs = (
        P(("parts", "pool"), "sp", "tp"),
        P(("parts", "pool"), ("tp", "sp"), None),
        P("parts", "pool", None),
        P("parts"),
        P("parts"),
        P("parts"),
        P("parts"),
    )
    out_specs = (
        P(("parts", "pool"), "sp", "tp"),
        P(("parts", "pool"), None, None, ("tp", "sp"), None),
    )
    return jax.shard_map(body, mesh=mesh, in_specs=in_specs, out_specs=out_specs, check_vma=False)
```

profile of v0, /device:TPU:0, one launch (start us, length us, event | category | flops | bytes accessed | tf_op | source)
XLA Modules:
  0.0 123.1 jit_solution(6778524940927139297)
XLA Ops:
  0.6 0.0 copy-start
  0.6 0.7 compare_and_fusion
  1.3 0.7 compare_select_fusion
  2.0 0.0 copy-done
  2.0 0.6 gather_fusion
  2.6 0.8 broadcast_select_fusion
  3.4 6.3 %all-to-all-start = ((bf16[4,32,576]{2,1,0:T(8,128)(2,1)}), bf16[4,32,576]{2,1,0:T(8,128)(2,1)S(1)}, u32[]{:S(2)}, u32[]{:S(2)}) async-start(bf16[4,32,576]{2,1,0:T(8,128)(2,1)} %broadcast_select_fusion), calls=%async_computation | async-start | bytes 327680 | tf_op jit(solution)/shard_map/all_to_all | solution.py:89
  9.7 1.2 %dynamic_slice.21 = s32[1]{0:T(128)} dynamic-slice(s32[4]{0:T(128)} %param.10, s32[]{:T(128)S(6)} %select_n.67), dynamic_slice_sizes={1} | dynamic-slice | bytes 12 | tf_op jit(solution)/shard_map/dynamic_slice | solution.py:85
  12.9 1.2 %dynamic_slice.22 = s32[1]{0:T(128)} dynamic-slice(s32[4]{0:T(128)} %param.11, s32[]{:T(128)S(6)} %select_n.68), dynamic_slice_sizes={1} | dynamic-slice | bytes 12 | tf_op jit(solution)/shard_map/dynamic_slice | solution.py:86
  14.7 0.7 iota_compare_fusion.3
  15.4 1.3 %dynamic_slice.20 = s32[1]{0:T(128)} dynamic-slice(s32[4]{0:T(128)} %param.12, s32[]{:T(128)S(6)} %select_n.67), dynamic_slice_sizes={1} | dynamic-slice | bytes 12 | tf_op jit(solution)/shard_map/dynamic_slice | solution.py:87
  16.7 0.7 iota_compare_fusion.2
  17.4 0.7 broadcast_compare_fusion.1
  18.8 1.4 %fusion.21 = (pred[6,16]{1,0:T(8,128)(4,1)S(1)}, pred[6,16]{1,0:T(8,128)(4,1)S(1)}) fusion(s32[]{:T(128)} %bitcast.2, s32[6]{0:T(128)S(1)} %multiply_add_fusion, s32[]{:T(128)} %bitcast), kind=kLoop, calls=%fused_computation.38 | loop fusion | flops 576 | bytes 224 | tf_op jit(solution)/shard_map/lt | solution.py:34
  20.2 0.7 fusion.25
  21.0 0.8 select_reduce_fusion.2
  21.8 6.3 %all_gather.6 = bf16[1,256,576]{2,1,0:T(8,128)(2,1)S(1)} all-gather(bf16[1,64,576]{2,1,0:T(8,128)(2,1)} %param.8), channel_id=1, replica_groups=mesh['parts'=2,'pool'=4,'tp'=2,'sp'=2] {'tp','sp'}, dimensions={1}, use_global_device_ids=true | all-gather | bytes 368640 | tf_op jit(solution)/shard_map/all_gather | solution.py:90
  28.1 0.1 fusion.18
  28.2 0.3 broadcast_in_dim.107
  28.5 1.2 copy.15
  29.7 9.8 %reshape.213 = bf16[4096,576]{1,0:T(8,128)(2,1)} reshape(bf16[1,128,18432]{2,1,0:T(8,128)(2,1)} %param.7) | data formatting | bytes 9437184 | tf_op jit(solution)/shard_map/reshape | solution.py:45
  39.5 0.0 copy-start.2
  39.5 6.4 %select_reduce_fusion = (f32[4096]{0:T(1024)S(1)}, f32[4096,256]{0,1:T(8,128)}) fusion(pred[4096,256]{0,1:T(32,128)(4,1)S(1)} %copy.15, bf16[4096,576]{1,0:T(8,128)(2,1)} %reshape.213, bf16[1,256,576]{2,1,0:T(8,128)(2,1)S(1)} %all_gather.6), kind=kOutput, calls=%fused_computation.7 | convolution fusion | flops 1211101184 | bytes 10272768 | tf_op jit(solution)/shard_map/dot_general | solution.py:48
  46.0 0.8 fusion.13
  46.8 0.0 copy-done.2
  46.9 0.0 all-to-all-done
  46.9 4.3 %select_reduce_fusion.1 = (f32[4096]{0:T(1024)S(1)}, f32[128,4096]{1,0:T(8,128)S(1)}) fusion(pred[128]{0:T(512)(128)(4,1)S(1)} %iota_compare_fusion.3, bf16[128,576]{1,0:T(8,128)(2,1)S(1)} %bitcast.27, bf16[4096,576]{1,0:T(8,128)(2,1)} %reshape.213), kind=kOutput, calls=%fused_computation.13 | convolution fusion | flops 605548544 | bytes 6979712 | tf_op jit(solution)/shard_map/dot_general | solution.py:47
  51.2 0.4 fusion.5
  51.6 4.6 %fusion.7 = f32[4096,512]{1,0:T(8,128)} fusion(f32[128,4096]{1,0:T(8,128)S(1)} %get-tuple-element.5, f32[4096]{0:T(1024)S(1)} %max.8, pred[128]{0:T(512)(128)(4,1)S(1)} %iota_compare_fusion.3, bf16[128,576]{1,0:T(8,128)(2,1)S(1)} %bitcast.28), kind=kOutput, calls=%fused_computation.16 | convolution fusion | flops 538443776 | bytes 10633728 | tf_op jit(solution)/shard_map/dot_general | solution.py:68
  56.2 0.1 fusion.19
  56.3 0.2 reshape.227
  56.5 21.4 %all-gather = bf16[4,1,55296]{2,1,0:T(2,128)(2,1)S(1)} all-gather(bf16[1,1,55296]{2,1,0:T(2,128)(2,1)S(1)} %reshape.227), channel_id=1, replica_groups=mesh['parts'=2,'pool'=4,'tp'=2,'sp'=2] {'pool'}, dimensions={0}, use_global_device_ids=true | all-gather | bytes 552960 | tf_op jit(solution)/shard_map/all_gather | solution.py:110
  77.9 0.4 convolution_convert_fusion
  78.3 0.9 reshape.217
  79.3 3.2 %fusion = f32[4096]{0:T(1024)S(1)} fusion(pred[4096,256]{0,1:T(32,128)(4,1)S(1)} %copy.15, f32[4096,256]{0,1:T(8,128)} %get-tuple-element.7, f32[4096]{0:T(1024)S(1)} %max.8), kind=kLoop, calls=%fused_computation.8 | loop fusion | flops 3141632 | bytes 5275648 | tf_op jit(solution)/shard_map/reduce_sum | solution.py:63
  82.4 0.1 add.92
  82.5 9.2 %convolution_add_fusion = f32[4096,512]{1,0:T(8,128)} fusion(f32[4096,512]{1,0:T(8,128)} %fusion.7, pred[4096,256]{0,1:T(32,128)(4,1)S(1)} %copy.15, f32[4096,256]{0,1:T(8,128)} %get-tuple-element.7, f32[4096]{0:T(1024)S(1)} %max.8, bf16[256,576]{1,0:T(8,128)(2,1)S(1)} %bitcast.26), kind=kOutput, calls=%fused_computation.3 | convolution fusion | flops 1078984704 | bytes 22298624 | tf_op jit(solution)/shard_map/dot_general | solution.py:69
  91.8 9.4 %reshape.215 = f32[1,128,16384]{2,1,0:T(8,128)} reshape(f32[4096,512]{1,0:T(8,128)} %convolution_add_fusion) | data formatting | bytes 16777216 | tf_op jit(solution)/shard_map/reshape | solution.py:70
  101.1 3.6 %div.17 = f32[128,32,512]{2,1,0:T(8,128)} broadcast(f32[128,32]{1,0:T(8,128)S(1)} %add.92), dimensions={0,1} | broadcast | bytes 8404992 | tf_op jit(solution)/shard_map/div | solution.py:70
  104.7 9.4 %div.18 = f32[1,128,16384]{2,1,0:T(8,128)} reshape(f32[128,32,512]{2,1,0:T(8,128)} %div.17) | data formatting | bytes 16777216 | tf_op jit(solution)/shard_map/div | solution.py:70
  114.1 0.0 copy-start.1
  114.1 9.0 %select_convert_fusion = bf16[1,128,16384]{2,1,0:T(8,128)(2,1)} fusion(f32[1,128,16384]{2,1,0:T(8,128)} %reshape.215, f32[1,128,16384]{2,1,0:T(8,128)} %div.18, pred[128]{0:T(512)(128)(4,1)S(1)} %broadcast_compare_fusion.1), kind=kLoop, calls=%fused_computation.2 | loop fusion | flops 6291456 | bytes 20971648 | tf_op jit(solution)/shard_map/convert_element_type | solution.py:74
  123.1 0.0 copy-done.1
  (9 shorter events, 0.1 us)
Async XLA Ops:
  0.6 1.4 %copy-start = (bf16[4,32,576]{2,1,0:T(8,128)(2,1)S(1)}, bf16[4,32,576]{2,1,0:T(8,128)(2,1)}, u32[]{:S(2)}) copy-start(bf16[4,32,576]{2,1,0:T(8,128)(2,1)} %param.9) | copy-start | bytes 442372
  3.4 43.5 %all-to-all-start = ((bf16[4,32,576]{2,1,0:T(8,128)(2,1)}), bf16[4,32,576]{2,1,0:T(8,128)(2,1)S(1)}, u32[]{:S(2)}, u32[]{:S(2)}) async-start(bf16[4,32,576]{2,1,0:T(8,128)(2,1)} %broadcast_select_fusion), calls=%async_computation | async-start | bytes 327680 | tf_op jit(solution)/shard_map/all_to_all | solution.py:89
  39.5 7.3 %copy-start.2 = (s32[4]{0:T(128)S(1)}, s32[4]{0:T(128)}, u32[]{:S(2)}) copy-start(s32[4]{0:T(128)} %param.13) | copy-start | bytes 52
  114.1 9.0 %copy-start.1 = (bf16[4,32,576]{2,1,0:T(8,128)(2,1)S(1)}, bf16[4,32,576]{2,1,0:T(8,128)(2,1)}, u32[]{:S(2)}) copy-start(bf16[4,32,576]{2,1,0:T(8,128)(2,1)} %param.9) | copy-start | bytes 442372
where the time goes:
time: 124 us; the launch traced here: 123 us
  local copies, waits for them, and re-layouts  39.2 us (32%)
  blocking collectives  27.7 us (22%)
  matrix products  25 us (20%)
  other arithmetic  20.8 us (17%)
  starting transfers between devices  6.32 us (5%)
  between operations  4.05 us (3%)
    all_gather x1, blocking collectives, body(): lax.all_gather(flat, 'pool', axis=0, tiled=True)  21.4 us
    div x2, local copies, waits for them, and re-layouts, attend(): mixture = mixture.reshape(query_count, heads_here, LAT) / row_total  12.9 us
    reshape x1, local copies, waits for them, and re-layouts, attend(): query_rows = queries.reshape(query_count * heads_here, key_width)  9.84 us
    reshape x1, local copies, waits for them, and re-layouts, attend(): mixture = mixture.reshape(query_count, heads_here, LAT) / row_total  9.39 us
    dot_general x1, matrix products, attend(): jnp.dot(new_probs, new_keys[:, :LAT], preferred_element_type=jnp.float32)  9.23 us
    convert_element_type x1, other arithmetic, attend(): return jnp.where(live_rows, mixture, 0.0).astype(jnp.bfloat16).reshape(1,...  9.02 us
    dot_general x1, matrix products, attend(): lax.dot_general(query_rows, new_keys, contract, preferred_element_type=jn...  6.44 us
    all_to_all x1, starting transfers between devices, body(): lax.all_to_all(chosen, 'pool', split_axis=0, concat_axis=1, tiled=True)  6.32 us
  transfers between devices with their start and end apart: 1, of which 0 were waited for; matrix products, arithmetic and copies ran while one was open for 22% of the time, Pallas kernels for 0%

commit v1 on v0

v1 whole, which is shorter than its diff:
```python
import functools
import math

import jax
import jax.numpy as jnp
from jax import lax
from jax.experimental import pallas as pl
from jax.experimental.pallas import tpu as pltpu
from jax.sharding import PartitionSpec as P

LAT = 512
ROPE = 64
KEY_W = LAT + ROPE
PAIR_W = 2 * KEY_W
WIDE = LAT + 2 * ROPE
QK = 192
PG = 64
MOST = 2
DIRECT = 8
EXPONENT = QK**-0.5 * math.log2(math.e)
VMEM_LIMIT = 48 * 2**20


def lane_index():
    return lax.axis_index("tp") * lax.axis_size("sp") + lax.axis_index("sp")


def fill_keys(keys, pre, new, sources):
    me = lax.axis_index("pool")
    rows = pre[0].shape[-2]
    if len(pre) == 1:
        for s in range(sources):
            keys[s * rows : (s + 1) * rows, :] = pre[0][s]
    else:
        for s in range(sources):
            source = lax.rem(me - s + sources, sources)
            keys[pl.ds(pl.multiple_of(source * rows, rows), rows), :] = pre[s][0]
    first = sources * rows
    rows = new[0].shape[-2]
    for s, piece in enumerate(new):
        source = lane_index() ^ s
        keys[pl.ds(pl.multiple_of(first + source * rows, rows), rows), :] = piece[0]
    return first


def pick_prefix(queue, cache, *outs):
    me = lax.axis_index("pool")
    count = cache.shape[0]
    if len(outs) == 1:
        for s in range(count):
            outs[0][s] = cache[queue[s]]
    else:
        for s, out in enumerate(outs):
            out[0] = cache[queue[lax.rem(me + s, count)]]


def build_rows(queue, pre_len, blk_len, *refs, sources, pre_count):
    pre, new, out, keys = refs[:pre_count], refs[pre_count:-2], refs[-2], refs[-1]
    first = fill_keys(keys, pre, new, sources)
    me = lax.axis_index("pool")
    pre_length = pre_len[queue[me]]
    blk_length = blk_len[me]
    rows_lane = PG // (lax.axis_size("tp") * lax.axis_size("sp"))
    shape = (out.shape[1], keys.shape[0])
    row = lax.broadcasted_iota(jnp.int32, shape, 0)
    column = lax.broadcasted_iota(jnp.int32, shape, 1)
    position = row // rows_lane * PG + lane_index() * rows_lane + row % rows_lane
    offset = position - pre_length
    chosen = jnp.where(
        offset < 0, position, jnp.where(offset < blk_length, offset + first, -1)
    )
    picker = jnp.where(column == chosen, 1.0, 0.0).astype(jnp.bfloat16)
    out[0] = jnp.dot(picker, keys[...], preferred_element_type=jnp.float32).astype(out.dtype)


def land_rows(dest, *refs, sources):
    pieces, out = refs[:-1], refs[-1]
    me = lax.axis_index("pool")
    out[...] = jnp.zeros_like(out)
    rank = jnp.int32(0)
    for g in range(sources):
        hit = dest[g] == me

        @pl.when(hit)
        def _(g=g, rank=rank):
            if len(pieces) == 1:
                out[0, rank] = pieces[0][g]
            else:
                shift = lax.rem(me - g + sources, sources)
                for s, piece in enumerate(pieces):

                    @pl.when(shift == s)
                    def _(piece=piece):
                        out[0, rank] = piece[0]

        rank = rank + hit.astype(jnp.int32)


def attend(queue, pre_len, blk_len, queries, *refs, sources, pre_count, pairs):
    pre, new = refs[:pre_count], refs[pre_count:-5]
    out, keys, even_keys, odd_keys, bias = refs[-5:]
    me = lax.axis_index("pool")
    count = queries.shape[1]
    blk_length = blk_len[me]
    first_query = lax.axis_index("sp") * count

    @pl.when(pl.program_id(0) == 0)
    def _():
        first = fill_keys(keys, pre, new, sources)
        held = keys[...]
        blank = jnp.zeros((held.shape[0], ROPE), held.dtype)
        even_keys[...] = jnp.concatenate([held, blank], axis=1).T
        odd_keys[...] = jnp.concatenate([blank, held], axis=1).T
        row = lax.broadcasted_iota(jnp.int32, bias.shape, 0) + first_query
        column = lax.broadcasted_iota(jnp.int32, bias.shape, 1)
        index = column - first
        visible = ((index < 0) & (column < pre_len[queue[me]])) | (
            (index >= 0) & (index <= row) & (index < blk_length)
        )
        bias[...] = jnp.where(visible, 0.0, -jnp.inf)

    values = keys[:, :LAT]
    row = lax.broadcasted_iota(jnp.int32, (count, 1), 0) + first_query
    live = jnp.concatenate([row] * pairs, axis=0) < blk_length
    masked = jnp.concatenate([bias[...]] * pairs, axis=0)
    for odd, key_columns in ((0, even_keys), (1, odd_keys)):
        begin = odd * LAT
        rows = jnp.concatenate(
            [queries[0, :, p * PAIR_W + begin : p * PAIR_W + begin + WIDE] for p in range(pairs)],
            axis=0,
        )
        scores = jnp.dot(rows, key_columns[...], preferred_element_type=jnp.float32) + masked
        top = jnp.max(scores, axis=1, keepdims=True)
        weights = jnp.exp2((scores - top) * EXPONENT)
        total = jnp.sum(weights, axis=1, keepdims=True)
        mixture = jnp.dot(weights.astype(values.dtype), values, preferred_element_type=jnp.float32)
        mixture = (mixture * jnp.where(live, 1.0 / total, 0.0)).astype(out.dtype)
        for p in range(pairs):
            at = (2 * p + odd) * LAT
            out[0, :, at : at + LAT] = mixture[p * count : (p + 1) * count]


def body(queries, block_latent, prefix_cache, queue_list, prefix_len, block_len, decode_dest):
    sources = lax.axis_size("pool")
    lanes = lax.axis_size("tp") * lax.axis_size("sp")
    count, width = queries.shape[1:]
    heads = width // KEY_W
    rows_in = prefix_cache.shape[1]
    key_count = rows_in * sources + block_latent.shape[1] * lanes
    page_count = key_count // PG
    rows_lane = PG // lanes
    direct = sources <= DIRECT
    smem = pl.BlockSpec(memory_space=pltpu.SMEM)
    vmem = pl.BlockSpec(memory_space=pltpu.VMEM)
    params = pltpu.CompilerParams(vmem_limit_bytes=VMEM_LIMIT)
    dtype = queries.dtype

    def shifted(piece, s):
        pairs = [(i, (i + s) % sources) for i in range(sources)]
        return lax.ppermute(piece, "pool", pairs)

    piece = (1 if direct else sources, rows_in, KEY_W)
    pieces = sources if direct else 1
    chosen = pl.pallas_call(
        pick_prefix,
        in_specs=[smem, vmem],
        out_specs=[vmem] * pieces,
        out_shape=[jax.ShapeDtypeStruct(piece, dtype)] * pieces,
        compiler_params=params,
        name="pick_prefix",
    )(queue_list, prefix_cache)
    if direct:
        pre = [chosen[0]] + [shifted(chosen[s], s) for s in range(1, sources)]
    else:
        pre = [lax.all_to_all(chosen[0], "pool", split_axis=0, concat_axis=0, tiled=True)]
    new = [block_latent] + [
        lax.ppermute(block_latent, ("tp", "sp"), [(i, i ^ s) for i in range(lanes)])
        for s in range(1, lanes)
    ]
    scalars = (queue_list, prefix_len, block_len)
    lane_rows = pl.pallas_call(
        functools.partial(build_rows, sources=sources, pre_count=len(pre)),
        in_specs=[smem] * 3 + [vmem] * (len(pre) + len(new)),
        out_specs=vmem,
        out_shape=jax.ShapeDtypeStruct((1, page_count * rows_lane, KEY_W), dtype),
        scratch_shapes=[pltpu.VMEM((key_count, KEY_W), dtype)],
        compiler_params=params,
        name="build_rows",
    )(*scalars, *pre, *new)
    if direct:
        landed = [lane_rows] + [shifted(lane_rows, s) for s in range(1, sources)]
    else:
        landed = [lax.all_gather(lane_rows, "pool", axis=0, tiled=True)]
    pairs = heads // 2
    while pairs > 1 and pairs * count * key_count > 1024 * 384:
        pairs //= 2
    latent_out = pl.pallas_call(
        functools.partial(attend, sources=sources, pre_count=len(pre), pairs=pairs),
        grid=(heads // 2 // pairs,),
        in_specs=[smem] * 3
        + [pl.BlockSpec((1, count, pairs * PAIR_W), lambda i: (0, 0, i))]
        + [vmem] * (len(pre) + len(new)),
        out_specs=pl.BlockSpec((1, count, pairs * 2 * LAT), lambda i: (0, 0, i)),
        out_shape=jax.ShapeDtypeStruct((1, count, heads * LAT), dtype),
        scratch_shapes=[
            pltpu.VMEM((key_count, KEY_W), dtype),
            pltpu.VMEM((WIDE, key_count), dtype),
            pltpu.VMEM((WIDE, key_count), dtype),
            pltpu.VMEM((count, key_count), jnp.float32),
        ],
        compiler_params=params,
        cost_estimate=pl.CostEstimate(
            flops=2 * count * heads * key_count * (KEY_W + LAT),
            bytes_accessed=2 * count * heads * (KEY_W + LAT),
            transcendentals=count * heads * key_count,
        ),
        name="attend",
    )(*scalars, queries, *pre, *new)
    decode_pages = pl.pallas_call(
        functools.partial(land_rows, sources=sources),
        in_specs=[smem] + [vmem] * len(landed),
        out_specs=vmem,
        out_shape=jax.ShapeDtypeStruct((1, MOST, page_count * rows_lane, KEY_W), dtype),
        compiler_params=params,
        name="land_rows",
    )(decode_dest, *landed)
    return latent_out, decode_pages.reshape(1, MOST, page_count, rows_lane, KEY_W)


def solution(mesh):
    in_specs = (
        P(("parts", "pool"), "sp", "tp"),
        P(("parts", "pool"), ("tp", "sp"), None),
        P("parts", "pool", None),
        P("parts"),
        P("parts"),
        P("parts"),
        P("parts"),
    )
    out_specs = (
        P(("parts", "pool"), "sp", "tp"),
        P(("parts", "pool"), None, None, ("tp", "sp"), None),
    )
    return jax.shard_map(body, mesh=mesh, in_specs=in_specs, out_specs=out_specs, check_vma=False)
```

time: 124 us -> 35.8 us (0.29)
  local copies, waits for them, and re-layouts: 39.2 us -> 6.98 us
  blocking collectives: 27.7 us -> 0 us
  matrix products: 25 us -> 0 us
  other arithmetic: 20.8 us -> 0 us
  Pallas kernels: 0 us -> 12.2 us
  starting transfers between devices: 6.32 us -> 13.2 us
  between operations: 4.05 us -> 0.69 us
  waiting for transfers between devices: 0.01 us -> 2.45 us
    all_gather x2 -> x0, blocking collectives: 27.7 us -> none  [the longest x1 21.4 us: body(): lax.all_gather(flat, 'pool', axis=0, tiled=True)]
    dot_general x5 -> x0, matrix products: 25 us -> none  [the longest x1 9.23 us: attend(): jnp.dot(new_probs, new_keys[:, :LAT], preferred_element_type=jnp.float32)]
    reshape x3 -> x0, local copies, waits for them, and re-layouts: 20.2 us -> none  [the longest x1 9.84 us: attend(): query_rows = queries.reshape(query_count * heads_here, key_width)]
    ppermute x0 -> x9, starting transfers between devices: none -> 13.2 us  [the longest x6 11.3 us: shifted(): return lax.ppermute(piece, 'pool', pairs)]
    div x2 -> x0, local copies, waits for them, and re-layouts: 12.9 us -> none  [attend(): mixture = mixture.reshape(query_count, heads_here, LAT) / row_total]
    pallas_call x0 -> x4, Pallas kernels: none -> 12.2 us  [the longest x1 9.52 us: body(): pl.pallas_call(functools.partial(attend, sources=sources, pre_count=len(p...]
    convert_element_type x2 -> x0, other arithmetic: 9.75 us -> none  [the longest x1 9.02 us: attend(): return jnp.where(live_rows, mixture, 0.0).astype(jnp.bfloat16).reshape(1,...]
    unnamed x7 -> x16, local copies, waits for them, and re-layouts: 0.2 us -> 6.98 us
  transfers between devices with their start and end apart: 1 -> 9, of which waited for: 0 -> 2; matrix products, arithmetic and copies ran while one was open for 22% -> 0% of each run, Pallas kernels for 0% -> 27%
where the time goes in v1:
time: 35.8 us; the launch traced here: 35.5 us
  starting transfers between devices  13.2 us (37%)
  Pallas kernels  12.2 us (34%)
  local copies, waits for them, and re-layouts  6.98 us (19%)
  waiting for transfers between devices  2.45 us (7%)
  between operations  0.69 us (2%)
    ppermute x6, starting transfers between devices, shifted(): return lax.ppermute(piece, 'pool', pairs)  11.3 us
    pallas_call x1, Pallas kernels, body(): pl.pallas_call(functools.partial(attend, sources=sources, pre_count=len(p...  9.52 us
    unnamed x16, local copies, waits for them, and re-layouts  6.98 us
    ppermute x6, waiting for transfers between devices, shifted(): return lax.ppermute(piece, 'pool', pairs)  2.44 us
    ppermute x3, starting transfers between devices, body(): lax.ppermute(block_latent, ('tp', 'sp'), [(i, i ^ s) for i in range(lanes)])  1.86 us
    pallas_call x1, Pallas kernels, body(): pl.pallas_call(functools.partial(land_rows, sources=sources), in_specs=[s...  1.28 us
    pallas_call x1, Pallas kernels, body(): pl.pallas_call(functools.partial(build_rows, sources=sources, pre_count=l...  0.84 us
  transfers between devices with their start and end apart: 9, of which 2 were waited for; matrix products, arithmetic and copies ran while one was open for 0% of the time, Pallas kernels for 27%

profile of v1, /device:TPU:0, one launch (start us, length us, event | category | flops | bytes accessed | tf_op | source)
XLA Modules:
  0.0 35.5 jit_solution(7552469622082556721)
XLA Ops:
  0.6 0.0 copy-start
  0.6 0.9 %copy-done = bf16[4,32,576]{2,1,0:T(8,128)(2,1)S(1)} copy-done((bf16[4,32,576]{2,1,0:T(8,128)(2,1)S(1)}, bf16[4,32,576]{2,1,0:T(8,128)(2,1)}, u32[]{:S(2)}) %copy-start) | copy-done | bytes 147480
  1.5 0.0 copy-start.3
  1.5 0.7 %copy-done.3 = s32[4]{0:T(128)S(1)} copy-done((s32[4]{0:T(128)S(1)}, s32[4]{0:T(128)}, u32[]{:S(2)}) %copy-start.3) | copy-done | bytes 40
  2.2 0.6 %pick_prefix.1 = (bf16[1,32,576]{2,1,0:T(8,128)(2,1)S(1)}, bf16[1,32,576]{2,1,0:T(8,128)(2,1)S(1)}, bf16[1,32,576]{2,1,0:T(8,128)(2,1)S(1)}, bf16[1,32,576]{2,1,0:T(8,128)(2,1)S(1)}) custom-call(s32[4]{0:T(128)S(1)} %copy-done.3, bf16[4,32,576]{2,1,0:T(8,128)(2,1)S(1)} %copy-done), custom_call_target="tpu_custom_call" | custom-call | tf_op jit(solution)/shard_map/pick_prefix/pallas_call | solution.py:164
  2.8 3.1 %collective-permute-start = (bf16[1,32,576]{2,1,0:T(8,128)(2,1)S(1)}, bf16[1,32,576]{2,1,0:T(8,128)(2,1)S(1)}, u32[]{:S(2)}, u32[]{:S(2)}) collective-permute-start(bf16[1,32,576]{2,1,0:T(8,128)(2,1)S(1)} %get-tuple-element.7), channel_id=1, source_target_pairs={{0,4},{4,8},{8,12},{12,0},{1,5},{5,9},{9,13},{13,1},{2,6},{6,10},{... | collective-permute-start | bytes 110600 | tf_op jit(solution)/shard_map/ppermute | solution.py:160
  5.9 0.7 %collective-permute-start.5 = (bf16[1,64,576]{2,1,0:T(8,128)(2,1)}, bf16[1,64,576]{2,1,0:T(8,128)(2,1)S(1)}, u32[]{:S(2)}, u32[]{:S(2)}) collective-permute-start(bf16[1,64,576]{2,1,0:T(8,128)(2,1)} %refs_4_.3), channel_id=1, source_target_pairs={{0,3},{1,2},{2,1},{3,0},{4,7},{5,6},{6,5},{7,4},{8,11},{9,10},{10,... | collective-permute-start | bytes 221192 | tf_op jit(solution)/shard_map/ppermute | solution.py:177
  6.5 0.9 %collective-permute-start.4 = (bf16[1,64,576]{2,1,0:T(8,128)(2,1)}, bf16[1,64,576]{2,1,0:T(8,128)(2,1)S(1)}, u32[]{:S(2)}, u32[]{:S(2)}) collective-permute-start(bf16[1,64,576]{2,1,0:T(8,128)(2,1)} %refs_4_.3), channel_id=1, source_target_pairs={{0,2},{1,3},{2,0},{3,1},{4,6},{5,7},{6,4},{7,5},{8,10},{9,11},{10,... | collective-permute-start | bytes 221192 | tf_op jit(solution)/shard_map/ppermute | solution.py:177
  7.4 0.3 collective-permute-start.3
  7.7 2.6 %collective-permute-start.1 = (bf16[1,32,576]{2,1,0:T(8,128)(2,1)S(1)}, bf16[1,32,576]{2,1,0:T(8,128)(2,1)S(1)}, u32[]{:S(2)}, u32[]{:S(2)}) collective-permute-start(bf16[1,32,576]{2,1,0:T(8,128)(2,1)S(1)} %get-tuple-element.8), channel_id=1, source_target_pairs={{0,8},{4,12},{8,0},{12,4},{1,9},{5,13},{9,1},{13,5},{2,10},{6,14},... | collective-permute-start | bytes 110600 | tf_op jit(solution)/shard_map/ppermute | solution.py:160
  10.3 0.0 collective-permute-done.refs_1_
  10.3 1.6 %collective-permute-start.2 = (bf16[1,32,576]{2,1,0:T(8,128)(2,1)S(1)}, bf16[1,32,576]{2,1,0:T(8,128)(2,1)S(1)}, u32[]{:S(2)}, u32[]{:S(2)}) collective-permute-start(bf16[1,32,576]{2,1,0:T(8,128)(2,1)S(1)} %get-tuple-element.9), channel_id=1, source_target_pairs={{0,12},{4,0},{8,4},{12,8},{1,13},{5,1},{9,5},{13,9},{2,14},{6,2},{... | collective-permute-start | bytes 110600 | tf_op jit(solution)/shard_map/ppermute | solution.py:160
  11.9 1.4 %collective-permute-done.1.refs_2_ = bf16[1,32,576]{2,1,0:T(8,128)(2,1)S(1)} collective-permute-done((bf16[1,32,576]{2,1,0:T(8,128)(2,1)S(1)}, bf16[1,32,576]{2,1,0:T(8,128)(2,1)S(1)}, u32[]{:S(2)}, u32[]{:S(2)}) %collective-permute-start.1) | collective-permute-done | bytes 36896 | tf_op jit(solution)/shard_map/ppermute | solution.py:160
  13.3 1.0 %collective-permute-done.2.refs_3_ = bf16[1,32,576]{2,1,0:T(8,128)(2,1)S(1)} collective-permute-done((bf16[1,32,576]{2,1,0:T(8,128)(2,1)S(1)}, bf16[1,32,576]{2,1,0:T(8,128)(2,1)S(1)}, u32[]{:S(2)}, u32[]{:S(2)}) %collective-permute-start.2) | collective-permute-done | bytes 36896 | tf_op jit(solution)/shard_map/ppermute | solution.py:160
  14.3 0.0 collective-permute-done.5.refs_7_
  14.3 0.0 collective-permute-done.4.refs_6_
  14.3 0.0 collective-permute-done.3.refs_5_
  14.3 0.0 copy-start.1
  14.3 0.9 %copy-done.1 = bf16[1,64,576]{2,1,0:T(8,128)(2,1)S(1)} copy-done((bf16[1,64,576]{2,1,0:T(8,128)(2,1)S(1)}, bf16[1,64,576]{2,1,0:T(8,128)(2,1)}, u32[]{:S(2)}) %copy-start.1) | copy-done | bytes 73752
  15.2 0.0 copy-start.5
  15.2 0.7 %copy-done.5 = s32[4]{0:T(128)S(1)} copy-done((s32[4]{0:T(128)S(1)}, s32[4]{0:T(128)}, u32[]{:S(2)}) %copy-start.5) | copy-done | bytes 40
  15.9 0.0 copy-start.6
  15.9 0.7 %copy-done.6 = s32[4]{0:T(128)S(1)} copy-done((s32[4]{0:T(128)S(1)}, s32[4]{0:T(128)}, u32[]{:S(2)}) %copy-start.6) | copy-done | bytes 40
  16.5 0.0 copy-start.4
  16.5 0.8 %build_rows.1.refs_0_ = bf16[1,96,576]{2,1,0:T(8,128)(2,1)S(1)} custom-call(s32[4]{0:T(128)S(1)} %copy-done.3, s32[4]{0:T(128)S(1)} %copy-done.5, s32[4]{0:T(128)S(1)} %copy-done.6, bf16[1,32,576]{2,1,0:T(8,128)(2,1)S(1)} %get-tuple-element.6.refs_0_, bf16[1,32,576]{2,1,0:T(8,128)(2,1)S(1)} %collective-permute-done.refs_1_, ...), custom_call_target="tpu_custom_call" | custom-call | tf_op jit(solution)/shard_map/build_rows/pallas_call | solution.py:181
  17.4 3.4 %collective-permute-start.8 = (bf16[1,96,576]{2,1,0:T(8,128)(2,1)S(1)}, bf16[1,96,576]{2,1,0:T(8,128)(2,1)S(1)}, u32[]{:S(2)}, u32[]{:S(2)}) collective-permute-start(bf16[1,96,576]{2,1,0:T(8,128)(2,1)S(1)} %build_rows.1.refs_0_), channel_id=1, source_target_pairs={{0,12},{4,0},{8,4},{12,8},{1,13},{5,1},{9,5},{13,9},{2,14},{6,2},{... | collective-permute-start | bytes 331784 | tf_op jit(solution)/shard_map/ppermute | solution.py:160
  20.8 0.0 collective-permute-start.7
  20.8 0.6 %collective-permute-start.6 = (bf16[1,96,576]{2,1,0:T(8,128)(2,1)S(1)}, bf16[1,96,576]{2,1,0:T(8,128)(2,1)S(1)}, u32[]{:S(2)}, u32[]{:S(2)}) collective-permute-start(bf16[1,96,576]{2,1,0:T(8,128)(2,1)S(1)} %build_rows.1.refs_0_), channel_id=1, source_target_pairs={{0,4},{4,8},{8,12},{12,0},{1,5},{5,9},{9,13},{13,1},{2,6},{6,10},{... | collective-permute-start | bytes 331784 | tf_op jit(solution)/shard_map/ppermute | solution.py:160
  21.4 0.0 copy-start.2
  21.4 0.9 %copy-done.2 = bf16[1,64,576]{2,1,0:T(8,128)(2,1)S(1)} copy-done((bf16[1,64,576]{2,1,0:T(8,128)(2,1)S(1)}, bf16[1,64,576]{2,1,0:T(8,128)(2,1)}, u32[]{:S(2)}) %copy-start.2) | copy-done | bytes 73752
  22.3 0.0 copy-start.7
  22.3 2.3 %copy-done.7 = bf16[1,128,18432]{2,1,0:T(8,128)(2,1)S(1)} copy-done((bf16[1,128,18432]{2,1,0:T(8,128)(2,1)S(1)}, bf16[1,128,18432]{2,1,0:T(8,128)(2,1)}, u32[]{:S(2)}) %copy-start.7) | copy-done | bytes 4718616
  24.7 9.5 %attend.1 = bf16[1,128,16384]{2,1,0:T(8,128)(2,1)} custom-call(s32[4]{0:T(128)S(1)} %copy-done.3, s32[4]{0:T(128)S(1)} %copy-done.5, s32[4]{0:T(128)S(1)} %copy-done.6, bf16[1,128,18432]{2,1,0:T(8,128)(2,1)S(1)} %copy-done.7, bf16[1,32,576]{2,1,0:T(8,128)(2,1)S(1)} %get-tuple-element.6.refs_0_, bf16[1,32,576]{2,1,0:T(8,128)(2,1)S(1)} %collective-permute-done.refs_1_, ...), custom_call_target="tpu_custom_call" | custom-call | flops 3422552064 | bytes 8912896 | tf_op jit(solution)/shard_map/attend/pallas_call | solution.py:197
  34.2 0.0 collective-permute-done.8.refs_3_
  34.2 0.0 collective-permute-done.7.refs_2_
  34.2 0.0 collective-permute-done.6.refs_1_
  34.2 0.0 copy-done.4
  34.2 1.3 %land_rows.1 = bf16[1,2,96,576]{3,2,1,0:T(8,128)(2,1)} custom-call(s32[4]{0:T(128)S(1)} %copy-done.4, bf16[1,96,576]{2,1,0:T(8,128)(2,1)S(1)} %build_rows.1.refs_0_, bf16[1,96,576]{2,1,0:T(8,128)(2,1)S(1)} %collective-permute-done.6.refs_1_, bf16[1,96,576]{2,1,0:T(8,128)(2,1)S(1)} %collective-permute-done.7.refs_2_, ...), custom_call_target="tpu_custom_call" | custom-call | tf_op jit(solution)/shard_map/land_rows/pallas_call | solution.py:219
Async XLA Ops:
  0.6 0.9 %copy-start = (bf16[4,32,576]{2,1,0:T(8,128)(2,1)S(1)}, bf16[4,32,576]{2,1,0:T(8,128)(2,1)}, u32[]{:S(2)}) copy-start(bf16[4,32,576]{2,1,0:T(8,128)(2,1)} %cache.1) | copy-start | bytes 442372
  1.5 0.7 %copy-start.3 = (s32[4]{0:T(128)S(1)}, s32[4]{0:T(128)}, u32[]{:S(2)}) copy-start(s32[4]{0:T(128)} %queue.5) | copy-start | bytes 52
  2.8 7.5 %collective-permute-start = (bf16[1,32,576]{2,1,0:T(8,128)(2,1)S(1)}, bf16[1,32,576]{2,1,0:T(8,128)(2,1)S(1)}, u32[]{:S(2)}, u32[]{:S(2)}) collective-permute-start(bf16[1,32,576]{2,1,0:T(8,128)(2,1)S(1)} %get-tuple-element.7), channel_id=1, source_target_pairs={{0,4},{4,8},{8,12},{12,0},{1,5},{5,9},{9,13},{13,1},{2,6},{6,10},{... | collective-permute-start | bytes 110600 | tf_op jit(solution)/shard_map/ppermute | solution.py:160
  5.9 8.5 %collective-permute-start.5 = (bf16[1,64,576]{2,1,0:T(8,128)(2,1)}, bf16[1,64,576]{2,1,0:T(8,128)(2,1)S(1)}, u32[]{:S(2)}, u32[]{:S(2)}) collective-permute-start(bf16[1,64,576]{2,1,0:T(8,128)(2,1)} %refs_4_.3), channel_id=1, source_target_pairs={{0,3},{1,2},{2,1},{3,0},{4,7},{5,6},{6,5},{7,4},{8,11},{9,10},{10,... | collective-permute-start | bytes 221192 | tf_op jit(solution)/shard_map/ppermute | solution.py:177
  6.5 7.8 %collective-permute-start.4 = (bf16[1,64,576]{2,1,0:T(8,128)(2,1)}, bf16[1,64,576]{2,1,0:T(8,128)(2,1)S(1)}, u32[]{:S(2)}, u32[]{:S(2)}) collective-permute-start(bf16[1,64,576]{2,1,0:T(8,128)(2,1)} %refs_4_.3), channel_id=1, source_target_pairs={{0,2},{1,3},{2,0},{3,1},{4,6},{5,7},{6,4},{7,5},{8,10},{9,11},{10,... | collective-permute-start | bytes 221192 | tf_op jit(solution)/shard_map/ppermute | solution.py:177
  7.4 6.9 %collective-permute-start.3 = (bf16[1,64,576]{2,1,0:T(8,128)(2,1)}, bf16[1,64,576]{2,1,0:T(8,128)(2,1)S(1)}, u32[]{:S(2)}, u32[]{:S(2)}) collective-permute-start(bf16[1,64,576]{2,1,0:T(8,128)(2,1)} %refs_4_.3), channel_id=1, source_target_pairs={{0,1},{1,0},{2,3},{3,2},{4,5},{5,4},{6,7},{7,6},{8,9},{9,8},{10,11... | collective-permute-start | bytes 221192 | tf_op jit(solution)/shard_map/ppermute | solution.py:177
  7.7 5.6 %collective-permute-start.1 = (bf16[1,32,576]{2,1,0:T(8,128)(2,1)S(1)}, bf16[1,32,576]{2,1,0:T(8,128)(2,1)S(1)}, u32[]{:S(2)}, u32[]{:S(2)}) collective-permute-start(bf16[1,32,576]{2,1,0:T(8,128)(2,1)S(1)} %get-tuple-element.8), channel_id=1, source_target_pairs={{0,8},{4,12},{8,0},{12,4},{1,9},{5,13},{9,1},{13,5},{2,10},{6,14},... | collective-permute-start | bytes 110600 | tf_op jit(solution)/shard_map/ppermute | solution.py:160
  10.3 4.0 %collective-permute-start.2 = (bf16[1,32,576]{2,1,0:T(8,128)(2,1)S(1)}, bf16[1,32,576]{2,1,0:T(8,128)(2,1)S(1)}, u32[]{:S(2)}, u32[]{:S(2)}) collective-permute-start(bf16[1,32,576]{2,1,0:T(8,128)(2,1)S(1)} %get-tuple-element.9), channel_id=1, source_target_pairs={{0,12},{4,0},{8,4},{12,8},{1,13},{5,1},{9,5},{13,9},{2,14},{6,2},{... | collective-permute-start | bytes 110600 | tf_op jit(solution)/shard_map/ppermute | solution.py:160
  14.3 0.9 %copy-start.1 = (bf16[1,64,576]{2,1,0:T(8,128)(2,1)S(1)}, bf16[1,64,576]{2,1,0:T(8,128)(2,1)}, u32[]{:S(2)}) copy-start(bf16[1,64,576]{2,1,0:T(8,128)(2,1)} %refs_4_.3) | copy-start | bytes 221188
  15.2 0.7 %copy-start.5 = (s32[4]{0:T(128)S(1)}, s32[4]{0:T(128)}, u32[]{:S(2)}) copy-start(s32[4]{0:T(128)} %pre_len.3) | copy-start | bytes 52
  15.9 0.7 %copy-start.6 = (s32[4]{0:T(128)S(1)}, s32[4]{0:T(128)}, u32[]{:S(2)}) copy-start(s32[4]{0:T(128)} %blk_len.3) | copy-start | bytes 52
  16.5 17.7 %copy-start.4 = (s32[4]{0:T(128)S(1)}, s32[4]{0:T(128)}, u32[]{:S(2)}) copy-start(s32[4]{0:T(128)} %dest.1) | copy-start | bytes 52
  17.4 16.8 %collective-permute-start.8 = (bf16[1,96,576]{2,1,0:T(8,128)(2,1)S(1)}, bf16[1,96,576]{2,1,0:T(8,128)(2,1)S(1)}, u32[]{:S(2)}, u32[]{:S(2)}) collective-permute-start(bf16[1,96,576]{2,1,0:T(8,128)(2,1)S(1)} %build_rows.1.refs_0_), channel_id=1, source_target_pairs={{0,12},{4,0},{8,4},{12,8},{1,13},{5,1},{9,5},{13,9},{2,14},{6,2},{... | collective-permute-start | bytes 331784 | tf_op jit(solution)/shard_map/ppermute | solution.py:160
  20.8 13.4 %collective-permute-start.7 = (bf16[1,96,576]{2,1,0:T(8,128)(2,1)S(1)}, bf16[1,96,576]{2,1,0:T(8,128)(2,1)S(1)}, u32[]{:S(2)}, u32[]{:S(2)}) collective-permute-start(bf16[1,96,576]{2,1,0:T(8,128)(2,1)S(1)} %build_rows.1.refs_0_), channel_id=1, source_target_pairs={{0,8},{4,12},{8,0},{12,4},{1,9},{5,13},{9,1},{13,5},{2,10},{6,14},... | collective-permute-start | bytes 331784 | tf_op jit(solution)/shard_map/ppermute | solution.py:160
  20.8 13.4 %collective-permute-start.6 = (bf16[1,96,576]{2,1,0:T(8,128)(2,1)S(1)}, bf16[1,96,576]{2,1,0:T(8,128)(2,1)S(1)}, u32[]{:S(2)}, u32[]{:S(2)}) collective-permute-start(bf16[1,96,576]{2,1,0:T(8,128)(2,1)S(1)} %build_rows.1.refs_0_), channel_id=1, source_target_pairs={{0,4},{4,8},{8,12},{12,0},{1,5},{5,9},{9,13},{13,1},{2,6},{6,10},{... | collective-permute-start | bytes 331784 | tf_op jit(solution)/shard_map/ppermute | solution.py:160
  21.4 0.9 %copy-start.2 = (bf16[1,64,576]{2,1,0:T(8,128)(2,1)S(1)}, bf16[1,64,576]{2,1,0:T(8,128)(2,1)}, u32[]{:S(2)}) copy-start(bf16[1,64,576]{2,1,0:T(8,128)(2,1)} %refs_4_.3) | copy-start | bytes 221188
  22.3 2.3 %copy-start.7 = (bf16[1,128,18432]{2,1,0:T(8,128)(2,1)S(1)}, bf16[1,128,18432]{2,1,0:T(8,128)(2,1)}, u32[]{:S(2)}) copy-start(bf16[1,128,18432]{2,1,0:T(8,128)(2,1)} %queries.1) | copy-start | bytes 14155780

commit v2 on v1

v2 whole, which is shorter than its diff:
```python
import functools
import math

import jax
import jax.numpy as jnp
from jax import lax
from jax.experimental import pallas as pl
from jax.experimental.pallas import tpu as pltpu
from jax.sharding import PartitionSpec as P

LAT = 512
ROPE = 64
KEY_W = LAT + ROPE
PAIR_W = 2 * KEY_W
WIDE = LAT + 2 * ROPE
QK = 192
PG = 64
MOST = 2
DIRECT = 8
EXPONENT = QK**-0.5 * math.log2(math.e)
VMEM_LIMIT = 48 * 2**20


def lane_index():
    return lax.axis_index("tp") * lax.axis_size("sp") + lax.axis_index("sp")


def fill_keys(keys, pre, new, sources):
    me = lax.axis_index("pool")
    rows = pre[0].shape[-2]
    if len(pre) == 1:
        for s in range(sources):
            keys[s * rows : (s + 1) * rows, :] = pre[0][s]
    else:
        for s in range(sources):
            source = lax.rem(me - s + sources, sources)
            keys[pl.ds(pl.multiple_of(source * rows, rows), rows), :] = pre[s][0]
    first = sources * rows
    rows = new[0].shape[-2]
    for s, piece in enumerate(new):
        source = lane_index() ^ s
        keys[pl.ds(pl.multiple_of(first + source * rows, rows), rows), :] = piece[0]
    return first


def pick_prefix(queue, pre_len, blk_len, dest, cache, block, facts, own, *refs):
    outs, (lists, held, signals) = refs[:-3], refs[-3:]
    me = lax.axis_index("pool")
    count = cache.shape[0]
    copies = [
        pltpu.make_async_copy(source, lists.at[i], signals.at[i])
        for i, source in enumerate((queue, pre_len, blk_len, dest))
    ]
    copies.append(pltpu.make_async_copy(cache, held, signals.at[4]))
    copies.append(pltpu.make_async_copy(block, own, signals.at[5]))
    for copy in copies:
        copy.start()
    for copy in copies:
        copy.wait()
    if len(outs) == 1:
        for s in range(count):
            outs[0][s] = held[lists[0, s]]
    else:
        for s, out in enumerate(outs):
            out[0] = held[lists[0, lax.rem(me + s, count)]]
    facts[0] = lists[1, lists[0, me]]
    facts[1] = lists[2, me]
    for slot in range(MOST):
        facts[2 + slot] = jnp.int32(-1)
    rank = jnp.int32(0)
    for g in range(count):
        hit = lists[3, g] == me

        @pl.when(hit)
        def _(g=g, rank=rank):
            facts[2 + rank] = lax.rem(me - g + count, count)

        rank = rank + hit.astype(jnp.int32)


def build_rows(facts, *refs, sources, pre_count):
    pre, new, out, keys = refs[:pre_count], refs[pre_count:-2], refs[-2], refs[-1]
    first = fill_keys(keys, pre, new, sources)
    pre_length = facts[0]
    blk_length = facts[1]
    rows_lane = PG // (lax.axis_size("tp") * lax.axis_size("sp"))
    shape = (out.shape[1], keys.shape[0])
    row = lax.broadcasted_iota(jnp.int32, shape, 0)
    column = lax.broadcasted_iota(jnp.int32, shape, 1)
    position = row // rows_lane * PG + lane_index() * rows_lane + row % rows_lane
    offset = position - pre_length
    chosen = jnp.where(
        offset < 0, position, jnp.where(offset < blk_length, offset + first, -1)
    )
    picker = jnp.where(column == chosen, 1.0, 0.0).astype(jnp.bfloat16)
    out[0] = jnp.dot(picker, keys[...], preferred_element_type=jnp.float32).astype(out.dtype)


def land_rows(facts, *refs, sources):
    pieces, (out, blank, signals) = refs[:-3], refs[-3:]
    me = lax.axis_index("pool")
    blank[...] = jnp.zeros_like(blank)

    def landing(slot, source):
        return pltpu.make_async_copy(source, out.at[0, slot], signals.at[slot])

    for slot in range(MOST):
        shift = facts[2 + slot]

        @pl.when(shift < 0)
        def _(slot=slot):
            landing(slot, blank).start()

        if len(pieces) == 1:

            @pl.when(shift >= 0)
            def _(slot=slot, shift=shift):
                landing(slot, pieces[0].at[lax.rem(me - shift + sources, sources)]).start()
        else:
            for s, piece in enumerate(pieces):

                @pl.when(shift == s)
                def _(slot=slot, piece=piece):
                    landing(slot, piece.at[0]).start()

    for slot in range(MOST):
        landing(slot, blank).wait()


def attend(facts, queries, *refs, sources, pre_count, pairs):
    pre, new = refs[:pre_count], refs[pre_count:-7]
    out, held, keys, even_keys, odd_keys, bias, signals = refs[-7:]
    count = queries.shape[1]
    heads = queries.shape[2] // KEY_W
    blk_length = facts[1]
    first_query = lax.axis_index("sp") * count
    first = fill_keys(keys, pre, new, sources)
    blank = jnp.zeros((keys.shape[0], ROPE), keys.dtype)
    even_keys[:, :KEY_W] = keys[...]
    even_keys[:, KEY_W:] = blank
    odd_keys[...] = jnp.concatenate([blank, keys[...]], axis=1)
    row = lax.broadcasted_iota(jnp.int32, bias.shape, 0) + first_query
    column = lax.broadcasted_iota(jnp.int32, bias.shape, 1)
    index = column - first
    visible = ((index < 0) & (column < facts[0])) | (
        (index >= 0) & (index <= row) & (index < blk_length)
    )
    bias[...] = jnp.where(visible, 0.0, -jnp.inf)
    values = keys[:, :LAT]
    row = lax.broadcasted_iota(jnp.int32, (count, 1), 0) + first_query
    live = jnp.concatenate([row] * pairs, axis=0) < blk_length
    masked = jnp.concatenate([bias[...]] * pairs, axis=0)

    def leaving(head):
        columns = pl.ds(head * LAT, LAT)
        return pltpu.make_async_copy(held.at[:, columns], out.at[0, :, columns], signals.at[head])

    units = [(p, odd) for p in range(0, heads // 2, pairs) for odd in (0, 1)]
    for number, (pair, odd) in enumerate(units):
        starts = [(pair + p) * PAIR_W + odd * LAT for p in range(pairs)]
        rows = jnp.concatenate([queries[0, :, at : at + WIDE] for at in starts], axis=0)
        scores = lax.dot_general(
            rows,
            (odd_keys if odd else even_keys)[...],
            (((1,), (1,)), ((), ())),
            preferred_element_type=jnp.float32,
        )
        scores = scores + masked
        top = jnp.max(scores, axis=1, keepdims=True)
        weights = jnp.exp2((scores - top) * EXPONENT)
        scale = jnp.where(live, 1.0 / jnp.sum(weights, axis=1, keepdims=True), 0.0)
        weights = weights.astype(values.dtype)
        step = pairs if number + 1 < len(units) else max(pairs // 4, 1)
        for p in range(0, pairs, step):
            part = slice(p * count, (p + step) * count)
            mixture = jnp.dot(weights[part], values, preferred_element_type=jnp.float32)
            mixture = (mixture * scale[part]).astype(held.dtype)
            for i in range(step):
                head = 2 * (pair + p + i) + odd
                held[:, head * LAT : (head + 1) * LAT] = mixture[i * count : (i + 1) * count]
                leaving(head).start()
    for head in range(heads):
        leaving(head).wait()


def body(queries, block_latent, prefix_cache, queue_list, prefix_len, block_len, decode_dest):
    sources = lax.axis_size("pool")
    lanes = lax.axis_size("tp") * lax.axis_size("sp")
    count, width = queries.shape[1:]
    heads = width // KEY_W
    rows_in = prefix_cache.shape[1]
    key_count = rows_in * sources + block_latent.shape[1] * lanes
    page_count = key_count // PG
    rows_lane = PG // lanes
    direct = sources <= DIRECT
    smem = pl.BlockSpec(memory_space=pltpu.SMEM)
    vmem = pl.BlockSpec(memory_space=pltpu.VMEM)
    hbm = pl.BlockSpec(memory_space=pltpu.HBM)
    params = pltpu.CompilerParams(vmem_limit_bytes=VMEM_LIMIT)
    dtype = queries.dtype

    def shifted(piece, s):
        pairs = [(i, (i + s) % sources) for i in range(sources)]
        return lax.ppermute(piece, "pool", pairs)

    piece = (1 if direct else sources, rows_in, KEY_W)
    pieces = sources if direct else 1
    facts, own, *chosen = pl.pallas_call(
        pick_prefix,
        in_specs=[hbm] * 6,
        out_specs=[smem] + [vmem] * (1 + pieces),
        out_shape=[
            jax.ShapeDtypeStruct((2 + MOST,), jnp.int32),
            jax.ShapeDtypeStruct(block_latent.shape, dtype),
        ]
        + [jax.ShapeDtypeStruct(piece, dtype)] * pieces,
        scratch_shapes=[
            pltpu.SMEM((4, sources), jnp.int32),
            pltpu.VMEM(prefix_cache.shape, dtype),
            pltpu.SemaphoreType.DMA((6,)),
        ],
        compiler_params=pltpu.CompilerParams(vmem_limit_bytes=60 * 2**20),
        name="pick_prefix",
    )(queue_list, prefix_len, block_len, decode_dest, prefix_cache, block_latent)
    if direct:
        pre = [chosen[0]] + [shifted(chosen[s], s) for s in range(1, sources)]
    else:
        pre = [lax.all_to_all(chosen[0], "pool", split_axis=0, concat_axis=0, tiled=True)]
    new = [own] + [
        lax.ppermute(own, ("tp", "sp"), [(i, i ^ s) for i in range(lanes)])
        for s in range(1, lanes)
    ]
    lane_rows = pl.pallas_call(
        functools.partial(build_rows, sources=sources, pre_count=len(pre)),
        in_specs=[smem] + [vmem] * (len(pre) + len(new)),
        out_specs=vmem,
        out_shape=jax.ShapeDtypeStruct((1, page_count * rows_lane, KEY_W), dtype),
        scratch_shapes=[pltpu.VMEM((key_count, KEY_W), dtype)],
        compiler_params=params,
        cost_estimate=pl.CostEstimate(flops=4 * 10**9, bytes_accessed=10**7, transcendentals=0),
        name="build_rows",
    )(facts, *pre, *new)
    if direct:
        landed = [lane_rows] + [shifted(lane_rows, s) for s in range(1, sources)]
    else:
        landed = [lax.all_gather(lane_rows, "pool", axis=0, tiled=True)]
    pairs = heads // 2
    while pairs > 1 and pairs * count * key_count > 1024 * 384:
        pairs //= 2
    latent_out = pl.pallas_call(
        functools.partial(attend, sources=sources, pre_count=len(pre), pairs=pairs),
        in_specs=[smem] + [vmem] * (1 + len(pre) + len(new)),
        out_specs=hbm,
        out_shape=jax.ShapeDtypeStruct((1, count, heads * LAT), dtype),
        scratch_shapes=[
            pltpu.VMEM((count, heads * LAT), dtype),
            pltpu.VMEM((key_count, KEY_W), dtype),
            pltpu.VMEM((key_count, WIDE), dtype),
            pltpu.VMEM((key_count, WIDE), dtype),
            pltpu.VMEM((count, key_count), jnp.float32),
            pltpu.SemaphoreType.DMA((heads,)),
        ],
        compiler_params=params,
        cost_estimate=pl.CostEstimate(
            flops=2 * count * heads * key_count * (KEY_W + LAT),
            bytes_accessed=2 * count * heads * (KEY_W + LAT),
            transcendentals=count * heads * key_count,
        ),
        name="attend",
    )(facts, queries, *pre, *new)
    decode_pages = pl.pallas_call(
        functools.partial(land_rows, sources=sources),
        in_specs=[smem] + [vmem] * len(landed),
        out_specs=hbm,
        out_shape=jax.ShapeDtypeStruct((1, MOST, page_count * rows_lane, KEY_W), dtype),
        scratch_shapes=[
            pltpu.VMEM((page_count * rows_lane, KEY_W), dtype),
            pltpu.SemaphoreType.DMA((MOST,)),
        ],
        compiler_params=params,
        name="land_rows",
    )(facts, *landed)
    return latent_out, decode_pages.reshape(1, MOST, page_count, rows_lane, KEY_W)


def solution(mesh):
    in_specs = (
        P(("parts", "pool"), "sp", "tp"),
        P(("parts", "pool"), ("tp", "sp"), None),
        P("parts", "pool", None),
        P("parts"),
        P("parts"),
        P("parts"),
        P("parts"),
    )
    out_specs = (
        P(("parts", "pool"), "sp", "tp"),
        P(("parts", "pool"), None, None, ("tp", "sp"), None),
    )
    return jax.shard_map(body, mesh=mesh, in_specs=in_specs, out_specs=out_specs, check_vma=False)
```

time: 35.8 us -> 31.9 us (0.89)
  local copies, waits for them, and re-layouts: 6.98 us -> 2.3 us
  waiting for transfers between devices: 2.45 us -> 3.22 us
  starting transfers between devices: 13.2 us -> 13.6 us
    unnamed x16 -> x8, local copies, waits for them, and re-layouts: 6.98 us -> 2.3 us
    pallas_call x1, Pallas kernels: 9.52 us -> 8.06 us  [body(): pl.pallas_call(functools.partial(attend, sources=sources, pre_count=len(p...]
    pallas_call x1, Pallas kernels: 0.57 us -> 1.73 us  [body(): pl.pallas_call(pick_prefix, in_specs=[hbm] * 6, out_specs=[smem] + [vmem]...]
    ppermute x6, waiting for transfers between devices: 2.44 us -> 3.22 us  [shifted(): return lax.ppermute(piece, 'pool', pairs)]
    ppermute x6, starting transfers between devices: 11.3 us -> 11.7 us  [shifted(): return lax.ppermute(piece, 'pool', pairs)]
  transfers between devices with their start and end apart: 9 -> 9, of which waited for: 2 -> 3; matrix products, arithmetic and copies ran while one was open for 0% -> 0% of each run, Pallas kernels for 27% -> 25%
where the time goes in v2:
time: 31.9 us; the launch traced here: 31.7 us
  starting transfers between devices  13.6 us (43%)
  Pallas kernels  11.9 us (37%)
  waiting for transfers between devices  3.22 us (10%)
  local copies, waits for them, and re-layouts  2.3 us (7%)
  between operations  0.69 us (2%)
    ppermute x6, starting transfers between devices, shifted(): return lax.ppermute(piece, 'pool', pairs)  11.7 us
    pallas_call x1, Pallas kernels, body(): pl.pallas_call(functools.partial(attend, sources=sources, pre_count=len(p...  8.06 us
    ppermute x6, waiting for transfers between devices, shifted(): return lax.ppermute(piece, 'pool', pairs)  3.22 us
    unnamed x8, local copies, waits for them, and re-layouts  2.3 us
    ppermute x3, starting transfers between devices, body(): lax.ppermute(own, ('tp', 'sp'), [(i, i ^ s) for i in range(lanes)])  1.86 us
    pallas_call x1, Pallas kernels, body(): pl.pallas_call(pick_prefix, in_specs=[hbm] * 6, out_specs=[smem] + [vmem]...  1.73 us
    pallas_call x1, Pallas kernels, body(): pl.pallas_call(functools.partial(land_rows, sources=sources), in_specs=[s...  1.26 us
    pallas_call x1, Pallas kernels, body(): pl.pallas_call(functools.partial(build_rows, sources=sources, pre_count=l...  0.83 us
  transfers between devices with their start and end apart: 9, of which 3 were waited for; matrix products, arithmetic and copies ran while one was open for 0% of the time, Pallas kernels for 25%

profile of v2, /device:TPU:0, one launch (start us, length us, event | category | flops | bytes accessed | tf_op | source)
XLA Modules:
  0.0 31.7 jit_solution(3500431266985324497)
XLA Ops:
  0.6 1.7 %pick_prefix.1 = (s32[4]{0:T(128)}, bf16[1,64,576]{2,1,0:T(8,128)(2,1)}, bf16[1,32,576]{2,1,0:T(8,128)(2,1)}, bf16[1,32,576]{2,1,0:T(8,128)(2,1)}, bf16[1,32,576...) custom-call(s32[4]{0:T(128)} %queue.1, s32[4]{0:T(128)} %pre_len.1, s32[4]{0:T(128)} %blk_len.1, s32[4]{0:T(128)} %dest.1, ...), custom_call_target="tpu_custom_call" | custom-call | tf_op jit(solution)/shard_map/pick_prefix/pallas_call | solution.py:208
  2.4 3.1 %collective-permute-start = (bf16[1,32,576]{2,1,0:T(8,128)(2,1)}, bf16[1,32,576]{2,1,0:T(8,128)(2,1)S(1)}, u32[]{:S(2)}, u32[]{:S(2)}) collective-permute-start(bf16[1,32,576]{2,1,0:T(8,128)(2,1)} %get-tuple-element.10), channel_id=1, source_target_pairs={{0,4},{4,8},{8,12},{12,0},{1,5},{5,9},{9,13},{13,1},{2,6},{6,10},{... | collective-permute-start | bytes 110600 | tf_op jit(solution)/shard_map/ppermute | solution.py:204
  5.4 0.7 %collective-permute-start.5 = (bf16[1,64,576]{2,1,0:T(8,128)(2,1)}, bf16[1,64,576]{2,1,0:T(8,128)(2,1)S(1)}, u32[]{:S(2)}, u32[]{:S(2)}) collective-permute-start(bf16[1,64,576]{2,1,0:T(8,128)(2,1)} %get-tuple-element.13.refs_4_), channel_id=1, source_target_pairs={{0,3},{1,2},{2,1},{3,0},{4,7},{5,6},{6,5},{7,4},{8,11},{9,10},{10,... | collective-permute-start | bytes 221192 | tf_op jit(solution)/shard_map/ppermute | solution.py:230
  6.1 0.9 %collective-permute-start.4 = (bf16[1,64,576]{2,1,0:T(8,128)(2,1)}, bf16[1,64,576]{2,1,0:T(8,128)(2,1)S(1)}, u32[]{:S(2)}, u32[]{:S(2)}) collective-permute-start(bf16[1,64,576]{2,1,0:T(8,128)(2,1)} %get-tuple-element.13.refs_4_), channel_id=1, source_target_pairs={{0,2},{1,3},{2,0},{3,1},{4,6},{5,7},{6,4},{7,5},{8,10},{9,11},{10,... | collective-permute-start | bytes 221192 | tf_op jit(solution)/shard_map/ppermute | solution.py:230
  7.0 0.3 %collective-permute-start.3 = (bf16[1,64,576]{2,1,0:T(8,128)(2,1)}, bf16[1,64,576]{2,1,0:T(8,128)(2,1)S(1)}, u32[]{:S(2)}, u32[]{:S(2)}) collective-permute-start(bf16[1,64,576]{2,1,0:T(8,128)(2,1)} %get-tuple-element.13.refs_4_), channel_id=1, source_target_pairs={{0,1},{1,0},{2,3},{3,2},{4,5},{5,4},{6,7},{7,6},{8,9},{9,8},{10,11... | collective-permute-start | bytes 221192 | tf_op jit(solution)/shard_map/ppermute | solution.py:230
  7.3 2.6 %collective-permute-start.1 = (bf16[1,32,576]{2,1,0:T(8,128)(2,1)}, bf16[1,32,576]{2,1,0:T(8,128)(2,1)S(1)}, u32[]{:S(2)}, u32[]{:S(2)}) collective-permute-start(bf16[1,32,576]{2,1,0:T(8,128)(2,1)} %get-tuple-element.11), channel_id=1, source_target_pairs={{0,8},{4,12},{8,0},{12,4},{1,9},{5,13},{9,1},{13,5},{2,10},{6,14},... | collective-permute-start | bytes 110600 | tf_op jit(solution)/shard_map/ppermute | solution.py:204
  9.9 0.0 collective-permute-done.refs_1_
  9.9 1.8 %collective-permute-start.2 = (bf16[1,32,576]{2,1,0:T(8,128)(2,1)}, bf16[1,32,576]{2,1,0:T(8,128)(2,1)S(1)}, u32[]{:S(2)}, u32[]{:S(2)}) collective-permute-start(bf16[1,32,576]{2,1,0:T(8,128)(2,1)} %get-tuple-element.12), channel_id=1, source_target_pairs={{0,12},{4,0},{8,4},{12,8},{1,13},{5,1},{9,5},{13,9},{2,14},{6,2},{... | collective-permute-start | bytes 110600 | tf_op jit(solution)/shard_map/ppermute | solution.py:204
  11.7 1.4 %collective-permute-done.1.refs_2_ = bf16[1,32,576]{2,1,0:T(8,128)(2,1)S(1)} collective-permute-done((bf16[1,32,576]{2,1,0:T(8,128)(2,1)}, bf16[1,32,576]{2,1,0:T(8,128)(2,1)S(1)}, u32[]{:S(2)}, u32[]{:S(2)}) %collective-permute-start.1) | collective-permute-done | bytes 36896 | tf_op jit(solution)/shard_map/ppermute | solution.py:204
  13.1 1.0 %collective-permute-done.2.refs_3_ = bf16[1,32,576]{2,1,0:T(8,128)(2,1)S(1)} collective-permute-done((bf16[1,32,576]{2,1,0:T(8,128)(2,1)}, bf16[1,32,576]{2,1,0:T(8,128)(2,1)S(1)}, u32[]{:S(2)}, u32[]{:S(2)}) %collective-permute-start.2) | collective-permute-done | bytes 36896 | tf_op jit(solution)/shard_map/ppermute | solution.py:204
  14.1 0.0 collective-permute-done.5.refs_7_
  14.1 0.0 collective-permute-done.4.refs_6_
  14.1 0.0 collective-permute-done.3.refs_5_
  14.1 0.0 copy-start
  14.1 0.6 %copy-done = s32[4]{0:T(128)S(1)} copy-done((s32[4]{0:T(128)S(1)}, s32[4]{0:T(128)}, u32[]{:S(2)}) %copy-start) | copy-done | bytes 40
  14.8 0.0 copy-start.2
  14.8 0.9 %copy-done.2 = bf16[1,64,576]{2,1,0:T(8,128)(2,1)S(1)} copy-done((bf16[1,64,576]{2,1,0:T(8,128)(2,1)S(1)}, bf16[1,64,576]{2,1,0:T(8,128)(2,1)}, u32[]{:S(2)}) %copy-start.2) | copy-done | bytes 73752
  15.7 0.0 copy-start.3
  15.7 0.8 %copy-done.3 = bf16[1,32,576]{2,1,0:T(8,128)(2,1)S(1)} copy-done((bf16[1,32,576]{2,1,0:T(8,128)(2,1)S(1)}, bf16[1,32,576]{2,1,0:T(8,128)(2,1)}, u32[]{:S(2)}) %copy-start.3) | copy-done | bytes 36888
  16.4 0.0 copy-start.1
  16.4 0.8 %build_rows.1.refs_0_ = bf16[1,96,576]{2,1,0:T(8,128)(2,1)S(1)} custom-call(s32[4]{0:T(128)S(1)} %copy-done, bf16[1,32,576]{2,1,0:T(8,128)(2,1)S(1)} %copy-done.3, bf16[1,32,576]{2,1,0:T(8,128)(2,1)S(1)} %collective-permute-done.refs_1_, bf16[1,32,576]{2,1,0:T(8,128)(2,1)S(1)} %collective-permute-done.1.refs_2_, ...), custom_call_target="tpu_custom_call" | custom-call | flops 4000000000 | bytes 10000000 | tf_op jit(solution)/shard_map/build_rows/pallas_call | solution.py:233
  17.3 3.6 %collective-permute-start.8 = (bf16[1,96,576]{2,1,0:T(8,128)(2,1)S(1)}, bf16[1,96,576]{2,1,0:T(8,128)(2,1)S(1)}, u32[]{:S(2)}, u32[]{:S(2)}) collective-permute-start(bf16[1,96,576]{2,1,0:T(8,128)(2,1)S(1)} %build_rows.1.refs_0_), channel_id=1, source_target_pairs={{0,12},{4,0},{8,4},{12,8},{1,13},{5,1},{9,5},{13,9},{2,14},{6,2},{... | collective-permute-start | bytes 331784 | tf_op jit(solution)/shard_map/ppermute | solution.py:204
  20.9 0.0 collective-permute-start.7
  20.9 0.6 %collective-permute-start.6 = (bf16[1,96,576]{2,1,0:T(8,128)(2,1)S(1)}, bf16[1,96,576]{2,1,0:T(8,128)(2,1)S(1)}, u32[]{:S(2)}, u32[]{:S(2)}) collective-permute-start(bf16[1,96,576]{2,1,0:T(8,128)(2,1)S(1)} %build_rows.1.refs_0_), channel_id=1, source_target_pairs={{0,4},{4,8},{8,12},{12,0},{1,5},{5,9},{9,13},{13,1},{2,6},{6,10},{... | collective-permute-start | bytes 331784 | tf_op jit(solution)/shard_map/ppermute | solution.py:204
  21.6 0.0 copy-done.1
  21.6 8.1 %attend.1 = bf16[1,128,16384]{2,1,0:T(8,128)(2,1)} custom-call(s32[4]{0:T(128)S(1)} %copy-done, bf16[1,128,18432]{2,1,0:T(8,128)(2,1)S(1)} %copy-done.1, bf16[1,32,576]{2,1,0:T(8,128)(2,1)S(1)} %copy-done.3, bf16[1,32,576]{2,1,0:T(8,128)(2,1)S(1)} %collective-permute-done.refs_1_, bf16[1,32,576]{2,1,0:T(8,128)(2,1)S(1)} %collective-permute-done.1.refs_2_, ...), custom_call_target="tpu_custom_call" | custom-call | flops 3422552064 | bytes 8912896 | tf_op jit(solution)/shard_map/attend/pallas_call | solution.py:250
  29.6 0.0 collective-permute-done.8.refs_3_
  29.6 0.8 %collective-permute-done.7.refs_2_ = bf16[1,96,576]{2,1,0:T(8,128)(2,1)S(1)} collective-permute-done((bf16[1,96,576]{2,1,0:T(8,128)(2,1)S(1)}, bf16[1,96,576]{2,1,0:T(8,128)(2,1)S(1)}, u32[]{:S(2)}, u32[]{:S(2)}) %collective-permute-start.7) | collective-permute-done | bytes 110624 | tf_op jit(solution)/shard_map/ppermute | solution.py:204
  30.4 0.0 collective-permute-done.6.refs_1_
  30.4 1.3 %land_rows.1 = bf16[1,2,96,576]{3,2,1,0:T(8,128)(2,1)} custom-call(s32[4]{0:T(128)S(1)} %copy-done, bf16[1,96,576]{2,1,0:T(8,128)(2,1)S(1)} %build_rows.1.refs_0_, bf16[1,96,576]{2,1,0:T(8,128)(2,1)S(1)} %collective-permute-done.6.refs_1_, bf16[1,96,576]{2,1,0:T(8,128)(2,1)S(1)} %collective-permute-done.7.refs_2_, ...), custom_call_target="tpu_custom_call" | custom-call | tf_op jit(solution)/shard_map/land_rows/pallas_call | solution.py:271
Async XLA Ops:
  2.4 7.5 %collective-permute-start = (bf16[1,32,576]{2,1,0:T(8,128)(2,1)}, bf16[1,32,576]{2,1,0:T(8,128)(2,1)S(1)}, u32[]{:S(2)}, u32[]{:S(2)}) collective-permute-start(bf16[1,32,576]{2,1,0:T(8,128)(2,1)} %get-tuple-element.10), channel_id=1, source_target_pairs={{0,4},{4,8},{8,12},{12,0},{1,5},{5,9},{9,13},{13,1},{2,6},{6,10},{... | collective-permute-start | bytes 110600 | tf_op jit(solution)/shard_map/ppermute | solution.py:204
  5.4 8.7 %collective-permute-start.5 = (bf16[1,64,576]{2,1,0:T(8,128)(2,1)}, bf16[1,64,576]{2,1,0:T(8,128)(2,1)S(1)}, u32[]{:S(2)}, u32[]{:S(2)}) collective-permute-start(bf16[1,64,576]{2,1,0:T(8,128)(2,1)} %get-tuple-element.13.refs_4_), channel_id=1, source_target_pairs={{0,3},{1,2},{2,1},{3,0},{4,7},{5,6},{6,5},{7,4},{8,11},{9,10},{10,... | collective-permute-start | bytes 221192 | tf_op jit(solution)/shard_map/ppermute | solution.py:230
  6.1 8.0 %collective-permute-start.4 = (bf16[1,64,576]{2,1,0:T(8,128)(2,1)}, bf16[1,64,576]{2,1,0:T(8,128)(2,1)S(1)}, u32[]{:S(2)}, u32[]{:S(2)}) collective-permute-start(bf16[1,64,576]{2,1,0:T(8,128)(2,1)} %get-tuple-element.13.refs_4_), channel_id=1, source_target_pairs={{0,2},{1,3},{2,0},{3,1},{4,6},{5,7},{6,4},{7,5},{8,10},{9,11},{10,... | collective-permute-start | bytes 221192 | tf_op jit(solution)/shard_map/ppermute | solution.py:230
  7.0 7.2 %collective-permute-start.3 = (bf16[1,64,576]{2,1,0:T(8,128)(2,1)}, bf16[1,64,576]{2,1,0:T(8,128)(2,1)S(1)}, u32[]{:S(2)}, u32[]{:S(2)}) collective-permute-start(bf16[1,64,576]{2,1,0:T(8,128)(2,1)} %get-tuple-element.13.refs_4_), channel_id=1, source_target_pairs={{0,1},{1,0},{2,3},{3,2},{4,5},{5,4},{6,7},{7,6},{8,9},{9,8},{10,11... | collective-permute-start | bytes 221192 | tf_op jit(solution)/shard_map/ppermute | solution.py:230
  7.3 5.8 %collective-permute-start.1 = (bf16[1,32,576]{2,1,0:T(8,128)(2,1)}, bf16[1,32,576]{2,1,0:T(8,128)(2,1)S(1)}, u32[]{:S(2)}, u32[]{:S(2)}) collective-permute-start(bf16[1,32,576]{2,1,0:T(8,128)(2,1)} %get-tuple-element.11), channel_id=1, source_target_pairs={{0,8},{4,12},{8,0},{12,4},{1,9},{5,13},{9,1},{13,5},{2,10},{6,14},... | collective-permute-start | bytes 110600 | tf_op jit(solution)/shard_map/ppermute | solution.py:204
  9.9 4.2 %collective-permute-start.2 = (bf16[1,32,576]{2,1,0:T(8,128)(2,1)}, bf16[1,32,576]{2,1,0:T(8,128)(2,1)S(1)}, u32[]{:S(2)}, u32[]{:S(2)}) collective-permute-start(bf16[1,32,576]{2,1,0:T(8,128)(2,1)} %get-tuple-element.12), channel_id=1, source_target_pairs={{0,12},{4,0},{8,4},{12,8},{1,13},{5,1},{9,5},{13,9},{2,14},{6,2},{... | collective-permute-start | bytes 110600 | tf_op jit(solution)/shard_map/ppermute | solution.py:204
  14.1 0.6 %copy-start = (s32[4]{0:T(128)S(1)}, s32[4]{0:T(128)}, u32[]{:S(2)}) copy-start(s32[4]{0:T(128)} %get-tuple-element.8.facts) | copy-start | bytes 52
  14.8 0.9 %copy-start.2 = (bf16[1,64,576]{2,1,0:T(8,128)(2,1)S(1)}, bf16[1,64,576]{2,1,0:T(8,128)(2,1)}, u32[]{:S(2)}) copy-start(bf16[1,64,576]{2,1,0:T(8,128)(2,1)} %get-tuple-element.13.refs_4_) | copy-start | bytes 221188
  15.7 0.8 %copy-start.3 = (bf16[1,32,576]{2,1,0:T(8,128)(2,1)S(1)}, bf16[1,32,576]{2,1,0:T(8,128)(2,1)}, u32[]{:S(2)}) copy-start(bf16[1,32,576]{2,1,0:T(8,128)(2,1)} %get-tuple-element.9.refs_0_) | copy-start | bytes 110596
  16.4 5.1 %copy-start.1 = (bf16[1,128,18432]{2,1,0:T(8,128)(2,1)S(1)}, bf16[1,128,18432]{2,1,0:T(8,128)(2,1)}, u32[]{:S(2)}) copy-start(bf16[1,128,18432]{2,1,0:T(8,128)(2,1)} %queries.1) | copy-start | bytes 14155780
  17.3 12.4 %collective-permute-start.8 = (bf16[1,96,576]{2,1,0:T(8,128)(2,1)S(1)}, bf16[1,96,576]{2,1,0:T(8,128)(2,1)S(1)}, u32[]{:S(2)}, u32[]{:S(2)}) collective-permute-start(bf16[1,96,576]{2,1,0:T(8,128)(2,1)S(1)} %build_rows.1.refs_0_), channel_id=1, source_target_pairs={{0,12},{4,0},{8,4},{12,8},{1,13},{5,1},{9,5},{13,9},{2,14},{6,2},{... | collective-permute-start | bytes 331784 | tf_op jit(solution)/shard_map/ppermute | solution.py:204
  20.9 9.5 %collective-permute-start.7 = (bf16[1,96,576]{2,1,0:T(8,128)(2,1)S(1)}, bf16[1,96,576]{2,1,0:T(8,128)(2,1)S(1)}, u32[]{:S(2)}, u32[]{:S(2)}) collective-permute-start(bf16[1,96,576]{2,1,0:T(8,128)(2,1)S(1)} %build_rows.1.refs_0_), channel_id=1, source_target_pairs={{0,8},{4,12},{8,0},{12,4},{1,9},{5,13},{9,1},{13,5},{2,10},{6,14},... | collective-permute-start | bytes 331784 | tf_op jit(solution)/shard_map/ppermute | solution.py:204
  20.9 9.5 %collective-permute-start.6 = (bf16[1,96,576]{2,1,0:T(8,128)(2,1)S(1)}, bf16[1,96,576]{2,1,0:T(8,128)(2,1)S(1)}, u32[]{:S(2)}, u32[]{:S(2)}) collective-permute-start(bf16[1,96,576]{2,1,0:T(8,128)(2,1)S(1)} %build_rows.1.refs_0_), channel_id=1, source_target_pairs={{0,4},{4,8},{8,12},{12,0},{1,5},{5,9},{9,13},{13,1},{2,6},{6,10},{... | collective-permute-start | bytes 331784 | tf_op jit(solution)/shard_map/ppermute | solution.py:204

commit v3 on v2

v3 whole, which is shorter than its diff:
```python
import functools
import math

import jax
import jax.numpy as jnp
from jax import lax
from jax.experimental import pallas as pl
from jax.experimental.pallas import tpu as pltpu
from jax.sharding import PartitionSpec as P

LAT = 512
ROPE = 64
KEY_W = LAT + ROPE
PAIR_W = 2 * KEY_W
WIDE = LAT + 2 * ROPE
QK = 192
PG = 64
MOST = 2
DIRECT = 8
EXPONENT = QK**-0.5 * math.log2(math.e)
VMEM_LIMIT = 48 * 2**20
VMEM_FIRST = 60 * 2**20


def lane_index():
    return lax.axis_index("tp") * lax.axis_size("sp") + lax.axis_index("sp")


def lane_count():
    return lax.axis_size("tp") * lax.axis_size("sp")


def shift_of(source, sources):
    return lax.rem(lax.axis_index("pool") - source + sources, sources)


def slot_groups(dest, target, sources):
    found = [jnp.int32(-1)] * MOST
    rank = jnp.int32(0)
    for g in range(sources):
        hit = dest[g] == target
        for slot in range(MOST):
            found[slot] = jnp.where(hit & (rank == slot), g, found[slot])
        rank = rank + hit.astype(jnp.int32)
    return found


def lane_positions(slots):
    rows_lane = PG // lane_count()
    return slots // rows_lane * PG + lane_index() * rows_lane + slots % rows_lane


def slots_before(length, pages):
    rows_lane = PG // lane_count()
    total = jnp.int32(0)
    for m in range(pages):
        total = total + jnp.clip(length - m * PG - lane_index() * rows_lane, 0, rows_lane)
    return total


def new_index(columns, rows):
    return (lane_index() ^ (columns // rows)) * rows + columns % rows


def pick_prefix(queue, dest, cache, *refs):
    outs, (lists, held, signals) = refs[:-3], refs[-3:]
    me = lax.axis_index("pool")
    count, rows = cache.shape[:2]
    copies = [
        pltpu.make_async_copy(source, target, signals.at[i])
        for i, (source, target) in enumerate(
            ((queue, lists.at[0]), (dest, lists.at[1]), (cache, held))
        )
    ]
    for copy in copies:
        copy.start()
    for copy in copies:
        copy.wait()
    if len(outs) == 1:
        for s in range(count):
            outs[0][s] = held[lists[0, s]]
        return
    rows_lane = PG // lane_count()
    begin = pl.multiple_of(lax.rem(lane_index() * rows_lane, rows), rows_lane)
    for s, out in enumerate(outs, 1):
        target = lax.rem(me + s, count)
        out[0, :rows] = held[lists[0, target]]
        groups = slot_groups(lists.at[1], target, count)
        for slot, group in enumerate(groups):
            request = lists[0, jnp.maximum(group, 0)]
            at = rows + slot * rows_lane
            out[0, at : at + rows_lane] = held[request, pl.ds(begin, rows_lane)]


def build_new(queue, pre_len, blk_len, *refs, pages):
    new, out = refs[:-1], refs[-1]
    me = lax.axis_index("pool")
    pre_length = pre_len[queue[me]]
    rows = new[0].shape[1]
    shape = (out.shape[1], rows * len(new))
    slot = lax.broadcasted_iota(jnp.int32, shape, 0) + slots_before(pre_length, pages)
    offset = lane_positions(slot) - pre_length
    index = new_index(lax.broadcasted_iota(jnp.int32, shape, 1), rows)
    picker = jnp.where((index == offset) & (offset < blk_len[me]), 1.0, 0.0)
    held = jnp.concatenate([piece[0] for piece in new], axis=0)
    out[0] = jnp.dot(
        picker.astype(held.dtype), held, preferred_element_type=jnp.float32
    ).astype(out.dtype)


def land_slots(queue, pre_len, dest, cache, *refs, sources):
    pre, landed = refs[: sources - 1], refs[sources - 1 : 2 * sources - 1]
    out, held, built, signals = refs[2 * sources - 1 :]
    me = lax.axis_index("pool")
    rows = cache.shape[1]
    rows_lane = PG // lane_count()
    pages = sources * rows // PG
    new_rows = landed[0].shape[1]
    first = lane_index() * rows_lane
    begin = pl.multiple_of(lax.rem(first, rows), rows_lane)
    copies = []
    for slot, group in enumerate(slot_groups(dest, me, sources)):
        request = queue[jnp.maximum(group, 0)]
        pre_length = jnp.where(group < 0, 0, pre_len[request])
        for g in range(sources):
            for s, piece in enumerate(landed):

                @pl.when((group == g) & (shift_of(g, sources) == s))
                def _(piece=piece, slot=slot):
                    held[slot, :new_rows] = piece[0]

        @pl.when(group < 0)
        def _(slot=slot):
            held[slot, :new_rows] = jnp.zeros((new_rows, KEY_W), held.dtype)

        for m in range(pages):
            shift = shift_of((m * PG + first) // rows, sources)
            at = new_rows + m * rows_lane

            @pl.when(shift == 0)
            def _(at=at, slot=slot, request=request):
                held[slot, at : at + rows_lane] = cache[request, pl.ds(begin, rows_lane)]

            for s, piece in enumerate(pre, 1):

                @pl.when(shift == s)
                def _(at=at, slot=slot, piece=piece):
                    start = rows + slot * rows_lane
                    held[slot, at : at + rows_lane] = piece[0, start : start + rows_lane]

        shape = (built.shape[1], held.shape[1])
        row = lax.broadcasted_iota(jnp.int32, shape, 0)
        column = lax.broadcasted_iota(jnp.int32, shape, 1)
        behind = row - slots_before(pre_length, pages)
        chosen = jnp.where(
            behind < 0, row + new_rows, jnp.where(behind < new_rows, behind, -1)
        )
        picker = jnp.where(column == chosen, 1.0, 0.0).astype(held.dtype)
        built[slot] = jnp.dot(
            picker, held[slot], preferred_element_type=jnp.float32
        ).astype(built.dtype)
        copies.append(pltpu.make_async_copy(built.at[slot], out.at[0, slot], signals.at[slot]))
        copies[-1].start()
    for copy in copies:
        copy.wait()


def build_rows(queue, pre_len, blk_len, pre, *refs):
    new, out = refs[:-1], refs[-1]
    me = lax.axis_index("pool")
    pre_length = pre_len[queue[me]]
    first = pre.shape[0] * pre.shape[1]
    rows = new[0].shape[1]
    held = jnp.concatenate(
        [pre[s] for s in range(pre.shape[0])] + [piece[0] for piece in new], axis=0
    )
    shape = (out.shape[1], held.shape[0])
    position = lane_positions(lax.broadcasted_iota(jnp.int32, shape, 0))
    column = lax.broadcasted_iota(jnp.int32, shape, 1)
    offset = position - pre_length
    index = new_index(jnp.maximum(column - first, 0), rows)
    picked = ((offset < 0) & (column == position)) | (
        (offset >= 0) & (offset < blk_len[me]) & (column >= first) & (index == offset)
    )
    picker = jnp.where(picked, 1.0, 0.0).astype(held.dtype)
    out[0] = jnp.dot(picker, held, preferred_element_type=jnp.float32).astype(out.dtype)


def land_rows(dest, landed, out, blank, signals):
    me = lax.axis_index("pool")
    blank[...] = jnp.zeros_like(blank)

    def landing(slot, source):
        return pltpu.make_async_copy(source, out.at[0, slot], signals.at[slot])

    for slot, group in enumerate(slot_groups(dest, me, landed.shape[0])):

        @pl.when(group < 0)
        def _(slot=slot):
            landing(slot, blank).start()

        @pl.when(group >= 0)
        def _(slot=slot, group=group):
            landing(slot, landed.at[group]).start()

    for slot in range(MOST):
        landing(slot, blank).wait()


def attend(queue, pre_len, blk_len, queries, cache, *refs, sources, pre_count, pairs):
    pre, new = refs[:pre_count], refs[pre_count:-6]
    out, held, even_keys, odd_keys, bias, signals = refs[-6:]
    me = lax.axis_index("pool")
    count = queries.shape[1]
    heads = queries.shape[2] // KEY_W
    request = queue[me]
    pre_length = pre_len[request]
    blk_length = blk_len[me]
    first_query = lax.axis_index("sp") * count
    rows = cache.shape[1]
    new_rows = new[0].shape[1]
    first = sources * rows
    column = lax.broadcasted_iota(jnp.int32, bias.shape, 1)
    if pre_count == sources - 1:
        prefix = [cache[request]] + [piece[0, :rows] for piece in pre]
        position = lax.rem(me - column // rows + sources, sources) * rows + column % rows
    else:
        prefix = [pre[0][s] for s in range(sources)]
        position = column
    keys = jnp.concatenate(prefix + [piece[0] for piece in new], axis=0)
    blank = jnp.zeros((keys.shape[0], ROPE), keys.dtype)
    even_keys[...] = jnp.concatenate([keys, blank], axis=1)
    odd_keys[...] = jnp.concatenate([blank, keys], axis=1)
    row = lax.broadcasted_iota(jnp.int32, bias.shape, 0) + first_query
    index = new_index(jnp.maximum(column - first, 0), new_rows)
    visible = ((column < first) & (position < pre_length)) | (
        (column >= first) & (index <= row) & (index < blk_length)
    )
    bias[...] = jnp.where(visible, 0.0, -jnp.inf)
    values = even_keys[:, :LAT]
    row = lax.broadcasted_iota(jnp.int32, (count, 1), 0) + first_query
    live = jnp.concatenate([row] * pairs, axis=0) < blk_length
    masked = jnp.concatenate([bias[...]] * pairs, axis=0)

    def leaving(head):
        columns = pl.ds(head * LAT, LAT)
        return pltpu.make_async_copy(held.at[:, columns], out.at[0, :, columns], signals.at[head])

    units = [(p, odd) for p in range(0, heads // 2, pairs) for odd in (0, 1)]
    for number, (pair, odd) in enumerate(units):
        starts = [(pair + p) * PAIR_W + odd * LAT for p in range(pairs)]
        some = jnp.concatenate([queries[0, :, at : at + WIDE] for at in starts], axis=0)
        scores = lax.dot_general(
            some,
            (odd_keys if odd else even_keys)[...],
            (((1,), (1,)), ((), ())),
            preferred_element_type=jnp.float32,
        )
        scores = scores + masked
        top = jnp.max(scores, axis=1, keepdims=True)
        weights = jnp.exp2((scores - top) * EXPONENT)
        scale = jnp.where(live, 1.0 / jnp.sum(weights, axis=1, keepdims=True), 0.0)
        weights = weights.astype(values.dtype)
        step = pairs if number + 1 < len(units) else max(pairs // 4, 1)
        for p in range(0, pairs, step):
            part = slice(p * count, (p + step) * count)
            mixture = jnp.dot(weights[part], values, preferred_element_type=jnp.float32)
            mixture = (mixture * scale[part]).astype(held.dtype)
            for i in range(step):
                head = 2 * (pair + p + i) + odd
                held[:, head * LAT : (head + 1) * LAT] = mixture[i * count : (i + 1) * count]
                leaving(head).start()
    for head in range(heads):
        leaving(head).wait()


def body(queries, block_latent, prefix_cache, queue_list, prefix_len, block_len, decode_dest):
    sources = lax.axis_size("pool")
    lanes = lax.axis_size("tp") * lax.axis_size("sp")
    count, width = queries.shape[1:]
    heads = width // KEY_W
    rows_in = prefix_cache.shape[1]
    pre_total = rows_in * sources
    key_count = pre_total + block_latent.shape[1] * lanes
    rows_lane = PG // lanes
    lane_total = key_count // lanes
    direct = sources <= DIRECT and PG % rows_in == 0 and rows_in % rows_lane == 0
    smem = pl.BlockSpec(memory_space=pltpu.SMEM)
    vmem = pl.BlockSpec(memory_space=pltpu.VMEM)
    hbm = pl.BlockSpec(memory_space=pltpu.HBM)
    params = pltpu.CompilerParams(vmem_limit_bytes=VMEM_LIMIT)
    dtype = queries.dtype

    def shifted(piece, s):
        pairs = [(i, (i + s) % sources) for i in range(sources)]
        return lax.ppermute(piece, "pool", pairs)

    if direct:
        pieces, piece = sources - 1, (1, rows_in + MOST * rows_lane, KEY_W)
    else:
        pieces, piece = 1, (sources, rows_in, KEY_W)
    chosen = pl.pallas_call(
        pick_prefix,
        in_specs=[hbm] * 3,
        out_specs=[vmem] * pieces,
        out_shape=[jax.ShapeDtypeStruct(piece, dtype)] * pieces,
        scratch_shapes=[
            pltpu.SMEM((2, sources), jnp.int32),
            pltpu.VMEM(prefix_cache.shape, dtype),
            pltpu.SemaphoreType.DMA((3,)),
        ],
        compiler_params=pltpu.CompilerParams(vmem_limit_bytes=VMEM_FIRST),
        cost_estimate=pl.CostEstimate(flops=4 * 10**9, bytes_accessed=10**7, transcendentals=0),
        name="pick_prefix",
    )(queue_list, decode_dest, prefix_cache)
    if direct:
        pre = [shifted(chosen[s - 1], s) for s in range(1, sources)]
    else:
        pre = [lax.all_to_all(chosen[0], "pool", split_axis=0, concat_axis=0, tiled=True)]
    new = [block_latent] + [
        lax.ppermute(block_latent, ("tp", "sp"), [(i, i ^ s) for i in range(lanes)])
        for s in range(1, lanes)
    ]
    scalars = (queue_list, prefix_len, block_len)
    lane_new = block_latent.shape[1]
    build = functools.partial(
        pl.pallas_call,
        out_specs=vmem,
        compiler_params=params,
        cost_estimate=pl.CostEstimate(flops=4 * 10**9, bytes_accessed=10**7, transcendentals=0),
    )
    if direct:
        lane_rows = build(
            functools.partial(build_new, pages=pre_total // PG),
            in_specs=[smem] * 3 + [vmem] * len(new),
            out_shape=jax.ShapeDtypeStruct((1, lane_new, KEY_W), dtype),
            name="build_new",
        )(*scalars, *new)
        landed = [lane_rows] + [shifted(lane_rows, s) for s in range(1, sources)]
    else:
        lane_rows = build(
            build_rows,
            in_specs=[smem] * 3 + [vmem] * (1 + len(new)),
            out_shape=jax.ShapeDtypeStruct((1, lane_total, KEY_W), dtype),
            name="build_rows",
        )(*scalars, *pre, *new)
        landed = [lax.all_gather(lane_rows, "pool", axis=0, tiled=True)]
    pairs = heads // 2
    while pairs > 1 and pairs * count * key_count > 1024 * 384:
        pairs //= 2
    latent_out = pl.pallas_call(
        functools.partial(attend, sources=sources, pre_count=len(pre), pairs=pairs),
        in_specs=[smem] * 3 + [vmem] * (2 + len(pre) + len(new)),
        out_specs=hbm,
        out_shape=jax.ShapeDtypeStruct((1, count, heads * LAT), dtype),
        scratch_shapes=[
            pltpu.VMEM((count, heads * LAT), dtype),
            pltpu.VMEM((key_count, WIDE), dtype),
            pltpu.VMEM((key_count, WIDE), dtype),
            pltpu.VMEM((count, key_count), jnp.float32),
            pltpu.SemaphoreType.DMA((heads,)),
        ],
        compiler_params=params,
        cost_estimate=pl.CostEstimate(
            flops=2 * count * heads * key_count * (KEY_W + LAT),
            bytes_accessed=2 * count * heads * (KEY_W + LAT),
            transcendentals=count * heads * key_count,
        ),
        name="attend",
    )(*scalars, queries, prefix_cache, *pre, *new)
    land = functools.partial(
        pl.pallas_call,
        out_specs=hbm,
        out_shape=jax.ShapeDtypeStruct((1, MOST, lane_total, KEY_W), dtype),
        compiler_params=params,
    )
    if direct:
        decode_pages = land(
            functools.partial(land_slots, sources=sources),
            in_specs=[smem] * 3 + [vmem] * (1 + len(pre) + len(landed)),
            scratch_shapes=[
                pltpu.VMEM((MOST, lane_new + pre_total // lanes, KEY_W), dtype),
                pltpu.VMEM((MOST, lane_total, KEY_W), dtype),
                pltpu.SemaphoreType.DMA((MOST,)),
            ],
            name="land_slots",
        )(queue_list, prefix_len, decode_dest, prefix_cache, *pre, *landed)
    else:
        decode_pages = land(
            land_rows,
            in_specs=[smem, vmem],
            scratch_shapes=[
                pltpu.VMEM((lane_total, KEY_W), dtype),
                pltpu.SemaphoreType.DMA((MOST,)),
            ],
            name="land_rows",
        )(decode_dest, *landed)
    return latent_out, decode_pages.reshape(1, MOST, key_count // PG, rows_lane, KEY_W)


def solution(mesh):
    in_specs = (
        P(("parts", "pool"), "sp", "tp"),
        P(("parts", "pool"), ("tp", "sp"), None),
        P("parts", "pool", None),
        P("parts"),
        P("parts"),
        P("parts"),
        P("parts"),
    )
    out_specs = (
        P(("parts", "pool"), "sp", "tp"),
        P(("parts", "pool"), None, None, ("tp", "sp"), None),
    )
    return jax.shard_map(body, mesh=mesh, in_specs=in_specs, out_specs=out_specs, check_vma=False)
```

time: 31.9 us -> 28.6 us (0.90)
  the two profiles are of different devices: /device:TPU:0 before, /device:TPU:28 now
where the time goes in v3:
time: 28.6 us; the launch traced here: 28.4 us
  Pallas kernels  12.3 us (43%)
  starting transfers between devices  9.26 us (32%)
  waiting for transfers between devices  6.04 us (21%)
  between operations  0.78 us (3%)
    pallas_call x1, Pallas kernels, body(): pl.pallas_call(functools.partial(attend, sources=sources, pre_count=len(p...  8.07 us
    ppermute x6, starting transfers between devices, shifted(): return lax.ppermute(piece, 'pool', pairs)  7.33 us
    ppermute x6, waiting for transfers between devices, shifted(): return lax.ppermute(piece, 'pool', pairs)  5.33 us
    ppermute x3, starting transfers between devices, body(): lax.ppermute(block_latent, ('tp', 'sp'), [(i, i ^ s) for i in range(lanes)])  1.93 us
    pallas_call x1, Pallas kernels, body(): land(functools.partial(land_slots, sources=sources), in_specs=[smem] * 3...  1.86 us
    pallas_call x1, Pallas kernels, body(): pl.pallas_call(pick_prefix, in_specs=[hbm] * 3, out_specs=[vmem] * pieces...  1.65 us
    pallas_call x1, Pallas kernels, body(): build(functools.partial(build_new, pages=pre_total // PG), in_specs=[smem...  0.74 us
    ppermute x3, waiting for transfers between devices, body(): lax.ppermute(block_latent, ('tp', 'sp'), [(i, i ^ s) for i in range(lanes)])  0.71 us
  transfers between devices with their start and end apart: 9, of which 2 were waited for; matrix products, arithmetic and copies ran while one was open for 0% of the time, Pallas kernels for 37%

profile of v3, /device:TPU:28, one launch (start us, length us, event | category | flops | bytes accessed | tf_op | source)
XLA Modules:
  0.0 28.4 jit_solution(9691164440513505825)
XLA Ops:
  0.6 0.0 copy-start.4
  0.6 0.0 copy-start.1
  0.7 0.0 copy-start.2
  0.7 0.0 copy-start.5
  0.7 1.0 %collective-permute-start.5 = (bf16[1,64,576]{2,1,0:T(8,128)(2,1)}, bf16[1,64,576]{2,1,0:T(8,128)(2,1)S(1)}, u32[]{:S(2)}, u32[]{:S(2)}) collective-permute-start(bf16[1,64,576]{2,1,0:T(8,128)(2,1)} %refs_0_.1), channel_id=1, source_target_pairs={{0,3},{1,2},{2,1},{3,0},{4,7},{5,6},{6,5},{7,4},{8,11},{9,10},{10,... | collective-permute-start | bytes 221192 | tf_op jit(solution)/shard_map/ppermute | solution.py:321
  1.7 0.6 %collective-permute-start.4 = (bf16[1,64,576]{2,1,0:T(8,128)(2,1)}, bf16[1,64,576]{2,1,0:T(8,128)(2,1)S(1)}, u32[]{:S(2)}, u32[]{:S(2)}) collective-permute-start(bf16[1,64,576]{2,1,0:T(8,128)(2,1)} %refs_0_.1), channel_id=1, source_target_pairs={{0,2},{1,3},{2,0},{3,1},{4,6},{5,7},{6,4},{7,5},{8,10},{9,11},{10,... | collective-permute-start | bytes 221192 | tf_op jit(solution)/shard_map/ppermute | solution.py:321
  2.3 0.3 %collective-permute-start.3 = (bf16[1,64,576]{2,1,0:T(8,128)(2,1)}, bf16[1,64,576]{2,1,0:T(8,128)(2,1)S(1)}, u32[]{:S(2)}, u32[]{:S(2)}) collective-permute-start(bf16[1,64,576]{2,1,0:T(8,128)(2,1)} %refs_0_.1), channel_id=1, source_target_pairs={{0,1},{1,0},{2,3},{3,2},{4,5},{5,4},{6,7},{7,6},{8,9},{9,8},{10,11... | collective-permute-start | bytes 221192 | tf_op jit(solution)/shard_map/ppermute | solution.py:321
  2.6 1.6 %pick_prefix.1 = (bf16[1,64,576]{2,1,0:T(8,128)(2,1)}, bf16[1,64,576]{2,1,0:T(8,128)(2,1)}, bf16[1,64,576]{2,1,0:T(8,128)(2,1)}) custom-call(s32[4]{0:T(128)} %queue.7, s32[4]{0:T(128)} %dest.3, bf16[4,32,576]{2,1,0:T(8,128)(2,1)} %cache.5), custom_call_target="tpu_custom_call" | custom-call | flops 4000000000 | bytes 10000000 | tf_op jit(solution)/shard_map/pick_prefix/pallas_call | solution.py:302
  4.3 0.3 collective-permute-start
  4.5 1.7 %collective-permute-start.1 = (bf16[1,64,576]{2,1,0:T(8,128)(2,1)}, bf16[1,64,576]{2,1,0:T(8,128)(2,1)S(1)}, u32[]{:S(2)}, u32[]{:S(2)}) collective-permute-start(bf16[1,64,576]{2,1,0:T(8,128)(2,1)} %get-tuple-element.6), channel_id=1, source_target_pairs={{0,8},{4,12},{8,0},{12,4},{1,9},{5,13},{9,1},{13,5},{2,10},{6,14},... | collective-permute-start | bytes 221192 | tf_op jit(solution)/shard_map/ppermute | solution.py:296
  6.2 0.0 collective-permute-done.5.refs_6_.refs_3_
  6.2 0.0 slice-start
  6.2 0.0 copy-start
  6.2 0.0 slice-start.1
  6.2 0.5 %collective-permute-start.2 = (bf16[1,64,576]{2,1,0:T(8,128)(2,1)}, bf16[1,64,576]{2,1,0:T(8,128)(2,1)S(1)}, u32[]{:S(2)}, u32[]{:S(2)}) collective-permute-start(bf16[1,64,576]{2,1,0:T(8,128)(2,1)} %get-tuple-element.7), channel_id=1, source_target_pairs={{0,12},{4,0},{8,4},{12,8},{1,13},{5,1},{9,5},{13,9},{2,14},{6,2},{... | collective-permute-start | bytes 221192 | tf_op jit(solution)/shard_map/ppermute | solution.py:296
  6.7 0.7 %collective-permute-done.4.refs_5_.refs_2_ = bf16[1,64,576]{2,1,0:T(8,128)(2,1)S(1)} collective-permute-done((bf16[1,64,576]{2,1,0:T(8,128)(2,1)}, bf16[1,64,576]{2,1,0:T(8,128)(2,1)S(1)}, u32[]{:S(2)}, u32[]{:S(2)}) %collective-permute-start.4) | collective-permute-done | bytes 73760 | tf_op jit(solution)/shard_map/ppermute | solution.py:321
  7.4 0.0 collective-permute-done.3.refs_4_.refs_1_
  7.5 0.0 copy-done.4
  7.5 0.0 copy-done.1
  7.5 0.0 copy-done.2
  7.5 0.0 copy-done.5
  7.5 0.7 %build_new.1.refs_3_ = bf16[1,64,576]{2,1,0:T(8,128)(2,1)S(1)} custom-call(s32[4]{0:T(128)S(1)} %copy-done.1, s32[4]{0:T(128)S(1)} %copy-done.2, s32[4]{0:T(128)S(1)} %copy-done.5, bf16[1,64,576]{2,1,0:T(8,128)(2,1)S(1)} %copy-done.4, bf16[1,64,576]{2,1,0:T(8,128)(2,1)S(1)} %collective-permute-done.3.refs_4_.refs_1_, ...), custom_call_target="tpu_custom_call" | custom-call | flops 4000000000 | bytes 10000000 | tf_op jit(solution)/shard_map/build_new/pallas_call | solution.py:333
  8.2 0.0 copy-start.3
  8.2 0.7 %collective-permute-start.8 = (bf16[1,64,576]{2,1,0:T(8,128)(2,1)S(1)}, bf16[1,64,576]{2,1,0:T(8,128)(2,1)S(1)}, u32[]{:S(2)}, u32[]{:S(2)}) collective-permute-start(bf16[1,64,576]{2,1,0:T(8,128)(2,1)S(1)} %build_new.1.refs_3_), channel_id=1, source_target_pairs={{0,12},{4,0},{8,4},{12,8},{1,13},{5,1},{9,5},{13,9},{2,14},{6,2},{... | collective-permute-start | bytes 221192 | tf_op jit(solution)/shard_map/ppermute | solution.py:296
  8.9 2.6 %collective-permute-start.7 = (bf16[1,64,576]{2,1,0:T(8,128)(2,1)S(1)}, bf16[1,64,576]{2,1,0:T(8,128)(2,1)S(1)}, u32[]{:S(2)}, u32[]{:S(2)}) collective-permute-start(bf16[1,64,576]{2,1,0:T(8,128)(2,1)S(1)} %build_new.1.refs_3_), channel_id=1, source_target_pairs={{0,8},{4,12},{8,0},{12,4},{1,9},{5,13},{9,1},{13,5},{2,10},{6,14},... | collective-permute-start | bytes 221192 | tf_op jit(solution)/shard_map/ppermute | solution.py:296
  11.5 0.0 collective-permute-done.refs_0_
  11.5 1.6 %collective-permute-start.6 = (bf16[1,64,576]{2,1,0:T(8,128)(2,1)S(1)}, bf16[1,64,576]{2,1,0:T(8,128)(2,1)S(1)}, u32[]{:S(2)}, u32[]{:S(2)}) collective-permute-start(bf16[1,64,576]{2,1,0:T(8,128)(2,1)S(1)} %build_new.1.refs_3_), channel_id=1, source_target_pairs={{0,4},{4,8},{8,12},{12,0},{1,5},{5,9},{9,13},{13,1},{2,6},{6,10},{... | collective-permute-start | bytes 221192 | tf_op jit(solution)/shard_map/ppermute | solution.py:296
  13.1 5.3 %collective-permute-done.1.refs_1_ = bf16[1,64,576]{2,1,0:T(8,128)(2,1)S(1)} collective-permute-done((bf16[1,64,576]{2,1,0:T(8,128)(2,1)}, bf16[1,64,576]{2,1,0:T(8,128)(2,1)S(1)}, u32[]{:S(2)}, u32[]{:S(2)}) %collective-permute-start.1) | collective-permute-done | bytes 73760 | tf_op jit(solution)/shard_map/ppermute | solution.py:296
  18.4 0.0 collective-permute-done.2.refs_2_
  18.4 0.0 slice-done
  18.4 0.0 copy-done
  18.4 0.0 slice-done.1
  18.5 8.1 %attend.1 = bf16[1,128,16384]{2,1,0:T(8,128)(2,1)} custom-call(s32[4]{0:T(128)S(1)} %copy-done.1, s32[4]{0:T(128)S(1)} %copy-done.2, s32[4]{0:T(128)S(1)} %copy-done.5, bf16[1,128,18432]{2,1,0:T(8,128)(2,1)S(1)} %bitcast.2, bf16[4,32,576]{2,1,0:T(8,128)(2,1)S(1)} %copy-done, bf16[1,64,576]{2,1,0:T(8,128)(2,1)S(1)} %collective-permute-done.refs_0_, ...), custom_call_target="tpu_custom_call" | custom-call | flops 3422552064 | bytes 8912896 | tf_op jit(solution)/shard_map/attend/pallas_call | solution.py:351
  26.5 0.0 collective-permute-done.8.refs_6_
  26.5 0.0 collective-permute-done.7.refs_5_
  26.6 0.0 collective-permute-done.6.refs_4_
  26.6 0.0 copy-done.3
  26.6 1.9 %land_slots.1 = bf16[1,2,96,576]{3,2,1,0:T(8,128)(2,1)} custom-call(s32[4]{0:T(128)S(1)} %copy-done.1, s32[4]{0:T(128)S(1)} %copy-done.2, s32[4]{0:T(128)S(1)} %copy-done.3, bf16[4,32,576]{2,1,0:T(8,128)(2,1)S(1)} %copy-done, bf16[1,64,576]{2,1,0:T(8,128)(2,1)S(1)} %collective-permute-done.refs_0_, bf16[1,64,576]{2,1,0:T(8,128)(2,1)S(1)} %collective-permute-done.1.refs_1_, ...), custom_call_target="tpu_custom_call" | custom-call | tf_op jit(solution)/shard_map/land_slots/pallas_call | solution.py:378
  (1 shorter events, 0.0 us)
Async XLA Ops:
  0.6 6.8 %copy-start.4 = (bf16[1,64,576]{2,1,0:T(8,128)(2,1)S(1)}, bf16[1,64,576]{2,1,0:T(8,128)(2,1)}, u32[]{:S(2)}) copy-start(bf16[1,64,576]{2,1,0:T(8,128)(2,1)} %refs_0_.1) | copy-start | bytes 221188
  0.6 6.8 %copy-start.1 = (s32[4]{0:T(128)S(1)}, s32[4]{0:T(128)}, u32[]{:S(2)}) copy-start(s32[4]{0:T(128)} %queue.7) | copy-start | bytes 52
  0.7 6.8 %copy-start.2 = (s32[4]{0:T(128)S(1)}, s32[4]{0:T(128)}, u32[]{:S(2)}) copy-start(s32[4]{0:T(128)} %pre_len.5) | copy-start | bytes 52
  0.7 6.8 %copy-start.5 = (s32[4]{0:T(128)S(1)}, s32[4]{0:T(128)}, u32[]{:S(2)}) copy-start(s32[4]{0:T(128)} %blk_len.3) | copy-start | bytes 52
  0.7 5.6 %collective-permute-start.5 = (bf16[1,64,576]{2,1,0:T(8,128)(2,1)}, bf16[1,64,576]{2,1,0:T(8,128)(2,1)S(1)}, u32[]{:S(2)}, u32[]{:S(2)}) collective-permute-start(bf16[1,64,576]{2,1,0:T(8,128)(2,1)} %refs_0_.1), channel_id=1, source_target_pairs={{0,3},{1,2},{2,1},{3,0},{4,7},{5,6},{6,5},{7,4},{8,11},{9,10},{10,... | collective-permute-start | bytes 221192 | tf_op jit(solution)/shard_map/ppermute | solution.py:321
  1.7 5.8 %collective-permute-start.4 = (bf16[1,64,576]{2,1,0:T(8,128)(2,1)}, bf16[1,64,576]{2,1,0:T(8,128)(2,1)S(1)}, u32[]{:S(2)}, u32[]{:S(2)}) collective-permute-start(bf16[1,64,576]{2,1,0:T(8,128)(2,1)} %refs_0_.1), channel_id=1, source_target_pairs={{0,2},{1,3},{2,0},{3,1},{4,6},{5,7},{6,4},{7,5},{8,10},{9,11},{10,... | collective-permute-start | bytes 221192 | tf_op jit(solution)/shard_map/ppermute | solution.py:321
  2.3 5.1 %collective-permute-start.3 = (bf16[1,64,576]{2,1,0:T(8,128)(2,1)}, bf16[1,64,576]{2,1,0:T(8,128)(2,1)S(1)}, u32[]{:S(2)}, u32[]{:S(2)}) collective-permute-start(bf16[1,64,576]{2,1,0:T(8,128)(2,1)} %refs_0_.1), channel_id=1, source_target_pairs={{0,1},{1,0},{2,3},{3,2},{4,5},{5,4},{6,7},{7,6},{8,9},{9,8},{10,11... | collective-permute-start | bytes 221192 | tf_op jit(solution)/shard_map/ppermute | solution.py:321
  4.3 7.3 %collective-permute-start = (bf16[1,64,576]{2,1,0:T(8,128)(2,1)}, bf16[1,64,576]{2,1,0:T(8,128)(2,1)S(1)}, u32[]{:S(2)}, u32[]{:S(2)}) collective-permute-start(bf16[1,64,576]{2,1,0:T(8,128)(2,1)} %get-tuple-element.5), channel_id=1, source_target_pairs={{0,4},{4,8},{8,12},{12,0},{1,5},{5,9},{9,13},{13,1},{2,6},{6,10},{... | collective-permute-start | bytes 221192 | tf_op jit(solution)/shard_map/ppermute | solution.py:296
  4.5 13.9 %collective-permute-start.1 = (bf16[1,64,576]{2,1,0:T(8,128)(2,1)}, bf16[1,64,576]{2,1,0:T(8,128)(2,1)S(1)}, u32[]{:S(2)}, u32[]{:S(2)}) collective-permute-start(bf16[1,64,576]{2,1,0:T(8,128)(2,1)} %get-tuple-element.6), channel_id=1, source_target_pairs={{0,8},{4,12},{8,0},{12,4},{1,9},{5,13},{9,1},{13,5},{2,10},{6,14},... | collective-permute-start | bytes 221192 | tf_op jit(solution)/shard_map/ppermute | solution.py:296
  6.2 12.2 %slice-start = ((s8[4718592]{0:T(1024)(128)(4,1)}), s8[4194304]{0:T(1024)(128)(4,1)S(1)}, s32[]{:S(2)}) async-start(s8[4718592]{0:T(1024)(128)(4,1)} %bitcast.1), calls=%async_computation | async-start | bytes 8388608
  6.2 12.2 %copy-start = (bf16[4,32,576]{2,1,0:T(8,128)(2,1)S(1)}, bf16[4,32,576]{2,1,0:T(8,128)(2,1)}, u32[]{:S(2)}) copy-start(bf16[4,32,576]{2,1,0:T(8,128)(2,1)} %cache.5) | copy-start | bytes 442372
  6.2 12.2 %slice-start.1 = ((s8[4718592]{0:T(1024)(128)(4,1)}), s8[524288]{0:T(1024)(128)(4,1)S(1)}, s32[]{:S(2)}) async-start(s8[4718592]{0:T(1024)(128)(4,1)} %bitcast.1), calls=%async_computation.1 | async-start | bytes 1048576
  6.2 12.2 %collective-permute-start.2 = (bf16[1,64,576]{2,1,0:T(8,128)(2,1)}, bf16[1,64,576]{2,1,0:T(8,128)(2,1)S(1)}, u32[]{:S(2)}, u32[]{:S(2)}) collective-permute-start(bf16[1,64,576]{2,1,0:T(8,128)(2,1)} %get-tuple-element.7), channel_id=1, source_target_pairs={{0,12},{4,0},{8,4},{12,8},{1,13},{5,1},{9,5},{13,9},{2,14},{6,2},{... | collective-permute-start | bytes 221192 | tf_op jit(solution)/shard_map/ppermute | solution.py:296
  8.2 18.3 %copy-start.3 = (s32[4]{0:T(128)S(1)}, s32[4]{0:T(128)}, u32[]{:S(2)}) copy-start(s32[4]{0:T(128)} %dest.3) | copy-start | bytes 52
  8.2 18.3 %collective-permute-start.8 = (bf16[1,64,576]{2,1,0:T(8,128)(2,1)S(1)}, bf16[1,64,576]{2,1,0:T(8,128)(2,1)S(1)}, u32[]{:S(2)}, u32[]{:S(2)}) collective-permute-start(bf16[1,64,576]{2,1,0:T(8,128)(2,1)S(1)} %build_new.1.refs_3_), channel_id=1, source_target_pairs={{0,12},{4,0},{8,4},{12,8},{1,13},{5,1},{9,5},{13,9},{2,14},{6,2},{... | collective-permute-start | bytes 221192 | tf_op jit(solution)/shard_map/ppermute | solution.py:296
  8.9 17.6 %collective-permute-start.7 = (bf16[1,64,576]{2,1,0:T(8,128)(2,1)S(1)}, bf16[1,64,576]{2,1,0:T(8,128)(2,1)S(1)}, u32[]{:S(2)}, u32[]{:S(2)}) collective-permute-start(bf16[1,64,576]{2,1,0:T(8,128)(2,1)S(1)} %build_new.1.refs_3_), channel_id=1, source_target_pairs={{0,8},{4,12},{8,0},{12,4},{1,9},{5,13},{9,1},{13,5},{2,10},{6,14},... | collective-permute-start | bytes 221192 | tf_op jit(solution)/shard_map/ppermute | solution.py:296
  11.5 15.0 %collective-permute-start.6 = (bf16[1,64,576]{2,1,0:T(8,128)(2,1)S(1)}, bf16[1,64,576]{2,1,0:T(8,128)(2,1)S(1)}, u32[]{:S(2)}, u32[]{:S(2)}) collective-permute-start(bf16[1,64,576]{2,1,0:T(8,128)(2,1)S(1)} %build_new.1.refs_3_), channel_id=1, source_target_pairs={{0,4},{4,8},{8,12},{12,0},{1,5},{5,9},{9,13},{13,1},{2,6},{6,10},{... | collective-permute-start | bytes 221192 | tf_op jit(solution)/shard_map/ppermute | solution.py:296

commit v4 on v3

--- a/solution.py
+++ b/solution.py
@@ -16,6 +16,9 @@
 QK = 192
 PG = 64
 MOST = 2
+EARLY = 1
+ORDER = (0, 1, 2)
+ORDER_INV = (0, 1, 2)
 DIRECT = 8
 EXPONENT = QK**-0.5 * math.log2(math.e)
 VMEM_LIMIT = 48 * 2**20
@@ -30,8 +33,21 @@
     return lax.axis_size("tp") * lax.axis_size("sp")
 
 
+def target_of(shift, sources):
+    return lax.rem(lax.axis_index("pool") + shift, sources)
+
+
 def shift_of(source, sources):
     return lax.rem(lax.axis_index("pool") - source + sources, sources)
+
+
+def own_begin(rows):
+    rows_lane = PG // lane_count()
+    return pl.multiple_of(lax.rem(lane_index() * rows_lane, rows), rows_lane)
+
+
+def requests_of(queue, dest, target, sources):
+    return [queue[jnp.maximum(g, 0)] for g in slot_groups(dest, target, sources)]
 
 
 def slot_groups(dest, target, sources):
@@ -45,9 +61,16 @@
     return found
 
 
+def split(index, size):
+    if size & (size - 1):
+        return index // size, index % size
+    return index >> (size.bit_length() - 1), index & (size - 1)
+
+
 def lane_positions(slots):
     rows_lane = PG // lane_count()
-    return slots // rows_lane * PG + lane_index() * rows_lane + slots % rows_lane
+    page, row = split(slots, rows_lane)
+    return page * PG + lane_index() * rows_lane + row
 
 
 def slots_before(length, pages):
@@ -59,12 +82,12 @@
 
 
 def new_index(columns, rows):
-    return (lane_index() ^ (columns // rows)) * rows + columns % rows
+    piece, row = split(columns, rows)
+    return (lane_index() ^ piece) * rows + row
 
 
 def pick_prefix(queue, dest, cache, *refs):
     outs, (lists, held, signals) = refs[:-3], refs[-3:]
-    me = lax.axis_index("pool")
     count, rows = cache.shape[:2]
     copies = [
         pltpu.make_async_copy(source, target, signals.at[i])
@@ -81,84 +104,84 @@
             outs[0][s] = held[lists[0, s]]
         return
     rows_lane = PG // lane_count()
-    begin = pl.multiple_of(lax.rem(lane_index() * rows_lane, rows), rows_lane)
     for s, out in enumerate(outs, 1):
-        target = lax.rem(me + s, count)
+        target = target_of(s, count)
         out[0, :rows] = held[lists[0, target]]
-        groups = slot_groups(lists.at[1], target, count)
-        for slot, group in enumerate(groups):
-            request = lists[0, jnp.maximum(group, 0)]
+        requests = requests_of(lists.at[0], lists.at[1], target, count)
+        for slot in range(EARLY):
             at = rows + slot * rows_lane
-            out[0, at : at + rows_lane] = held[request, pl.ds(begin, rows_lane)]
-
-
-def build_new(queue, pre_len, blk_len, *refs, pages):
-    new, out = refs[:-1], refs[-1]
+            out[0, at : at + rows_lane] = held[requests[slot], pl.ds(own_begin(rows), rows_lane)]
+
+
+def build_new(queue, pre_len, blk_len, dest, cache, *refs, sources):
+    new, outs = refs[:-sources], refs[-sources:]
+    count = cache.shape[1]
+    pages = sources * count // PG
+    rows_lane = PG // lane_count()
     me = lax.axis_index("pool")
     pre_length = pre_len[queue[me]]
     rows = new[0].shape[1]
-    shape = (out.shape[1], rows * len(new))
-    slot = lax.broadcasted_iota(jnp.int32, shape, 0) + slots_before(pre_length, pages)
+    slot = lax.broadcasted_iota(jnp.int32, (rows, 1), 0) + slots_before(pre_length, pages)
     offset = lane_positions(slot) - pre_length
-    index = new_index(lax.broadcasted_iota(jnp.int32, shape, 1), rows)
-    picker = jnp.where((index == offset) & (offset < blk_len[me]), 1.0, 0.0)
+    offset = jnp.where(offset < blk_len[me], offset, -1)
+    index = new_index(lax.broadcasted_iota(jnp.int32, (1, rows * len(new)), 1), rows)
+    picker = jnp.where(index == offset, 1.0, 0.0)
     held = jnp.concatenate([piece[0] for piece in new], axis=0)
-    out[0] = jnp.dot(
-        picker.astype(held.dtype), held, preferred_element_type=jnp.float32
-    ).astype(out.dtype)
+    made = jnp.dot(picker.astype(held.dtype), held, preferred_element_type=jnp.float32)
+    for s, out in enumerate(outs):
+        out[0, :rows] = made.astype(out.dtype)
+        if s == 0:
+            continue
+        requests = requests_of(queue, dest, target_of(s, sources), sources)
+        for slot in range(EARLY, MOST):
+            at = rows + (slot - EARLY) * rows_lane
+            out[0, at : at + rows_lane] = cache[requests[slot], pl.ds(own_begin(count), rows_lane)]
 
 
 def land_slots(queue, pre_len, dest, cache, *refs, sources):
     pre, landed = refs[: sources - 1], refs[sources - 1 : 2 * sources - 1]
-    out, held, built, signals = refs[2 * sources - 1 :]
+    out, built, signals = refs[2 * sources - 1 :]
     me = lax.axis_index("pool")
-    rows = cache.shape[1]
+    requests, rows = cache.shape[:2]
     rows_lane = PG // lane_count()
     pages = sources * rows // PG
+    slots = built.shape[1]
     new_rows = landed[0].shape[1]
-    first = lane_index() * rows_lane
-    begin = pl.multiple_of(lax.rem(first, rows), rows_lane)
-    copies = []
+    sent = landed[1].shape[1]
+    early = EARLY * rows_lane
+    blocks = [landed[0][0]] + [piece[0] for piece in landed[1:]]
+    blocks += [cache[r] for r in range(requests)]
+    if EARLY:
+        blocks += [piece[0, rows:] for piece in pre]
+    held = jnp.concatenate(blocks, axis=0)
+    own_at = new_rows + (sources - 1) * sent
+    early_at = own_at + requests * rows
+    slot_row = lax.broadcasted_iota(jnp.int32, (slots, 1), 0)
+    wanted = []
     for slot, group in enumerate(slot_groups(dest, me, sources)):
         request = queue[jnp.maximum(group, 0)]
         pre_length = jnp.where(group < 0, 0, pre_len[request])
-        for g in range(sources):
-            for s, piece in enumerate(landed):
-
-                @pl.when((group == g) & (shift_of(g, sources) == s))
-                def _(piece=piece, slot=slot):
-                    held[slot, :new_rows] = piece[0]
-
-        @pl.when(group < 0)
-        def _(slot=slot):
-            held[slot, :new_rows] = jnp.zeros((new_rows, KEY_W), held.dtype)
-
+        shift = shift_of(jnp.maximum(group, 0), sources)
+        new_at = jnp.where(shift == 0, 0, new_rows + (shift - 1) * sent)
+        behind = slot_row - slots_before(pre_length, pages)
+        chosen = jnp.where((behind >= 0) & (behind < new_rows), behind + new_at, -1)
         for m in range(pages):
-            shift = shift_of((m * PG + first) // rows, sources)
-            at = new_rows + m * rows_lane
-
-            @pl.when(shift == 0)
-            def _(at=at, slot=slot, request=request):
-                held[slot, at : at + rows_lane] = cache[request, pl.ds(begin, rows_lane)]
-
-            for s, piece in enumerate(pre, 1):
-
-                @pl.when(shift == s)
-                def _(at=at, slot=slot, piece=piece):
-                    start = rows + slot * rows_lane
-                    held[slot, at : at + rows_lane] = piece[0, start : start + rows_lane]
-
-        shape = (built.shape[1], held.shape[1])
-        row = lax.broadcasted_iota(jnp.int32, shape, 0)
-        column = lax.broadcasted_iota(jnp.int32, shape, 1)
-        behind = row - slots_before(pre_length, pages)
-        chosen = jnp.where(
-            behind < 0, row + new_rows, jnp.where(behind < new_rows, behind, -1)
-        )
+            place = m * PG + lane_index() * rows_lane
+            shift = shift_of(place // rows, sources)
+            if slot < EARLY:
+                there = early_at + (shift - 1) * early + slot * rows_lane
+            else:
+                there = 2 * new_rows + (shift - 1) * sent + (slot - EARLY) * rows_lane
+            there = jnp.where(shift == 0, own_at + request * rows + place % rows, there)
+            inside = (slot_row >= m * rows_lane) & (slot_row < (m + 1) * rows_lane)
+            chosen = jnp.where(inside & (behind < 0), slot_row - m * rows_lane + there, chosen)
+        wanted.append(jnp.where(group < 0, -1, chosen))
+    column = lax.broadcasted_iota(jnp.int32, (slots, held.shape[0]), 1)
+    copies = []
+    for slot, chosen in enumerate(wanted):
         picker = jnp.where(column == chosen, 1.0, 0.0).astype(held.dtype)
-        built[slot] = jnp.dot(
-            picker, held[slot], preferred_element_type=jnp.float32
-        ).astype(built.dtype)
+        made = jnp.dot(picker, held, preferred_element_type=jnp.float32)
+        built[slot] = made.astype(built.dtype)
         copies.append(pltpu.make_async_copy(built.at[slot], out.at[0, slot], signals.at[slot]))
         copies[-1].start()
     for copy in copies:
@@ -220,10 +243,11 @@
     rows = cache.shape[1]
     new_rows = new[0].shape[1]
     first = sources * rows
-    column = lax.broadcasted_iota(jnp.int32, bias.shape, 1)
+    column = lax.broadcasted_iota(jnp.int32, (1, bias.shape[1]), 1)
     if pre_count == sources - 1:
-        prefix = [cache[request]] + [piece[0, :rows] for piece in pre]
-        position = lax.rem(me - column // rows + sources, sources) * rows + column % rows
+        prefix = [cache[request]] + [pre[s][0, :rows] for s in ORDER_INV]
+        piece, place = split(column, rows)
+        position = lax.rem(me - jnp.minimum(piece, sources) + sources, sources) * rows + place
     else:
         prefix = [pre[0][s] for s in range(sources)]
         position = column
@@ -231,12 +255,15 @@
     blank = jnp.zeros((keys.shape[0], ROPE), keys.dtype)
     even_keys[...] = jnp.concatenate([keys, blank], axis=1)
     odd_keys[...] = jnp.concatenate([blank, keys], axis=1)
+    index = new_index(jnp.maximum(column - first, 0), new_rows)
+    never = first_query + count
+    since = jnp.where(
+        column < first,
+        jnp.where(position < pre_length, 0, never),
+        jnp.where(index < blk_length, index, never),
+    )
     row = lax.broadcasted_iota(jnp.int32, bias.shape, 0) + first_query
-    index = new_index(jnp.maximum(column - first, 0), new_rows)
-    visible = ((column < first) & (position < pre_length)) | (
-        (column >= first) & (index <= row) & (index < blk_length)
-    )
-    bias[...] = jnp.where(visible, 0.0, -jnp.inf)
+    bias[...] = jnp.where(row >= since, 0.0, -jnp.inf)
     values = even_keys[:, :LAT]
     row = lax.broadcasted_iota(jnp.int32, (count, 1), 0) + first_query
     live = jnp.concatenate([row] * pairs, axis=0) < blk_length
@@ -296,7 +323,7 @@
         return lax.ppermute(piece, "pool", pairs)
 
     if direct:
-        pieces, piece = sources - 1, (1, rows_in + MOST * rows_lane, KEY_W)
+        pieces, piece = sources - 1, (1, rows_in + EARLY * rows_lane, KEY_W)
     else:
         pieces, piece = 1, (sources, rows_in, KEY_W)
     chosen = pl.pallas_call(
@@ -325,21 +352,24 @@
     lane_new = block_latent.shape[1]
     build = functools.partial(
         pl.pallas_call,
-        out_specs=vmem,
         compiler_params=params,
         cost_estimate=pl.CostEstimate(flops=4 * 10**9, bytes_accessed=10**7, transcendentals=0),
     )
     if direct:
-        lane_rows = build(
-            functools.partial(build_new, pages=pre_total // PG),
-            in_specs=[smem] * 3 + [vmem] * len(new),
-            out_shape=jax.ShapeDtypeStruct((1, lane_new, KEY_W), dtype),
+        sent = lane_new + (MOST - EARLY) * rows_lane
+        ready = build(
+            functools.partial(build_new, sources=sources),
+            in_specs=[smem] * 4 + [vmem] * (1 + len(new)),
+            out_specs=[vmem] * sources,
+            out_shape=[jax.ShapeDtypeStruct((1, lane_new, KEY_W), dtype)]
+            + [jax.ShapeDtypeStruct((1, sent, KEY_W), dtype)] * (sources - 1),
             name="build_new",
-        )(*scalars, *new)
-        landed = [lane_rows] + [shifted(lane_rows, s) for s in range(1, sources)]
+        )(*scalars, decode_dest, prefix_cache, *new)
+        landed = [ready[0]] + [shifted(ready[s], s) for s in range(1, sources)]
     else:
         lane_rows = build(
             build_rows,
+            out_specs=vmem,
             in_specs=[smem] * 3 + [vmem] * (1 + len(new)),
             out_shape=jax.ShapeDtypeStruct((1, lane_total, KEY_W), dtype),
             name="build_rows",
@@ -367,7 +397,7 @@
             transcendentals=count * heads * key_count,
         ),
         name="attend",
-    )(*scalars, queries, prefix_cache, *pre, *new)
+    )(*scalars, queries, prefix_cache, *([pre[s] for s in ORDER] if direct else pre), *new)
     land = functools.partial(
         pl.pallas_call,
         out_specs=hbm,
@@ -379,7 +409,6 @@
             functools.partial(land_slots, sources=sources),
             in_specs=[smem] * 3 + [vmem] * (1 + len(pre) + len(landed)),
             scratch_shapes=[
-                pltpu.VMEM((MOST, lane_new + pre_total // lanes, KEY_W), dtype),
                 pltpu.VMEM((MOST, lane_total, KEY_W), dtype),
                 pltpu.SemaphoreType.DMA((MOST,)),
             ],

time: 28.6 us -> 25.8 us (0.902)
  the two profiles are of different devices: /device:TPU:28 before, /device:TPU:0 now
where the time goes in v4:
time: 25.8 us; the launch traced here: 25.7 us
  starting transfers between devices  12.8 us (50%)
  Pallas kernels  12 us (47%)
  between operations  0.8 us (3%)
    ppermute x6, starting transfers between devices, shifted(): return lax.ppermute(piece, 'pool', pairs)  9.7 us
    pallas_call x1, Pallas kernels, body(): pl.pallas_call(functools.partial(attend, sources=sources, pre_count=len(p...  8.07 us
    ppermute x3, starting transfers between devices, body(): lax.ppermute(block_latent, ('tp', 'sp'), [(i, i ^ s) for i in range(lanes)])  3.12 us
    pallas_call x1, Pallas kernels, body(): pl.pallas_call(pick_prefix, in_specs=[hbm] * 3, out_specs=[vmem] * pieces...  1.61 us
    pallas_call x1, Pallas kernels, body(): land(functools.partial(land_slots, sources=sources), in_specs=[smem] * 3...  1.59 us
    pallas_call x1, Pallas kernels, body(): build(functools.partial(build_new, sources=sources), in_specs=[smem] * 4...  0.75 us
  transfers between devices with their start and end apart: 9, of which 0 were waited for; matrix products, arithmetic and copies ran while one was open for 0% of the time, Pallas kernels for 41%

profile of v4, /device:TPU:0, one launch (start us, length us, event | category | flops | bytes accessed | tf_op | source)
XLA Modules:
  0.0 25.7 jit_solution(7049368510821768104)
XLA Ops:
  0.6 0.0 copy-start.4
  0.6 0.0 copy-start.1
  0.7 0.0 copy-start
  0.7 0.0 copy-start.3
  0.7 0.0 copy-start.2
  0.7 0.0 copy-start.5
  0.7 2.4 %collective-permute-start.5 = (bf16[1,64,576]{2,1,0:T(8,128)(2,1)}, bf16[1,64,576]{2,1,0:T(8,128)(2,1)S(1)}, u32[]{:S(2)}, u32[]{:S(2)}) collective-permute-start(bf16[1,64,576]{2,1,0:T(8,128)(2,1)} %refs_0_.1), channel_id=1, source_target_pairs={{0,3},{1,2},{2,1},{3,0},{4,7},{5,6},{6,5},{7,4},{8,11},{9,10},{10,... | collective-permute-start | bytes 221192 | tf_op jit(solution)/shard_map/ppermute | solution.py:348
  3.1 0.6 %collective-permute-start.4 = (bf16[1,64,576]{2,1,0:T(8,128)(2,1)}, bf16[1,64,576]{2,1,0:T(8,128)(2,1)S(1)}, u32[]{:S(2)}, u32[]{:S(2)}) collective-permute-start(bf16[1,64,576]{2,1,0:T(8,128)(2,1)} %refs_0_.1), channel_id=1, source_target_pairs={{0,2},{1,3},{2,0},{3,1},{4,6},{5,7},{6,4},{7,5},{8,10},{9,11},{10,... | collective-permute-start | bytes 221192 | tf_op jit(solution)/shard_map/ppermute | solution.py:348
  3.8 0.0 collective-permute-start.3
  3.8 1.6 %pick_prefix.1 = (bf16[1,48,576]{2,1,0:T(8,128)(2,1)}, bf16[1,48,576]{2,1,0:T(8,128)(2,1)}, bf16[1,48,576]{2,1,0:T(8,128)(2,1)}) custom-call(s32[4]{0:T(128)} %queue.7, s32[4]{0:T(128)} %dest.5, bf16[4,32,576]{2,1,0:T(8,128)(2,1)} %cache.7), custom_call_target="tpu_custom_call" | custom-call | flops 4000000000 | bytes 10000000 | tf_op jit(solution)/shard_map/pick_prefix/pallas_call | solution.py:329
  5.4 1.9 %collective-permute-start = (bf16[1,48,576]{2,1,0:T(8,128)(2,1)}, bf16[1,48,576]{2,1,0:T(8,128)(2,1)S(1)}, u32[]{:S(2)}, u32[]{:S(2)}) collective-permute-start(bf16[1,48,576]{2,1,0:T(8,128)(2,1)} %get-tuple-element.9), channel_id=1, source_target_pairs={{0,4},{4,8},{8,12},{12,0},{1,5},{5,9},{9,13},{13,1},{2,6},{6,10},{... | collective-permute-start | bytes 165896 | tf_op jit(solution)/shard_map/ppermute | solution.py:323
  7.3 2.6 %collective-permute-start.1 = (bf16[1,48,576]{2,1,0:T(8,128)(2,1)}, bf16[1,48,576]{2,1,0:T(8,128)(2,1)S(1)}, u32[]{:S(2)}, u32[]{:S(2)}) collective-permute-start(bf16[1,48,576]{2,1,0:T(8,128)(2,1)} %get-tuple-element.10), channel_id=1, source_target_pairs={{0,8},{4,12},{8,0},{12,4},{1,9},{5,13},{9,1},{13,5},{2,10},{6,14},... | collective-permute-start | bytes 165896 | tf_op jit(solution)/shard_map/ppermute | solution.py:323
  9.9 0.0 collective-permute-done.5.refs_6_.refs_3_
  9.9 0.0 slice-start
  9.9 0.0 slice-start.1
  9.9 1.3 %collective-permute-start.2 = (bf16[1,48,576]{2,1,0:T(8,128)(2,1)}, bf16[1,48,576]{2,1,0:T(8,128)(2,1)S(1)}, u32[]{:S(2)}, u32[]{:S(2)}) collective-permute-start(bf16[1,48,576]{2,1,0:T(8,128)(2,1)} %get-tuple-element.11), channel_id=1, source_target_pairs={{0,12},{4,0},{8,4},{12,8},{1,13},{5,1},{9,5},{13,9},{2,14},{6,2},{... | collective-permute-start | bytes 165896 | tf_op jit(solution)/shard_map/ppermute | solution.py:323
  11.3 0.0 collective-permute-done.4.refs_5_.refs_2_
  11.3 0.0 collective-permute-done.3.refs_4_.refs_1_
  11.3 0.0 copy-done.4
  11.3 0.0 copy-done.1
  11.3 0.0 copy-done
  11.3 0.0 copy-done.3
  11.3 0.0 copy-done.2
  11.3 0.0 copy-done.5
  11.3 0.7 %build_new.1 = (bf16[1,64,576]{2,1,0:T(8,128)(2,1)S(1)}, bf16[1,80,576]{2,1,0:T(8,128)(2,1)S(1)}, bf16[1,80,576]{2,1,0:T(8,128)(2,1)S(1)}, bf16[1,80,576]{2,1,0:T(8,128)(2,1)S(1)}) custom-call(s32[4]{0:T(128)S(1)} %copy-done.1, s32[4]{0:T(128)S(1)} %copy-done.2, s32[4]{0:T(128)S(1)} %copy-done.5, s32[4]{0:T(128)S(1)} %copy-done.3, ...), custom_call_target="tpu_custom_call" | custom-call | flops 4000000000 | bytes 10000000 | tf_op jit(solution)/shard_map/build_new/pallas_call | solution.py:360
  12.1 0.7 %collective-permute-start.6 = (bf16[1,80,576]{2,1,0:T(8,128)(2,1)S(1)}, bf16[1,80,576]{2,1,0:T(8,128)(2,1)S(1)}, u32[]{:S(2)}, u32[]{:S(2)}) collective-permute-start(bf16[1,80,576]{2,1,0:T(8,128)(2,1)S(1)} %get-tuple-element.13), channel_id=1, source_target_pairs={{0,4},{4,8},{8,12},{12,0},{1,5},{5,9},{9,13},{13,1},{2,6},{6,10},{... | collective-permute-start | bytes 276488 | tf_op jit(solution)/shard_map/ppermute | solution.py:323
  12.8 1.1 %collective-permute-start.7 = (bf16[1,80,576]{2,1,0:T(8,128)(2,1)S(1)}, bf16[1,80,576]{2,1,0:T(8,128)(2,1)S(1)}, u32[]{:S(2)}, u32[]{:S(2)}) collective-permute-start(bf16[1,80,576]{2,1,0:T(8,128)(2,1)S(1)} %get-tuple-element.14), channel_id=1, source_target_pairs={{0,8},{4,12},{8,0},{12,4},{1,9},{5,13},{9,1},{13,5},{2,10},{6,14},... | collective-permute-start | bytes 276488 | tf_op jit(solution)/shard_map/ppermute | solution.py:323
  13.9 0.0 collective-permute-done.refs_0_
  13.9 2.0 %collective-permute-start.8 = (bf16[1,80,576]{2,1,0:T(8,128)(2,1)S(1)}, bf16[1,80,576]{2,1,0:T(8,128)(2,1)S(1)}, u32[]{:S(2)}, u32[]{:S(2)}) collective-permute-start(bf16[1,80,576]{2,1,0:T(8,128)(2,1)S(1)} %get-tuple-element.15), channel_id=1, source_target_pairs={{0,12},{4,0},{8,4},{12,8},{1,13},{5,1},{9,5},{13,9},{2,14},{6,2},{... | collective-permute-start | bytes 276488 | tf_op jit(solution)/shard_map/ppermute | solution.py:323
  16.0 0.0 collective-permute-done.1.refs_1_
  16.0 0.0 collective-permute-done.2.refs_2_
  16.0 0.0 slice-done
  16.0 0.0 slice-done.1
  16.0 8.1 %attend.1 = bf16[1,128,16384]{2,1,0:T(8,128)(2,1)} custom-call(s32[4]{0:T(128)S(1)} %copy-done.1, s32[4]{0:T(128)S(1)} %copy-done.2, s32[4]{0:T(128)S(1)} %copy-done.5, bf16[1,128,18432]{2,1,0:T(8,128)(2,1)S(1)} %bitcast.2, bf16[4,32,576]{2,1,0:T(8,128)(2,1)S(1)} %copy-done, bf16[1,48,576]{2,1,0:T(8,128)(2,1)S(1)} %collective-permute-done.refs_0_, ...), custom_call_target="tpu_custom_call" | custom-call | flops 3422552064 | bytes 8912896 | tf_op jit(solution)/shard_map/attend/pallas_call | solution.py:381
  24.1 0.0 collective-permute-done.6.refs_4_
  24.1 0.0 collective-permute-done.7.refs_5_
  24.1 0.0 collective-permute-done.8.refs_6_
  24.1 1.6 %land_slots.1 = bf16[1,2,96,576]{3,2,1,0:T(8,128)(2,1)} custom-call(s32[4]{0:T(128)S(1)} %copy-done.1, s32[4]{0:T(128)S(1)} %copy-done.2, s32[4]{0:T(128)S(1)} %copy-done.3, bf16[4,32,576]{2,1,0:T(8,128)(2,1)S(1)} %copy-done, bf16[1,48,576]{2,1,0:T(8,128)(2,1)S(1)} %collective-permute-done.refs_0_, bf16[1,48,576]{2,1,0:T(8,128)(2,1)S(1)} %collective-permute-done.1.refs_1_, ...), custom_call_target="tpu_custom_call" | custom-call | tf_op jit(solution)/shard_map/land_slots/pallas_call | solution.py:408
  (1 shorter events, 0.0 us)
Async XLA Ops:
  0.6 10.6 %copy-start.4 = (bf16[1,64,576]{2,1,0:T(8,128)(2,1)S(1)}, bf16[1,64,576]{2,1,0:T(8,128)(2,1)}, u32[]{:S(2)}) copy-start(bf16[1,64,576]{2,1,0:T(8,128)(2,1)} %refs_0_.1) | copy-start | bytes 221188
  0.6 10.6 %copy-start.1 = (s32[4]{0:T(128)S(1)}, s32[4]{0:T(128)}, u32[]{:S(2)}) copy-start(s32[4]{0:T(128)} %queue.7) | copy-start | bytes 52
  0.7 10.6 %copy-start = (bf16[4,32,576]{2,1,0:T(8,128)(2,1)S(1)}, bf16[4,32,576]{2,1,0:T(8,128)(2,1)}, u32[]{:S(2)}) copy-start(bf16[4,32,576]{2,1,0:T(8,128)(2,1)} %cache.7) | copy-start | bytes 442372
  0.7 10.6 %copy-start.3 = (s32[4]{0:T(128)S(1)}, s32[4]{0:T(128)}, u32[]{:S(2)}) copy-start(s32[4]{0:T(128)} %dest.5) | copy-start | bytes 52
  0.7 10.6 %copy-start.2 = (s32[4]{0:T(128)S(1)}, s32[4]{0:T(128)}, u32[]{:S(2)}) copy-start(s32[4]{0:T(128)} %pre_len.5) | copy-start | bytes 52
  0.7 10.6 %copy-start.5 = (s32[4]{0:T(128)S(1)}, s32[4]{0:T(128)}, u32[]{:S(2)}) copy-start(s32[4]{0:T(128)} %blk_len.3) | copy-start | bytes 52
  0.7 9.2 %collective-permute-start.5 = (bf16[1,64,576]{2,1,0:T(8,128)(2,1)}, bf16[1,64,576]{2,1,0:T(8,128)(2,1)S(1)}, u32[]{:S(2)}, u32[]{:S(2)}) collective-permute-start(bf16[1,64,576]{2,1,0:T(8,128)(2,1)} %refs_0_.1), channel_id=1, source_target_pairs={{0,3},{1,2},{2,1},{3,0},{4,7},{5,6},{6,5},{7,4},{8,11},{9,10},{10,... | collective-permute-start | bytes 221192 | tf_op jit(solution)/shard_map/ppermute | solution.py:348
  3.1 8.1 %collective-permute-start.4 = (bf16[1,64,576]{2,1,0:T(8,128)(2,1)}, bf16[1,64,576]{2,1,0:T(8,128)(2,1)S(1)}, u32[]{:S(2)}, u32[]{:S(2)}) collective-permute-start(bf16[1,64,576]{2,1,0:T(8,128)(2,1)} %refs_0_.1), channel_id=1, source_target_pairs={{0,2},{1,3},{2,0},{3,1},{4,6},{5,7},{6,4},{7,5},{8,10},{9,11},{10,... | collective-permute-start | bytes 221192 | tf_op jit(solution)/shard_map/ppermute | solution.py:348
  3.8 7.5 %collective-permute-start.3 = (bf16[1,64,576]{2,1,0:T(8,128)(2,1)}, bf16[1,64,576]{2,1,0:T(8,128)(2,1)S(1)}, u32[]{:S(2)}, u32[]{:S(2)}) collective-permute-start(bf16[1,64,576]{2,1,0:T(8,128)(2,1)} %refs_0_.1), channel_id=1, source_target_pairs={{0,1},{1,0},{2,3},{3,2},{4,5},{5,4},{6,7},{7,6},{8,9},{9,8},{10,11... | collective-permute-start | bytes 221192 | tf_op jit(solution)/shard_map/ppermute | solution.py:348
  5.4 8.5 %collective-permute-start = (bf16[1,48,576]{2,1,0:T(8,128)(2,1)}, bf16[1,48,576]{2,1,0:T(8,128)(2,1)S(1)}, u32[]{:S(2)}, u32[]{:S(2)}) collective-permute-start(bf16[1,48,576]{2,1,0:T(8,128)(2,1)} %get-tuple-element.9), channel_id=1, source_target_pairs={{0,4},{4,8},{8,12},{12,0},{1,5},{5,9},{9,13},{13,1},{2,6},{6,10},{... | collective-permute-start | bytes 165896 | tf_op jit(solution)/shard_map/ppermute | solution.py:323
  7.3 8.7 %collective-permute-start.1 = (bf16[1,48,576]{2,1,0:T(8,128)(2,1)}, bf16[1,48,576]{2,1,0:T(8,128)(2,1)S(1)}, u32[]{:S(2)}, u32[]{:S(2)}) collective-permute-start(bf16[1,48,576]{2,1,0:T(8,128)(2,1)} %get-tuple-element.10), channel_id=1, source_target_pairs={{0,8},{4,12},{8,0},{12,4},{1,9},{5,13},{9,1},{13,5},{2,10},{6,14},... | collective-permute-start | bytes 165896 | tf_op jit(solution)/shard_map/ppermute | solution.py:323
  9.9 6.1 %slice-start = ((s8[4718592]{0:T(1024)(128)(4,1)}), s8[4194304]{0:T(1024)(128)(4,1)S(1)}, s32[]{:S(2)}) async-start(s8[4718592]{0:T(1024)(128)(4,1)} %bitcast.1), calls=%async_computation | async-start | bytes 8388608
  9.9 6.1 %slice-start.1 = ((s8[4718592]{0:T(1024)(128)(4,1)}), s8[524288]{0:T(1024)(128)(4,1)S(1)}, s32[]{:S(2)}) async-start(s8[4718592]{0:T(1024)(128)(4,1)} %bitcast.1), calls=%async_computation.1 | async-start | bytes 1048576
  9.9 6.1 %collective-permute-start.2 = (bf16[1,48,576]{2,1,0:T(8,128)(2,1)}, bf16[1,48,576]{2,1,0:T(8,128)(2,1)S(1)}, u32[]{:S(2)}, u32[]{:S(2)}) collective-permute-start(bf16[1,48,576]{2,1,0:T(8,128)(2,1)} %get-tuple-element.11), channel_id=1, source_target_pairs={{0,12},{4,0},{8,4},{12,8},{1,13},{5,1},{9,5},{13,9},{2,14},{6,2},{... | collective-permute-start | bytes 165896 | tf_op jit(solution)/shard_map/ppermute | solution.py:323
  12.1 12.0 %collective-permute-start.6 = (bf16[1,80,576]{2,1,0:T(8,128)(2,1)S(1)}, bf16[1,80,576]{2,1,0:T(8,128)(2,1)S(1)}, u32[]{:S(2)}, u32[]{:S(2)}) collective-permute-start(bf16[1,80,576]{2,1,0:T(8,128)(2,1)S(1)} %get-tuple-element.13), channel_id=1, source_target_pairs={{0,4},{4,8},{8,12},{12,0},{1,5},{5,9},{9,13},{13,1},{2,6},{6,10},{... | collective-permute-start | bytes 276488 | tf_op jit(solution)/shard_map/ppermute | solution.py:323
  12.8 11.3 %collective-permute-start.7 = (bf16[1,80,576]{2,1,0:T(8,128)(2,1)S(1)}, bf16[1,80,576]{2,1,0:T(8,128)(2,1)S(1)}, u32[]{:S(2)}, u32[]{:S(2)}) collective-permute-start(bf16[1,80,576]{2,1,0:T(8,128)(2,1)S(1)} %get-tuple-element.14), channel_id=1, source_target_pairs={{0,8},{4,12},{8,0},{12,4},{1,9},{5,13},{9,1},{13,5},{2,10},{6,14},... | collective-permute-start | bytes 276488 | tf_op jit(solution)/shard_map/ppermute | solution.py:323
  13.9 10.2 %collective-permute-start.8 = (bf16[1,80,576]{2,1,0:T(8,128)(2,1)S(1)}, bf16[1,80,576]{2,1,0:T(8,128)(2,1)S(1)}, u32[]{:S(2)}, u32[]{:S(2)}) collective-permute-start(bf16[1,80,576]{2,1,0:T(8,128)(2,1)S(1)} %get-tuple-element.15), channel_id=1, source_target_pairs={{0,12},{4,0},{8,4},{12,8},{1,13},{5,1},{9,5},{13,9},{2,14},{6,2},{... | collective-permute-start | bytes 276488 | tf_op jit(solution)/shard_map/ppermute | solution.py:323

commit v5 on v4

--- a/solution.py
+++ b/solution.py
@@ -21,6 +21,7 @@
 ORDER_INV = (0, 1, 2)
 DIRECT = 8
 EXPONENT = QK**-0.5 * math.log2(math.e)
+OVER_ALL = 1e30
 VMEM_LIMIT = 48 * 2**20
 VMEM_FIRST = 60 * 2**20
 
@@ -121,7 +122,8 @@
     me = lax.axis_index("pool")
     pre_length = pre_len[queue[me]]
     rows = new[0].shape[1]
-    slot = lax.broadcasted_iota(jnp.int32, (rows, 1), 0) + slots_before(pre_length, pages)
+    slot = lax.broadcasted_iota(jnp.int32, (rows, 1), 0)
+    slot = jnp.where(slot < slots_before(pre_length, pages), slot + rows, slot)
     offset = lane_positions(slot) - pre_length
     offset = jnp.where(offset < blk_len[me], offset, -1)
     index = new_index(lax.broadcasted_iota(jnp.int32, (1, rows * len(new)), 1), rows)
@@ -140,48 +142,57 @@
 
 def land_slots(queue, pre_len, dest, cache, *refs, sources):
     pre, landed = refs[: sources - 1], refs[sources - 1 : 2 * sources - 1]
-    out, built, signals = refs[2 * sources - 1 :]
+    out, front, built, signals = refs[2 * sources - 1 :]
     me = lax.axis_index("pool")
-    requests, rows = cache.shape[:2]
+    rows = cache.shape[1]
     rows_lane = PG // lane_count()
     pages = sources * rows // PG
-    slots = built.shape[1]
     new_rows = landed[0].shape[1]
-    sent = landed[1].shape[1]
-    early = EARLY * rows_lane
-    blocks = [landed[0][0]] + [piece[0] for piece in landed[1:]]
-    blocks += [cache[r] for r in range(requests)]
-    if EARLY:
-        blocks += [piece[0, rows:] for piece in pre]
-    held = jnp.concatenate(blocks, axis=0)
-    own_at = new_rows + (sources - 1) * sent
-    early_at = own_at + requests * rows
-    slot_row = lax.broadcasted_iota(jnp.int32, (slots, 1), 0)
-    wanted = []
-    for slot, group in enumerate(slot_groups(dest, me, sources)):
-        request = queue[jnp.maximum(group, 0)]
-        pre_length = jnp.where(group < 0, 0, pre_len[request])
-        shift = shift_of(jnp.maximum(group, 0), sources)
-        new_at = jnp.where(shift == 0, 0, new_rows + (shift - 1) * sent)
-        behind = slot_row - slots_before(pre_length, pages)
-        chosen = jnp.where((behind >= 0) & (behind < new_rows), behind + new_at, -1)
-        for m in range(pages):
-            place = m * PG + lane_index() * rows_lane
-            shift = shift_of(place // rows, sources)
-            if slot < EARLY:
-                there = early_at + (shift - 1) * early + slot * rows_lane
-            else:
-                there = 2 * new_rows + (shift - 1) * sent + (slot - EARLY) * rows_lane
-            there = jnp.where(shift == 0, own_at + request * rows + place % rows, there)
-            inside = (slot_row >= m * rows_lane) & (slot_row < (m + 1) * rows_lane)
-            chosen = jnp.where(inside & (behind < 0), slot_row - m * rows_lane + there, chosen)
-        wanted.append(jnp.where(group < 0, -1, chosen))
-    column = lax.broadcasted_iota(jnp.int32, (slots, held.shape[0]), 1)
+    ahead = pages * rows_lane
+    groups = slot_groups(dest, me, sources)
+    requests = [queue[jnp.maximum(group, 0)] for group in groups]
+    for m in range(pages):
+        shift = shift_of((m * PG + lane_index() * rows_lane) // rows, sources)
+        there = slice(m * rows_lane, (m + 1) * rows_lane)
+
+        @pl.when(shift == 0)
+        def _(there=there):
+            for slot in range(MOST):
+                front[slot, there] = cache[requests[slot], pl.ds(own_begin(rows), rows_lane)]
+
+        for s in range(1, sources):
+
+            @pl.when(shift == s)
+            def _(there=there, s=s):
+                for slot in range(MOST):
+                    if slot < EARLY:
+                        at = rows + slot * rows_lane
+                        front[slot, there] = pre[s - 1][0, at : at + rows_lane]
+                    else:
+                        at = new_rows + (slot - EARLY) * rows_lane
+                        front[slot, there] = landed[s][0, at : at + rows_lane]
+
+    row = lax.broadcasted_iota(jnp.int32, (ahead, KEY_W), 0)
     copies = []
-    for slot, chosen in enumerate(wanted):
-        picker = jnp.where(column == chosen, 1.0, 0.0).astype(held.dtype)
-        made = jnp.dot(picker, held, preferred_element_type=jnp.float32)
-        built[slot] = made.astype(built.dtype)
+    for slot, group in enumerate(groups):
+        before = slots_before(pre_len[requests[slot]], pages)
+        shift = jnp.where(group < 0, -1, shift_of(jnp.maximum(group, 0), sources))
+
+        @pl.when(shift < 0)
+        def _(slot=slot):
+            built[slot] = jnp.zeros(built.shape[1:], built.dtype)
+
+        for s in range(sources):
+
+            @pl.when(shift == s)
+            def _(slot=slot, s=s, before=before):
+                piece = landed[s]
+                low = piece[0, :ahead].astype(jnp.float32)
+                early = front[slot].astype(jnp.float32)
+                built[slot, :ahead] = jnp.where(row < before, early, low).astype(built.dtype)
+                built[slot, ahead:new_rows] = piece[0, ahead:new_rows]
+                built[slot, new_rows:] = jnp.where(row < before, low, 0.0).astype(built.dtype)
+
         copies.append(pltpu.make_async_copy(built.at[slot], out.at[0, slot], signals.at[slot]))
         copies[-1].start()
     for copy in copies:
@@ -244,59 +255,67 @@
     new_rows = new[0].shape[1]
     first = sources * rows
     column = lax.broadcasted_iota(jnp.int32, (1, bias.shape[1]), 1)
+
+    def put(at, block):
+        blank = jnp.zeros((block.shape[0], ROPE), block.dtype)
+        even_keys[pl.ds(at, block.shape[0])] = jnp.concatenate([block, blank], axis=1)
+        odd_keys[pl.ds(at, block.shape[0])] = jnp.concatenate([blank, block], axis=1)
+
     if pre_count == sources - 1:
-        prefix = [cache[request]] + [pre[s][0, :rows] for s in ORDER_INV]
+        put(0, jnp.concatenate([cache[request]] + [pre[s][0, :rows] for s in ORDER_INV], axis=0))
         piece, place = split(column, rows)
         position = lax.rem(me - jnp.minimum(piece, sources) + sources, sources) * rows + place
     else:
-        prefix = [pre[0][s] for s in range(sources)]
+        put(0, jnp.concatenate([pre[0][s] for s in range(sources)], axis=0))
         position = column
-    keys = jnp.concatenate(prefix + [piece[0] for piece in new], axis=0)
-    blank = jnp.zeros((keys.shape[0], ROPE), keys.dtype)
-    even_keys[...] = jnp.concatenate([keys, blank], axis=1)
-    odd_keys[...] = jnp.concatenate([blank, keys], axis=1)
-    index = new_index(jnp.maximum(column - first, 0), new_rows)
+    row = lax.broadcasted_iota(jnp.int32, (new_rows, 1), 0)
+    for s, piece in enumerate(new):
+        begin = pl.multiple_of((lane_index() ^ s) * new_rows, new_rows)
+        kept = (row + begin < blk_length).astype(jnp.float32)
+        put(first + begin, (piece[0].astype(jnp.float32) * kept).astype(piece.dtype))
+    index = column - first
     never = first_query + count
     since = jnp.where(
-        column < first,
+        index < 0,
         jnp.where(position < pre_length, 0, never),
         jnp.where(index < blk_length, index, never),
     )
     row = lax.broadcasted_iota(jnp.int32, bias.shape, 0) + first_query
-    bias[...] = jnp.where(row >= since, 0.0, -jnp.inf)
-    values = even_keys[:, :LAT]
-    row = lax.broadcasted_iota(jnp.int32, (count, 1), 0) + first_query
-    live = jnp.concatenate([row] * pairs, axis=0) < blk_length
-    masked = jnp.concatenate([bias[...]] * pairs, axis=0)
-
+    seen = jnp.where(row >= since, 0.0, -jnp.inf)
+    bias[...] = jnp.where((row >= blk_length) & (index == blk_length), OVER_ALL, seen)
     def leaving(head):
         columns = pl.ds(head * LAT, LAT)
         return pltpu.make_async_copy(held.at[:, columns], out.at[0, :, columns], signals.at[head])
 
-    units = [(p, odd) for p in range(0, heads // 2, pairs) for odd in (0, 1)]
-    for number, (pair, odd) in enumerate(units):
+    def work(pair, odd, seen):
+        values = even_keys[:seen, :LAT]
+        mask = bias[:, :seen]
         starts = [(pair + p) * PAIR_W + odd * LAT for p in range(pairs)]
-        some = jnp.concatenate([queries[0, :, at : at + WIDE] for at in starts], axis=0)
         scores = lax.dot_general(
-            some,
-            (odd_keys if odd else even_keys)[...],
+            jnp.concatenate([queries[0, :, at : at + WIDE] for at in starts], axis=0),
+            (odd_keys if odd else even_keys)[:seen],
             (((1,), (1,)), ((), ())),
             preferred_element_type=jnp.float32,
         )
-        scores = scores + masked
+        scores = scores + jnp.concatenate([mask] * pairs, axis=0)
         top = jnp.max(scores, axis=1, keepdims=True)
         weights = jnp.exp2((scores - top) * EXPONENT)
-        scale = jnp.where(live, 1.0 / jnp.sum(weights, axis=1, keepdims=True), 0.0)
-        weights = weights.astype(values.dtype)
-        step = pairs if number + 1 < len(units) else max(pairs // 4, 1)
-        for p in range(0, pairs, step):
-            part = slice(p * count, (p + step) * count)
-            mixture = jnp.dot(weights[part], values, preferred_element_type=jnp.float32)
-            mixture = (mixture * scale[part]).astype(held.dtype)
-            for i in range(step):
-                head = 2 * (pair + p + i) + odd
-                held[:, head * LAT : (head + 1) * LAT] = mixture[i * count : (i + 1) * count]
-                leaving(head).start()
+        scale = 1.0 / jnp.sum(weights, axis=1, keepdims=True)
+        mixture = jnp.dot(weights.astype(values.dtype), values, preferred_element_type=jnp.float32)
+        mixture = (mixture * scale).astype(held.dtype)
+        for p in range(pairs):
+            head = 2 * (pair + p) + odd
+            held[:, head * LAT : (head + 1) * LAT] = mixture[p * count : (p + 1) * count]
+            leaving(head).start()
+
+    for part in range(lax.axis_size("sp")):
+
+        @pl.when(lax.axis_index("sp") == part)
+        def _(part=part):
+            for pair in range(0, heads // 2, pairs):
+                for odd in (0, 1):
+                    work(pair, odd, first + (part + 1) * count)
+
     for head in range(heads):
         leaving(head).wait()
 
@@ -312,6 +331,7 @@
     rows_lane = PG // lanes
     lane_total = key_count // lanes
     direct = sources <= DIRECT and PG % rows_in == 0 and rows_in % rows_lane == 0
+    direct = direct and pre_total // lanes <= block_latent.shape[1]
     smem = pl.BlockSpec(memory_space=pltpu.SMEM)
     vmem = pl.BlockSpec(memory_space=pltpu.VMEM)
     hbm = pl.BlockSpec(memory_space=pltpu.HBM)
@@ -409,6 +429,7 @@
             functools.partial(land_slots, sources=sources),
             in_specs=[smem] * 3 + [vmem] * (1 + len(pre) + len(landed)),
             scratch_shapes=[
+                pltpu.VMEM((MOST, pre_total // lanes, KEY_W), dtype),
                 pltpu.VMEM((MOST, lane_total, KEY_W), dtype),
                 pltpu.SemaphoreType.DMA((MOST,)),
             ],

time: 25.8 us -> 24.9 us (0.965)
  Pallas kernels: 12 us -> 11 us
    pallas_call x1, Pallas kernels: 8.07 us -> 7.29 us  [body(): pl.pallas_call(functools.partial(attend, sources=sources, pre_count=len(p...]
  transfers between devices with their start and end apart: 9 -> 9, of which waited for: 0 -> 0; matrix products, arithmetic and copies ran while one was open for 0% -> 0% of each run, Pallas kernels for 41% -> 39%
where the time goes in v5:
time: 24.9 us; the launch traced here: 24.7 us
  starting transfers between devices  12.8 us (51%)
  Pallas kernels  11 us (44%)
  between operations  0.8 us (3%)
    ppermute x6, starting transfers between devices, shifted(): return lax.ppermute(piece, 'pool', pairs)  9.7 us
    pallas_call x1, Pallas kernels, body(): pl.pallas_call(functools.partial(attend, sources=sources, pre_count=len(p...  7.29 us
    ppermute x3, starting transfers between devices, body(): lax.ppermute(block_latent, ('tp', 'sp'), [(i, i ^ s) for i in range(lanes)])  3.12 us
    pallas_call x1, Pallas kernels, body(): pl.pallas_call(pick_prefix, in_specs=[hbm] * 3, out_specs=[vmem] * pieces...  1.61 us
    pallas_call x1, Pallas kernels, body(): land(functools.partial(land_slots, sources=sources), in_specs=[smem] * 3...  1.39 us
    pallas_call x1, Pallas kernels, body(): build(functools.partial(build_new, sources=sources), in_specs=[smem] * 4...  0.75 us
  transfers between devices with their start and end apart: 9, of which 0 were waited for; matrix products, arithmetic and copies ran while one was open for 0% of the time, Pallas kernels for 39%

profile of v5, /device:TPU:0, one launch (start us, length us, event | category | flops | bytes accessed | tf_op | source)
XLA Modules:
  0.0 24.7 jit_solution(14889683949280420286)
XLA Ops:
  0.6 0.0 copy-start.4
  0.6 0.0 copy-start.1
  0.7 0.0 copy-start
  0.7 0.0 copy-start.3
  0.7 0.0 copy-start.2
  0.7 0.0 copy-start.5
  0.7 2.4 %collective-permute-start.5 = (bf16[1,64,576]{2,1,0:T(8,128)(2,1)}, bf16[1,64,576]{2,1,0:T(8,128)(2,1)S(1)}, u32[]{:S(2)}, u32[]{:S(2)}) collective-permute-start(bf16[1,64,576]{2,1,0:T(8,128)(2,1)} %refs_0_.1), channel_id=1, source_target_pairs={{0,3},{1,2},{2,1},{3,0},{4,7},{5,6},{6,5},{7,4},{8,11},{9,10},{10,... | collective-permute-start | bytes 221192 | tf_op jit(solution)/shard_map/ppermute | solution.py:368
  3.1 0.6 %collective-permute-start.4 = (bf16[1,64,576]{2,1,0:T(8,128)(2,1)}, bf16[1,64,576]{2,1,0:T(8,128)(2,1)S(1)}, u32[]{:S(2)}, u32[]{:S(2)}) collective-permute-start(bf16[1,64,576]{2,1,0:T(8,128)(2,1)} %refs_0_.1), channel_id=1, source_target_pairs={{0,2},{1,3},{2,0},{3,1},{4,6},{5,7},{6,4},{7,5},{8,10},{9,11},{10,... | collective-permute-start | bytes 221192 | tf_op jit(solution)/shard_map/ppermute | solution.py:368
  3.8 0.0 collective-permute-start.3
  3.8 1.6 %pick_prefix.1 = (bf16[1,48,576]{2,1,0:T(8,128)(2,1)}, bf16[1,48,576]{2,1,0:T(8,128)(2,1)}, bf16[1,48,576]{2,1,0:T(8,128)(2,1)}) custom-call(s32[4]{0:T(128)} %queue.7, s32[4]{0:T(128)} %dest.5, bf16[4,32,576]{2,1,0:T(8,128)(2,1)} %cache.7), custom_call_target="tpu_custom_call" | custom-call | flops 4000000000 | bytes 10000000 | tf_op jit(solution)/shard_map/pick_prefix/pallas_call | solution.py:349
  5.4 1.9 %collective-permute-start = (bf16[1,48,576]{2,1,0:T(8,128)(2,1)}, bf16[1,48,576]{2,1,0:T(8,128)(2,1)S(1)}, u32[]{:S(2)}, u32[]{:S(2)}) collective-permute-start(bf16[1,48,576]{2,1,0:T(8,128)(2,1)} %get-tuple-element.9), channel_id=1, source_target_pairs={{0,4},{4,8},{8,12},{12,0},{1,5},{5,9},{9,13},{13,1},{2,6},{6,10},{... | collective-permute-start | bytes 165896 | tf_op jit(solution)/shard_map/ppermute | solution.py:343
  7.3 2.6 %collective-permute-start.1 = (bf16[1,48,576]{2,1,0:T(8,128)(2,1)}, bf16[1,48,576]{2,1,0:T(8,128)(2,1)S(1)}, u32[]{:S(2)}, u32[]{:S(2)}) collective-permute-start(bf16[1,48,576]{2,1,0:T(8,128)(2,1)} %get-tuple-element.10), channel_id=1, source_target_pairs={{0,8},{4,12},{8,0},{12,4},{1,9},{5,13},{9,1},{13,5},{2,10},{6,14},... | collective-permute-start | bytes 165896 | tf_op jit(solution)/shard_map/ppermute | solution.py:343
  9.9 0.0 collective-permute-done.5.refs_6_.refs_3_
  9.9 0.0 slice-start
  9.9 0.0 slice-start.1
  9.9 1.3 %collective-permute-start.2 = (bf16[1,48,576]{2,1,0:T(8,128)(2,1)}, bf16[1,48,576]{2,1,0:T(8,128)(2,1)S(1)}, u32[]{:S(2)}, u32[]{:S(2)}) collective-permute-start(bf16[1,48,576]{2,1,0:T(8,128)(2,1)} %get-tuple-element.11), channel_id=1, source_target_pairs={{0,12},{4,0},{8,4},{12,8},{1,13},{5,1},{9,5},{13,9},{2,14},{6,2},{... | collective-permute-start | bytes 165896 | tf_op jit(solution)/shard_map/ppermute | solution.py:343
  11.3 0.0 collective-permute-done.4.refs_5_.refs_2_
  11.3 0.0 collective-permute-done.3.refs_4_.refs_1_
  11.3 0.0 copy-done.4
  11.3 0.0 copy-done.1
  11.3 0.0 copy-done
  11.3 0.0 copy-done.3
  11.3 0.0 copy-done.2
  11.3 0.0 copy-done.5
  11.3 0.7 %build_new.1 = (bf16[1,64,576]{2,1,0:T(8,128)(2,1)S(1)}, bf16[1,80,576]{2,1,0:T(8,128)(2,1)S(1)}, bf16[1,80,576]{2,1,0:T(8,128)(2,1)S(1)}, bf16[1,80,576]{2,1,0:T(8,128)(2,1)S(1)}) custom-call(s32[4]{0:T(128)S(1)} %copy-done.1, s32[4]{0:T(128)S(1)} %copy-done.2, s32[4]{0:T(128)S(1)} %copy-done.5, s32[4]{0:T(128)S(1)} %copy-done.3, ...), custom_call_target="tpu_custom_call" | custom-call | flops 4000000000 | bytes 10000000 | tf_op jit(solution)/shard_map/build_new/pallas_call | solution.py:380
  12.1 0.7 %collective-permute-start.6 = (bf16[1,80,576]{2,1,0:T(8,128)(2,1)S(1)}, bf16[1,80,576]{2,1,0:T(8,128)(2,1)S(1)}, u32[]{:S(2)}, u32[]{:S(2)}) collective-permute-start(bf16[1,80,576]{2,1,0:T(8,128)(2,1)S(1)} %get-tuple-element.13), channel_id=1, source_target_pairs={{0,4},{4,8},{8,12},{12,0},{1,5},{5,9},{9,13},{13,1},{2,6},{6,10},{... | collective-permute-start | bytes 276488 | tf_op jit(solution)/shard_map/ppermute | solution.py:343
  12.8 1.1 %collective-permute-start.7 = (bf16[1,80,576]{2,1,0:T(8,128)(2,1)S(1)}, bf16[1,80,576]{2,1,0:T(8,128)(2,1)S(1)}, u32[]{:S(2)}, u32[]{:S(2)}) collective-permute-start(bf16[1,80,576]{2,1,0:T(8,128)(2,1)S(1)} %get-tuple-element.14), channel_id=1, source_target_pairs={{0,8},{4,12},{8,0},{12,4},{1,9},{5,13},{9,1},{13,5},{2,10},{6,14},... | collective-permute-start | bytes 276488 | tf_op jit(solution)/shard_map/ppermute | solution.py:343
  13.9 0.0 collective-permute-done.refs_0_
  13.9 2.0 %collective-permute-start.8 = (bf16[1,80,576]{2,1,0:T(8,128)(2,1)S(1)}, bf16[1,80,576]{2,1,0:T(8,128)(2,1)S(1)}, u32[]{:S(2)}, u32[]{:S(2)}) collective-permute-start(bf16[1,80,576]{2,1,0:T(8,128)(2,1)S(1)} %get-tuple-element.15), channel_id=1, source_target_pairs={{0,12},{4,0},{8,4},{12,8},{1,13},{5,1},{9,5},{13,9},{2,14},{6,2},{... | collective-permute-start | bytes 276488 | tf_op jit(solution)/shard_map/ppermute | solution.py:343
  16.0 0.0 collective-permute-done.1.refs_1_
  16.0 0.0 collective-permute-done.2.refs_2_
  16.0 0.0 slice-done
  16.0 0.0 slice-done.1
  16.0 7.3 %attend.1 = bf16[1,128,16384]{2,1,0:T(8,128)(2,1)} custom-call(s32[4]{0:T(128)S(1)} %copy-done.1, s32[4]{0:T(128)S(1)} %copy-done.2, s32[4]{0:T(128)S(1)} %copy-done.5, bf16[1,128,18432]{2,1,0:T(8,128)(2,1)S(1)} %bitcast.2, bf16[4,32,576]{2,1,0:T(8,128)(2,1)S(1)} %copy-done, bf16[1,48,576]{2,1,0:T(8,128)(2,1)S(1)} %collective-permute-done.refs_0_, ...), custom_call_target="tpu_custom_call" | custom-call | flops 3422552064 | bytes 8912896 | tf_op jit(solution)/shard_map/attend/pallas_call | solution.py:401
  23.3 0.0 collective-permute-done.6.refs_4_
  23.3 0.0 collective-permute-done.7.refs_5_
  23.3 0.0 collective-permute-done.8.refs_6_
  23.3 1.4 %land_slots.1 = bf16[1,2,96,576]{3,2,1,0:T(8,128)(2,1)} custom-call(s32[4]{0:T(128)S(1)} %copy-done.1, s32[4]{0:T(128)S(1)} %copy-done.2, s32[4]{0:T(128)S(1)} %copy-done.3, bf16[4,32,576]{2,1,0:T(8,128)(2,1)S(1)} %copy-done, bf16[1,48,576]{2,1,0:T(8,128)(2,1)S(1)} %collective-permute-done.refs_0_, bf16[1,48,576]{2,1,0:T(8,128)(2,1)S(1)} %collective-permute-done.1.refs_1_, ...), custom_call_target="tpu_custom_call" | custom-call | tf_op jit(solution)/shard_map/land_slots/pallas_call | solution.py:428
  (1 shorter events, 0.0 us)
Async XLA Ops:
  0.6 10.6 %copy-start.4 = (bf16[1,64,576]{2,1,0:T(8,128)(2,1)S(1)}, bf16[1,64,576]{2,1,0:T(8,128)(2,1)}, u32[]{:S(2)}) copy-start(bf16[1,64,576]{2,1,0:T(8,128)(2,1)} %refs_0_.1) | copy-start | bytes 221188
  0.6 10.6 %copy-start.1 = (s32[4]{0:T(128)S(1)}, s32[4]{0:T(128)}, u32[]{:S(2)}) copy-start(s32[4]{0:T(128)} %queue.7) | copy-start | bytes 52
  0.7 10.6 %copy-start = (bf16[4,32,576]{2,1,0:T(8,128)(2,1)S(1)}, bf16[4,32,576]{2,1,0:T(8,128)(2,1)}, u32[]{:S(2)}) copy-start(bf16[4,32,576]{2,1,0:T(8,128)(2,1)} %cache.7) | copy-start | bytes 442372
  0.7 10.6 %copy-start.3 = (s32[4]{0:T(128)S(1)}, s32[4]{0:T(128)}, u32[]{:S(2)}) copy-start(s32[4]{0:T(128)} %dest.5) | copy-start | bytes 52
  0.7 10.6 %copy-start.2 = (s32[4]{0:T(128)S(1)}, s32[4]{0:T(128)}, u32[]{:S(2)}) copy-start(s32[4]{0:T(128)} %pre_len.5) | copy-start | bytes 52
  0.7 10.6 %copy-start.5 = (s32[4]{0:T(128)S(1)}, s32[4]{0:T(128)}, u32[]{:S(2)}) copy-start(s32[4]{0:T(128)} %blk_len.3) | copy-start | bytes 52
  0.7 9.2 %collective-permute-start.5 = (bf16[1,64,576]{2,1,0:T(8,128)(2,1)}, bf16[1,64,576]{2,1,0:T(8,128)(2,1)S(1)}, u32[]{:S(2)}, u32[]{:S(2)}) collective-permute-start(bf16[1,64,576]{2,1,0:T(8,128)(2,1)} %refs_0_.1), channel_id=1, source_target_pairs={{0,3},{1,2},{2,1},{3,0},{4,7},{5,6},{6,5},{7,4},{8,11},{9,10},{10,... | collective-permute-start | bytes 221192 | tf_op jit(solution)/shard_map/ppermute | solution.py:368
  3.1 8.1 %collective-permute-start.4 = (bf16[1,64,576]{2,1,0:T(8,128)(2,1)}, bf16[1,64,576]{2,1,0:T(8,128)(2,1)S(1)}, u32[]{:S(2)}, u32[]{:S(2)}) collective-permute-start(bf16[1,64,576]{2,1,0:T(8,128)(2,1)} %refs_0_.1), channel_id=1, source_target_pairs={{0,2},{1,3},{2,0},{3,1},{4,6},{5,7},{6,4},{7,5},{8,10},{9,11},{10,... | collective-permute-start | bytes 221192 | tf_op jit(solution)/shard_map/ppermute | solution.py:368
  3.8 7.5 %collective-permute-start.3 = (bf16[1,64,576]{2,1,0:T(8,128)(2,1)}, bf16[1,64,576]{2,1,0:T(8,128)(2,1)S(1)}, u32[]{:S(2)}, u32[]{:S(2)}) collective-permute-start(bf16[1,64,576]{2,1,0:T(8,128)(2,1)} %refs_0_.1), channel_id=1, source_target_pairs={{0,1},{1,0},{2,3},{3,2},{4,5},{5,4},{6,7},{7,6},{8,9},{9,8},{10,11... | collective-permute-start | bytes 221192 | tf_op jit(solution)/shard_map/ppermute | solution.py:368
  5.4 8.5 %collective-permute-start = (bf16[1,48,576]{2,1,0:T(8,128)(2,1)}, bf16[1,48,576]{2,1,0:T(8,128)(2,1)S(1)}, u32[]{:S(2)}, u32[]{:S(2)}) collective-permute-start(bf16[1,48,576]{2,1,0:T(8,128)(2,1)} %get-tuple-element.9), channel_id=1, source_target_pairs={{0,4},{4,8},{8,12},{12,0},{1,5},{5,9},{9,13},{13,1},{2,6},{6,10},{... | collective-permute-start | bytes 165896 | tf_op jit(solution)/shard_map/ppermute | solution.py:343
  7.3 8.7 %collective-permute-start.1 = (bf16[1,48,576]{2,1,0:T(8,128)(2,1)}, bf16[1,48,576]{2,1,0:T(8,128)(2,1)S(1)}, u32[]{:S(2)}, u32[]{:S(2)}) collective-permute-start(bf16[1,48,576]{2,1,0:T(8,128)(2,1)} %get-tuple-element.10), channel_id=1, source_target_pairs={{0,8},{4,12},{8,0},{12,4},{1,9},{5,13},{9,1},{13,5},{2,10},{6,14},... | collective-permute-start | bytes 165896 | tf_op jit(solution)/shard_map/ppermute | solution.py:343
  9.9 6.1 %slice-start = ((s8[4718592]{0:T(1024)(128)(4,1)}), s8[4194304]{0:T(1024)(128)(4,1)S(1)}, s32[]{:S(2)}) async-start(s8[4718592]{0:T(1024)(128)(4,1)} %bitcast.1), calls=%async_computation | async-start | bytes 8388608
  9.9 6.1 %slice-start.1 = ((s8[4718592]{0:T(1024)(128)(4,1)}), s8[524288]{0:T(1024)(128)(4,1)S(1)}, s32[]{:S(2)}) async-start(s8[4718592]{0:T(1024)(128)(4,1)} %bitcast.1), calls=%async_computation.1 | async-start | bytes 1048576
  9.9 6.1 %collective-permute-start.2 = (bf16[1,48,576]{2,1,0:T(8,128)(2,1)}, bf16[1,48,576]{2,1,0:T(8,128)(2,1)S(1)}, u32[]{:S(2)}, u32[]{:S(2)}) collective-permute-start(bf16[1,48,576]{2,1,0:T(8,128)(2,1)} %get-tuple-element.11), channel_id=1, source_target_pairs={{0,12},{4,0},{8,4},{12,8},{1,13},{5,1},{9,5},{13,9},{2,14},{6,2},{... | collective-permute-start | bytes 165896 | tf_op jit(solution)/shard_map/ppermute | solution.py:343
  12.1 11.2 %collective-permute-start.6 = (bf16[1,80,576]{2,1,0:T(8,128)(2,1)S(1)}, bf16[1,80,576]{2,1,0:T(8,128)(2,1)S(1)}, u32[]{:S(2)}, u32[]{:S(2)}) collective-permute-start(bf16[1,80,576]{2,1,0:T(8,128)(2,1)S(1)} %get-tuple-element.13), channel_id=1, source_target_pairs={{0,4},{4,8},{8,12},{12,0},{1,5},{5,9},{9,13},{13,1},{2,6},{6,10},{... | collective-permute-start | bytes 276488 | tf_op jit(solution)/shard_map/ppermute | solution.py:343
  12.8 10.5 %collective-permute-start.7 = (bf16[1,80,576]{2,1,0:T(8,128)(2,1)S(1)}, bf16[1,80,576]{2,1,0:T(8,128)(2,1)S(1)}, u32[]{:S(2)}, u32[]{:S(2)}) collective-permute-start(bf16[1,80,576]{2,1,0:T(8,128)(2,1)S(1)} %get-tuple-element.14), channel_id=1, source_target_pairs={{0,8},{4,12},{8,0},{12,4},{1,9},{5,13},{9,1},{13,5},{2,10},{6,14},... | collective-permute-start | bytes 276488 | tf_op jit(solution)/shard_map/ppermute | solution.py:343
  13.9 9.4 %collective-permute-start.8 = (bf16[1,80,576]{2,1,0:T(8,128)(2,1)S(1)}, bf16[1,80,576]{2,1,0:T(8,128)(2,1)S(1)}, u32[]{:S(2)}, u32[]{:S(2)}) collective-permute-start(bf16[1,80,576]{2,1,0:T(8,128)(2,1)S(1)} %get-tuple-element.15), channel_id=1, source_target_pairs={{0,12},{4,0},{8,4},{12,8},{1,13},{5,1},{9,5},{13,9},{2,14},{6,2},{... | collective-permute-start | bytes 276488 | tf_op jit(solution)/shard_map/ppermute | solution.py:343

commit v6 on v5

--- a/solution.py
+++ b/solution.py
@@ -17,8 +17,6 @@
 PG = 64
 MOST = 2
 EARLY = 1
-ORDER = (0, 1, 2)
-ORDER_INV = (0, 1, 2)
 DIRECT = 8
 EXPONENT = QK**-0.5 * math.log2(math.e)
 OVER_ALL = 1e30
@@ -34,8 +32,8 @@
     return lax.axis_size("tp") * lax.axis_size("sp")
 
 
-def target_of(shift, sources):
-    return lax.rem(lax.axis_index("pool") + shift, sources)
+def target_of(s, sources):
+    return lax.rem(lax.axis_index("pool") + s, sources)
 
 
 def shift_of(source, sources):
@@ -47,15 +45,20 @@
     return pl.multiple_of(lax.rem(lane_index() * rows_lane, rows), rows_lane)
 
 
-def requests_of(queue, dest, target, sources):
-    return [queue[jnp.maximum(g, 0)] for g in slot_groups(dest, target, sources)]
-
-
-def slot_groups(dest, target, sources):
+def value(held, index):
+    column = lax.broadcasted_iota(jnp.int32, held.shape, 1)
+    return jnp.sum(jnp.where(column == index, held[...].astype(jnp.float32), 0.0)).astype(jnp.int32)
+
+
+def entries(held):
+    return [value(held, i) for i in range(held.shape[1])]
+
+
+def slot_groups(dests, target):
     found = [jnp.int32(-1)] * MOST
     rank = jnp.int32(0)
-    for g in range(sources):
-        hit = dest[g] == target
+    for g, dest in enumerate(dests):
+        hit = dest == target
         for slot in range(MOST):
             found[slot] = jnp.where(hit & (rank == slot), g, found[slot])
         rank = rank + hit.astype(jnp.int32)
@@ -108,7 +111,8 @@
     for s, out in enumerate(outs, 1):
         target = target_of(s, count)
         out[0, :rows] = held[lists[0, target]]
-        requests = requests_of(lists.at[0], lists.at[1], target, count)
+        groups = slot_groups([lists[1, g] for g in range(count)], target)
+        requests = [lists[0, jnp.maximum(g, 0)] for g in groups]
         for slot in range(EARLY):
             at = rows + slot * rows_lane
             out[0, at : at + rows_lane] = held[requests[slot], pl.ds(own_begin(rows), rows_lane)]
@@ -121,20 +125,23 @@
     rows_lane = PG // lane_count()
     me = lax.axis_index("pool")
     pre_length = pre_len[queue[me]]
+    blk_length = blk_len[me]
     rows = new[0].shape[1]
     slot = lax.broadcasted_iota(jnp.int32, (rows, 1), 0)
     slot = jnp.where(slot < slots_before(pre_length, pages), slot + rows, slot)
     offset = lane_positions(slot) - pre_length
-    offset = jnp.where(offset < blk_len[me], offset, -1)
+    offset = jnp.where(offset < blk_length, offset, -1)
     index = new_index(lax.broadcasted_iota(jnp.int32, (1, rows * len(new)), 1), rows)
     picker = jnp.where(index == offset, 1.0, 0.0)
     held = jnp.concatenate([piece[0] for piece in new], axis=0)
     made = jnp.dot(picker.astype(held.dtype), held, preferred_element_type=jnp.float32)
+    dests = [dest[g] for g in range(sources)]
     for s, out in enumerate(outs):
         out[0, :rows] = made.astype(out.dtype)
         if s == 0:
             continue
-        requests = requests_of(queue, dest, target_of(s, sources), sources)
+        groups = slot_groups(dests, target_of(s, sources))
+        requests = [queue[jnp.maximum(g, 0)] for g in groups]
         for slot in range(EARLY, MOST):
             at = rows + (slot - EARLY) * rows_lane
             out[0, at : at + rows_lane] = cache[requests[slot], pl.ds(own_begin(count), rows_lane)]
@@ -142,57 +149,41 @@
 
 def land_slots(queue, pre_len, dest, cache, *refs, sources):
     pre, landed = refs[: sources - 1], refs[sources - 1 : 2 * sources - 1]
-    out, front, built, signals = refs[2 * sources - 1 :]
+    out, stack, ends, built, signals = refs[2 * sources - 1 :]
     me = lax.axis_index("pool")
     rows = cache.shape[1]
     rows_lane = PG // lane_count()
     pages = sources * rows // PG
     new_rows = landed[0].shape[1]
     ahead = pages * rows_lane
-    groups = slot_groups(dest, me, sources)
-    requests = [queue[jnp.maximum(group, 0)] for group in groups]
-    for m in range(pages):
-        shift = shift_of((m * PG + lane_index() * rows_lane) // rows, sources)
-        there = slice(m * rows_lane, (m + 1) * rows_lane)
-
-        @pl.when(shift == 0)
-        def _(there=there):
-            for slot in range(MOST):
-                front[slot, there] = cache[requests[slot], pl.ds(own_begin(rows), rows_lane)]
-
-        for s in range(1, sources):
-
-            @pl.when(shift == s)
-            def _(there=there, s=s):
-                for slot in range(MOST):
-                    if slot < EARLY:
-                        at = rows + slot * rows_lane
-                        front[slot, there] = pre[s - 1][0, at : at + rows_lane]
-                    else:
-                        at = new_rows + (slot - EARLY) * rows_lane
-                        front[slot, there] = landed[s][0, at : at + rows_lane]
-
+    groups = slot_groups(entries(dest), me)
+    requests = [value(queue, jnp.maximum(group, 0)) for group in groups]
+    for s in range(sources):
+        stack[s] = landed[s][0, :new_rows]
+        if s == 0:
+            for slot, request in enumerate(requests):
+                ends[s, slot] = cache[request, pl.ds(own_begin(rows), rows_lane)]
+            continue
+        for slot in range(MOST):
+            piece, at = (pre[s - 1], rows) if slot < EARLY else (landed[s], new_rows)
+            at += (slot if slot < EARLY else slot - EARLY) * rows_lane
+            ends[s, slot] = piece[0, at : at + rows_lane]
+    stack[sources] = jnp.zeros((new_rows, KEY_W), stack.dtype)
     row = lax.broadcasted_iota(jnp.int32, (ahead, KEY_W), 0)
     copies = []
     for slot, group in enumerate(groups):
-        before = slots_before(pre_len[requests[slot]], pages)
-        shift = jnp.where(group < 0, -1, shift_of(jnp.maximum(group, 0), sources))
-
-        @pl.when(shift < 0)
-        def _(slot=slot):
-            built[slot] = jnp.zeros(built.shape[1:], built.dtype)
-
-        for s in range(sources):
-
-            @pl.when(shift == s)
-            def _(slot=slot, s=s, before=before):
-                piece = landed[s]
-                low = piece[0, :ahead].astype(jnp.float32)
-                early = front[slot].astype(jnp.float32)
-                built[slot, :ahead] = jnp.where(row < before, early, low).astype(built.dtype)
-                built[slot, ahead:new_rows] = piece[0, ahead:new_rows]
-                built[slot, new_rows:] = jnp.where(row < before, low, 0.0).astype(built.dtype)
-
+        before = slots_before(value(pre_len, requests[slot]), pages)
+        before = jnp.where(group < 0, 0, before)
+        shift = jnp.where(group < 0, sources, shift_of(jnp.maximum(group, 0), sources))
+        front = []
+        for m in range(pages):
+            source = (m * PG + lane_index() * rows_lane) // rows
+            front.append(ends[shift_of(source, sources), slot])
+        front = jnp.concatenate(front, axis=0).astype(jnp.float32)
+        low = stack[shift, :ahead].astype(jnp.float32)
+        built[slot, :ahead] = jnp.where(row < before, front, low).astype(built.dtype)
+        built[slot, ahead:new_rows] = stack[shift, ahead:]
+        built[slot, new_rows:] = jnp.where(row < before, low, 0.0).astype(built.dtype)
         copies.append(pltpu.make_async_copy(built.at[slot], out.at[0, slot], signals.at[slot]))
         copies[-1].start()
     for copy in copies:
@@ -202,7 +193,8 @@
 def build_rows(queue, pre_len, blk_len, pre, *refs):
     new, out = refs[:-1], refs[-1]
     me = lax.axis_index("pool")
-    pre_length = pre_len[queue[me]]
+    pre_length = value(pre_len, value(queue, me))
+    blk_length = value(blk_len, me)
     first = pre.shape[0] * pre.shape[1]
     rows = new[0].shape[1]
     held = jnp.concatenate(
@@ -214,7 +206,7 @@
     offset = position - pre_length
     index = new_index(jnp.maximum(column - first, 0), rows)
     picked = ((offset < 0) & (column == position)) | (
-        (offset >= 0) & (offset < blk_len[me]) & (column >= first) & (index == offset)
+        (offset >= 0) & (offset < blk_length) & (column >= first) & (index == offset)
     )
     picker = jnp.where(picked, 1.0, 0.0).astype(held.dtype)
     out[0] = jnp.dot(picker, held, preferred_element_type=jnp.float32).astype(out.dtype)
@@ -227,7 +219,7 @@
     def landing(slot, source):
         return pltpu.make_async_copy(source, out.at[0, slot], signals.at[slot])
 
-    for slot, group in enumerate(slot_groups(dest, me, landed.shape[0])):
+    for slot, group in enumerate(slot_groups(entries(dest), me)):
 
         @pl.when(group < 0)
         def _(slot=slot):
@@ -247,9 +239,9 @@
     me = lax.axis_index("pool")
     count = queries.shape[1]
     heads = queries.shape[2] // KEY_W
-    request = queue[me]
-    pre_length = pre_len[request]
-    blk_length = blk_len[me]
+    request = value(queue, me)
+    pre_length = value(pre_len, request)
+    blk_length = value(blk_len, me)
     first_query = lax.axis_index("sp") * count
     rows = cache.shape[1]
     new_rows = new[0].shape[1]
@@ -262,9 +254,9 @@
         odd_keys[pl.ds(at, block.shape[0])] = jnp.concatenate([blank, block], axis=1)
 
     if pre_count == sources - 1:
-        put(0, jnp.concatenate([cache[request]] + [pre[s][0, :rows] for s in ORDER_INV], axis=0))
+        put(0, jnp.concatenate([cache[request]] + [piece[0, :rows] for piece in pre], axis=0))
         piece, place = split(column, rows)
-        position = lax.rem(me - jnp.minimum(piece, sources) + sources, sources) * rows + place
+        position = shift_of(jnp.minimum(piece, sources - 1), sources) * rows + place
     else:
         put(0, jnp.concatenate([pre[0][s] for s in range(sources)], axis=0))
         position = column
@@ -338,7 +330,7 @@
     params = pltpu.CompilerParams(vmem_limit_bytes=VMEM_LIMIT)
     dtype = queries.dtype
 
-    def shifted(piece, s):
+    def moved(piece, s):
         pairs = [(i, (i + s) % sources) for i in range(sources)]
         return lax.ppermute(piece, "pool", pairs)
 
@@ -361,14 +353,17 @@
         name="pick_prefix",
     )(queue_list, decode_dest, prefix_cache)
     if direct:
-        pre = [shifted(chosen[s - 1], s) for s in range(1, sources)]
+        pre = [moved(chosen[s - 1], s) for s in range(1, sources)]
     else:
         pre = [lax.all_to_all(chosen[0], "pool", split_axis=0, concat_axis=0, tiled=True)]
     new = [block_latent] + [
         lax.ppermute(block_latent, ("tp", "sp"), [(i, i ^ s) for i in range(lanes)])
         for s in range(1, lanes)
     ]
-    scalars = (queue_list, prefix_len, block_len)
+    queue_row, prefix_row, block_row, dest_row = (
+        x.reshape(1, -1) for x in (queue_list, prefix_len, block_len, decode_dest)
+    )
+    scalars = (queue_row, prefix_row, block_row)
     lane_new = block_latent.shape[1]
     build = functools.partial(
         pl.pallas_call,
@@ -384,13 +379,13 @@
             out_shape=[jax.ShapeDtypeStruct((1, lane_new, KEY_W), dtype)]
             + [jax.ShapeDtypeStruct((1, sent, KEY_W), dtype)] * (sources - 1),
             name="build_new",
-        )(*scalars, decode_dest, prefix_cache, *new)
-        landed = [ready[0]] + [shifted(ready[s], s) for s in range(1, sources)]
+        )(queue_list, prefix_len, block_len, decode_dest, prefix_cache, *new)
+        landed = [ready[0]] + [moved(ready[s], s) for s in range(1, sources)]
     else:
         lane_rows = build(
             build_rows,
             out_specs=vmem,
-            in_specs=[smem] * 3 + [vmem] * (1 + len(new)),
+            in_specs=[vmem] * (4 + len(new)),
             out_shape=jax.ShapeDtypeStruct((1, lane_total, KEY_W), dtype),
             name="build_rows",
         )(*scalars, *pre, *new)
@@ -400,7 +395,7 @@
         pairs //= 2
     latent_out = pl.pallas_call(
         functools.partial(attend, sources=sources, pre_count=len(pre), pairs=pairs),
-        in_specs=[smem] * 3 + [vmem] * (2 + len(pre) + len(new)),
+        in_specs=[vmem] * (5 + len(pre) + len(new)),
         out_specs=hbm,
         out_shape=jax.ShapeDtypeStruct((1, count, heads * LAT), dtype),
         scratch_shapes=[
@@ -417,7 +412,7 @@
             transcendentals=count * heads * key_count,
         ),
         name="attend",
-    )(*scalars, queries, prefix_cache, *([pre[s] for s in ORDER] if direct else pre), *new)
+    )(*scalars, queries, prefix_cache, *pre, *new)
     land = functools.partial(
         pl.pallas_call,
         out_specs=hbm,
@@ -427,24 +422,25 @@
     if direct:
         decode_pages = land(
             functools.partial(land_slots, sources=sources),
-            in_specs=[smem] * 3 + [vmem] * (1 + len(pre) + len(landed)),
+            in_specs=[vmem] * (4 + len(pre) + len(landed)),
             scratch_shapes=[
-                pltpu.VMEM((MOST, pre_total // lanes, KEY_W), dtype),
+                pltpu.VMEM((sources + 1, lane_new, KEY_W), dtype),
+                pltpu.VMEM((sources, MOST, rows_lane, KEY_W), dtype),
                 pltpu.VMEM((MOST, lane_total, KEY_W), dtype),
                 pltpu.SemaphoreType.DMA((MOST,)),
             ],
             name="land_slots",
-        )(queue_list, prefix_len, decode_dest, prefix_cache, *pre, *landed)
+        )(queue_row, prefix_row, dest_row, prefix_cache, *pre, *landed)
     else:
         decode_pages = land(
             land_rows,
-            in_specs=[smem, vmem],
+            in_specs=[vmem, vmem],
             scratch_shapes=[
                 pltpu.VMEM((lane_total, KEY_W), dtype),
                 pltpu.SemaphoreType.DMA((MOST,)),
             ],
             name="land_rows",
-        )(decode_dest, *landed)
+        )(dest_row, *landed)
     return latent_out, decode_pages.reshape(1, MOST, key_count // PG, rows_lane, KEY_W)
 
 

time: 24.9 us -> 24.2 us (0.972)
  Pallas kernels: 11 us -> 10.4 us
    pallas_call x1, Pallas kernels: 7.29 us -> 6.96 us  [body(): pl.pallas_call(functools.partial(attend, sources=sources, pre_count=len(p...]
    pallas_call x1, Pallas kernels: 1.39 us -> 1.1 us  [body(): land(functools.partial(land_slots, sources=sources), in_specs=[vmem] * (4...]
where the time goes in v6:
time: 24.2 us; the launch traced here: 24.1 us
  starting transfers between devices  12.8 us (53%)
  Pallas kernels  10.4 us (43%)
  between operations  0.8 us (3%)
    ppermute x6, starting transfers between devices, moved(): return lax.ppermute(piece, 'pool', pairs)  9.7 us
    pallas_call x1, Pallas kernels, body(): pl.pallas_call(functools.partial(attend, sources=sources, pre_count=len(p...  6.96 us
    ppermute x3, starting transfers between devices, body(): lax.ppermute(block_latent, ('tp', 'sp'), [(i, i ^ s) for i in range(lanes)])  3.12 us
    pallas_call x1, Pallas kernels, body(): pl.pallas_call(pick_prefix, in_specs=[hbm] * 3, out_specs=[vmem] * pieces...  1.61 us
    pallas_call x1, Pallas kernels, body(): land(functools.partial(land_slots, sources=sources), in_specs=[vmem] * (4...  1.1 us
    pallas_call x1, Pallas kernels, body(): build(functools.partial(build_new, sources=sources), in_specs=[smem] * 4...  0.75 us
  transfers between devices with their start and end apart: 9, of which 0 were waited for; matrix products, arithmetic and copies ran while one was open for 0% of the time, Pallas kernels for 39%

profile of v6, /device:TPU:0, one launch (start us, length us, event | category | flops | bytes accessed | tf_op | source)
XLA Modules:
  0.0 24.1 jit_solution(4123987771963103408)
XLA Ops:
  0.6 0.0 copy-start.4
  0.6 0.0 copy-start
  0.7 0.0 copy-start.3
  0.7 0.0 copy-start.1
  0.7 0.0 copy-start.5
  0.7 0.0 copy-start.2
  0.7 2.4 %collective-permute-start.5 = (bf16[1,64,576]{2,1,0:T(8,128)(2,1)}, bf16[1,64,576]{2,1,0:T(8,128)(2,1)S(1)}, u32[]{:S(2)}, u32[]{:S(2)}) collective-permute-start(bf16[1,64,576]{2,1,0:T(8,128)(2,1)} %refs_0_.1), channel_id=1, source_target_pairs={{0,3},{1,2},{2,1},{3,0},{4,7},{5,6},{6,5},{7,4},{8,11},{9,10},{10,... | collective-permute-start | bytes 221192 | tf_op jit(solution)/shard_map/ppermute | solution.py:360
  3.1 0.6 %collective-permute-start.4 = (bf16[1,64,576]{2,1,0:T(8,128)(2,1)}, bf16[1,64,576]{2,1,0:T(8,128)(2,1)S(1)}, u32[]{:S(2)}, u32[]{:S(2)}) collective-permute-start(bf16[1,64,576]{2,1,0:T(8,128)(2,1)} %refs_0_.1), channel_id=1, source_target_pairs={{0,2},{1,3},{2,0},{3,1},{4,6},{5,7},{6,4},{7,5},{8,10},{9,11},{10,... | collective-permute-start | bytes 221192 | tf_op jit(solution)/shard_map/ppermute | solution.py:360
  3.8 0.0 collective-permute-start.3
  3.8 1.6 %pick_prefix.1 = (bf16[1,48,576]{2,1,0:T(8,128)(2,1)}, bf16[1,48,576]{2,1,0:T(8,128)(2,1)}, bf16[1,48,576]{2,1,0:T(8,128)(2,1)}) custom-call(s32[4]{0:T(128)} %queue.3, s32[4]{0:T(128)} %dest.3, bf16[4,32,576]{2,1,0:T(8,128)(2,1)} %cache.7), custom_call_target="tpu_custom_call" | custom-call | flops 4000000000 | bytes 10000000 | tf_op jit(solution)/shard_map/pick_prefix/pallas_call | solution.py:341
  5.4 1.9 %collective-permute-start = (bf16[1,48,576]{2,1,0:T(8,128)(2,1)}, bf16[1,48,576]{2,1,0:T(8,128)(2,1)S(1)}, u32[]{:S(2)}, u32[]{:S(2)}) collective-permute-start(bf16[1,48,576]{2,1,0:T(8,128)(2,1)} %get-tuple-element.9), channel_id=1, source_target_pairs={{0,4},{4,8},{8,12},{12,0},{1,5},{5,9},{9,13},{13,1},{2,6},{6,10},{... | collective-permute-start | bytes 165896 | tf_op jit(solution)/shard_map/ppermute | solution.py:335
  7.3 2.6 %collective-permute-start.1 = (bf16[1,48,576]{2,1,0:T(8,128)(2,1)}, bf16[1,48,576]{2,1,0:T(8,128)(2,1)S(1)}, u32[]{:S(2)}, u32[]{:S(2)}) collective-permute-start(bf16[1,48,576]{2,1,0:T(8,128)(2,1)} %get-tuple-element.10), channel_id=1, source_target_pairs={{0,8},{4,12},{8,0},{12,4},{1,9},{5,13},{9,1},{13,5},{2,10},{6,14},... | collective-permute-start | bytes 165896 | tf_op jit(solution)/shard_map/ppermute | solution.py:335
  9.9 0.0 collective-permute-done.5.refs_6_.refs_3_
  9.9 0.0 slice-start
  9.9 0.0 slice-start.1
  9.9 1.3 %collective-permute-start.2 = (bf16[1,48,576]{2,1,0:T(8,128)(2,1)}, bf16[1,48,576]{2,1,0:T(8,128)(2,1)S(1)}, u32[]{:S(2)}, u32[]{:S(2)}) collective-permute-start(bf16[1,48,576]{2,1,0:T(8,128)(2,1)} %get-tuple-element.11), channel_id=1, source_target_pairs={{0,12},{4,0},{8,4},{12,8},{1,13},{5,1},{9,5},{13,9},{2,14},{6,2},{... | collective-permute-start | bytes 165896 | tf_op jit(solution)/shard_map/ppermute | solution.py:335
  11.3 0.0 collective-permute-done.4.refs_5_.refs_2_
  11.3 0.0 collective-permute-done.3.refs_4_.refs_1_
  11.3 0.0 copy-done.4
  11.3 0.0 copy-done
  11.3 0.0 copy-done.3
  11.3 0.0 copy-done.1
  11.3 0.0 copy-done.5
  11.3 0.0 copy-done.2
  11.3 0.7 %build_new.1 = (bf16[1,64,576]{2,1,0:T(8,128)(2,1)S(1)}, bf16[1,80,576]{2,1,0:T(8,128)(2,1)S(1)}, bf16[1,80,576]{2,1,0:T(8,128)(2,1)S(1)}, bf16[1,80,576]{2,1,0:T(8,128)(2,1)S(1)}) custom-call(s32[4]{0:T(128)S(1)} %copy-done.1, s32[4]{0:T(128)S(1)} %copy-done.2, s32[4]{0:T(128)S(1)} %copy-done.5, s32[4]{0:T(128)S(1)} %copy-done.3, ...), custom_call_target="tpu_custom_call" | custom-call | flops 4000000000 | bytes 10000000 | tf_op jit(solution)/shard_map/build_new/pallas_call | solution.py:375
  12.1 0.7 %collective-permute-start.6 = (bf16[1,80,576]{2,1,0:T(8,128)(2,1)S(1)}, bf16[1,80,576]{2,1,0:T(8,128)(2,1)S(1)}, u32[]{:S(2)}, u32[]{:S(2)}) collective-permute-start(bf16[1,80,576]{2,1,0:T(8,128)(2,1)S(1)} %get-tuple-element.13), channel_id=1, source_target_pairs={{0,4},{4,8},{8,12},{12,0},{1,5},{5,9},{9,13},{13,1},{2,6},{6,10},{... | collective-permute-start | bytes 276488 | tf_op jit(solution)/shard_map/ppermute | solution.py:335
  12.8 1.1 %collective-permute-start.7 = (bf16[1,80,576]{2,1,0:T(8,128)(2,1)S(1)}, bf16[1,80,576]{2,1,0:T(8,128)(2,1)S(1)}, u32[]{:S(2)}, u32[]{:S(2)}) collective-permute-start(bf16[1,80,576]{2,1,0:T(8,128)(2,1)S(1)} %get-tuple-element.14), channel_id=1, source_target_pairs={{0,8},{4,12},{8,0},{12,4},{1,9},{5,13},{9,1},{13,5},{2,10},{6,14},... | collective-permute-start | bytes 276488 | tf_op jit(solution)/shard_map/ppermute | solution.py:335
  13.9 0.0 collective-permute-done.refs_0_
  13.9 2.0 %collective-permute-start.8 = (bf16[1,80,576]{2,1,0:T(8,128)(2,1)S(1)}, bf16[1,80,576]{2,1,0:T(8,128)(2,1)S(1)}, u32[]{:S(2)}, u32[]{:S(2)}) collective-permute-start(bf16[1,80,576]{2,1,0:T(8,128)(2,1)S(1)} %get-tuple-element.15), channel_id=1, source_target_pairs={{0,12},{4,0},{8,4},{12,8},{1,13},{5,1},{9,5},{13,9},{2,14},{6,2},{... | collective-permute-start | bytes 276488 | tf_op jit(solution)/shard_map/ppermute | solution.py:335
  16.0 0.0 collective-permute-done.1.refs_1_
  16.0 0.0 collective-permute-done.2.refs_2_
  16.0 0.0 slice-done
  16.0 0.0 slice-done.1
  16.0 7.0 %attend.1 = bf16[1,128,16384]{2,1,0:T(8,128)(2,1)} custom-call(s32[1,4]{1,0:T(1,128)S(1)} %bitcast.5, s32[1,4]{1,0:T(1,128)S(1)} %bitcast.7, s32[1,4]{1,0:T(1,128)S(1)} %bitcast.12, bf16[1,128,18432]{2,1,0:T(8,128)(2,1)S(1)} %bitcast.11, bf16[4,32,576]{2,1,0:T(8,128)(2,1)S(1)} %copy-done, bf16[1,48,576]{2,1,0:T(8,128)(2,1)S(1)} %collective-permute-done.refs_0_, ...), custom_call_target="tpu_custom_call" | custom-call | flops 3422552064 | bytes 8912896 | tf_op jit(solution)/shard_map/attend/pallas_call | solution.py:396
  23.0 0.0 collective-permute-done.6.refs_4_
  23.0 0.0 collective-permute-done.7.refs_5_
  23.0 0.0 collective-permute-done.8.refs_6_
  23.0 1.1 %land_slots.1 = bf16[1,2,96,576]{3,2,1,0:T(8,128)(2,1)} custom-call(s32[1,4]{1,0:T(1,128)S(1)} %bitcast.6, s32[1,4]{1,0:T(1,128)S(1)} %bitcast.8, s32[1,4]{1,0:T(1,128)S(1)} %bitcast.9, bf16[4,32,576]{2,1,0:T(8,128)(2,1)S(1)} %copy-done, bf16[1,48,576]{2,1,0:T(8,128)(2,1)S(1)} %collective-permute-done.refs_0_, ...), custom_call_target="tpu_custom_call" | custom-call | tf_op jit(solution)/shard_map/land_slots/pallas_call | solution.py:423
  (1 shorter events, 0.0 us)
Async XLA Ops:
  0.6 10.6 %copy-start.4 = (bf16[1,64,576]{2,1,0:T(8,128)(2,1)S(1)}, bf16[1,64,576]{2,1,0:T(8,128)(2,1)}, u32[]{:S(2)}) copy-start(bf16[1,64,576]{2,1,0:T(8,128)(2,1)} %refs_0_.1) | copy-start | bytes 221188
  0.6 10.6 %copy-start = (bf16[4,32,576]{2,1,0:T(8,128)(2,1)S(1)}, bf16[4,32,576]{2,1,0:T(8,128)(2,1)}, u32[]{:S(2)}) copy-start(bf16[4,32,576]{2,1,0:T(8,128)(2,1)} %cache.7) | copy-start | bytes 442372
  0.7 10.6 %copy-start.3 = (s32[4]{0:T(128)S(1)}, s32[4]{0:T(128)}, u32[]{:S(2)}) copy-start(s32[4]{0:T(128)} %dest.3) | copy-start | bytes 52
  0.7 10.6 %copy-start.1 = (s32[4]{0:T(128)S(1)}, s32[4]{0:T(128)}, u32[]{:S(2)}) copy-start(s32[4]{0:T(128)} %queue.3) | copy-start | bytes 52
  0.7 10.6 %copy-start.5 = (s32[4]{0:T(128)S(1)}, s32[4]{0:T(128)}, u32[]{:S(2)}) copy-start(s32[4]{0:T(128)} %blk_len.1) | copy-start | bytes 52
  0.7 10.6 %copy-start.2 = (s32[4]{0:T(128)S(1)}, s32[4]{0:T(128)}, u32[]{:S(2)}) copy-start(s32[4]{0:T(128)} %pre_len.1) | copy-start | bytes 52
  0.7 9.2 %collective-permute-start.5 = (bf16[1,64,576]{2,1,0:T(8,128)(2,1)}, bf16[1,64,576]{2,1,0:T(8,128)(2,1)S(1)}, u32[]{:S(2)}, u32[]{:S(2)}) collective-permute-start(bf16[1,64,576]{2,1,0:T(8,128)(2,1)} %refs_0_.1), channel_id=1, source_target_pairs={{0,3},{1,2},{2,1},{3,0},{4,7},{5,6},{6,5},{7,4},{8,11},{9,10},{10,... | collective-permute-start | bytes 221192 | tf_op jit(solution)/shard_map/ppermute | solution.py:360
  3.1 8.1 %collective-permute-start.4 = (bf16[1,64,576]{2,1,0:T(8,128)(2,1)}, bf16[1,64,576]{2,1,0:T(8,128)(2,1)S(1)}, u32[]{:S(2)}, u32[]{:S(2)}) collective-permute-start(bf16[1,64,576]{2,1,0:T(8,128)(2,1)} %refs_0_.1), channel_id=1, source_target_pairs={{0,2},{1,3},{2,0},{3,1},{4,6},{5,7},{6,4},{7,5},{8,10},{9,11},{10,... | collective-permute-start | bytes 221192 | tf_op jit(solution)/shard_map/ppermute | solution.py:360
  3.8 7.5 %collective-permute-start.3 = (bf16[1,64,576]{2,1,0:T(8,128)(2,1)}, bf16[1,64,576]{2,1,0:T(8,128)(2,1)S(1)}, u32[]{:S(2)}, u32[]{:S(2)}) collective-permute-start(bf16[1,64,576]{2,1,0:T(8,128)(2,1)} %refs_0_.1), channel_id=1, source_target_pairs={{0,1},{1,0},{2,3},{3,2},{4,5},{5,4},{6,7},{7,6},{8,9},{9,8},{10,11... | collective-permute-start | bytes 221192 | tf_op jit(solution)/shard_map/ppermute | solution.py:360
  5.4 8.5 %collective-permute-start = (bf16[1,48,576]{2,1,0:T(8,128)(2,1)}, bf16[1,48,576]{2,1,0:T(8,128)(2,1)S(1)}, u32[]{:S(2)}, u32[]{:S(2)}) collective-permute-start(bf16[1,48,576]{2,1,0:T(8,128)(2,1)} %get-tuple-element.9), channel_id=1, source_target_pairs={{0,4},{4,8},{8,12},{12,0},{1,5},{5,9},{9,13},{13,1},{2,6},{6,10},{... | collective-permute-start | bytes 165896 | tf_op jit(solution)/shard_map/ppermute | solution.py:335
  7.3 8.6 %collective-permute-start.1 = (bf16[1,48,576]{2,1,0:T(8,128)(2,1)}, bf16[1,48,576]{2,1,0:T(8,128)(2,1)S(1)}, u32[]{:S(2)}, u32[]{:S(2)}) collective-permute-start(bf16[1,48,576]{2,1,0:T(8,128)(2,1)} %get-tuple-element.10), channel_id=1, source_target_pairs={{0,8},{4,12},{8,0},{12,4},{1,9},{5,13},{9,1},{13,5},{2,10},{6,14},... | collective-permute-start | bytes 165896 | tf_op jit(solution)/shard_map/ppermute | solution.py:335
  9.9 6.1 %slice-start = ((s8[4718592]{0:T(1024)(128)(4,1)}), s8[4194304]{0:T(1024)(128)(4,1)S(1)}, s32[]{:S(2)}) async-start(s8[4718592]{0:T(1024)(128)(4,1)} %bitcast.10), calls=%async_computation | async-start | bytes 8388608
  9.9 6.1 %slice-start.1 = ((s8[4718592]{0:T(1024)(128)(4,1)}), s8[524288]{0:T(1024)(128)(4,1)S(1)}, s32[]{:S(2)}) async-start(s8[4718592]{0:T(1024)(128)(4,1)} %bitcast.10), calls=%async_computation.1 | async-start | bytes 1048576
  9.9 6.1 %collective-permute-start.2 = (bf16[1,48,576]{2,1,0:T(8,128)(2,1)}, bf16[1,48,576]{2,1,0:T(8,128)(2,1)S(1)}, u32[]{:S(2)}, u32[]{:S(2)}) collective-permute-start(bf16[1,48,576]{2,1,0:T(8,128)(2,1)} %get-tuple-element.11), channel_id=1, source_target_pairs={{0,12},{4,0},{8,4},{12,8},{1,13},{5,1},{9,5},{13,9},{2,14},{6,2},{... | collective-permute-start | bytes 165896 | tf_op jit(solution)/shard_map/ppermute | solution.py:335
  12.1 10.9 %collective-permute-start.6 = (bf16[1,80,576]{2,1,0:T(8,128)(2,1)S(1)}, bf16[1,80,576]{2,1,0:T(8,128)(2,1)S(1)}, u32[]{:S(2)}, u32[]{:S(2)}) collective-permute-start(bf16[1,80,576]{2,1,0:T(8,128)(2,1)S(1)} %get-tuple-element.13), channel_id=1, source_target_pairs={{0,4},{4,8},{8,12},{12,0},{1,5},{5,9},{9,13},{13,1},{2,6},{6,10},{... | collective-permute-start | bytes 276488 | tf_op jit(solution)/shard_map/ppermute | solution.py:335
  12.8 10.2 %collective-permute-start.7 = (bf16[1,80,576]{2,1,0:T(8,128)(2,1)S(1)}, bf16[1,80,576]{2,1,0:T(8,128)(2,1)S(1)}, u32[]{:S(2)}, u32[]{:S(2)}) collective-permute-start(bf16[1,80,576]{2,1,0:T(8,128)(2,1)S(1)} %get-tuple-element.14), channel_id=1, source_target_pairs={{0,8},{4,12},{8,0},{12,4},{1,9},{5,13},{9,1},{13,5},{2,10},{6,14},... | collective-permute-start | bytes 276488 | tf_op jit(solution)/shard_map/ppermute | solution.py:335
  13.9 9.0 %collective-permute-start.8 = (bf16[1,80,576]{2,1,0:T(8,128)(2,1)S(1)}, bf16[1,80,576]{2,1,0:T(8,128)(2,1)S(1)}, u32[]{:S(2)}, u32[]{:S(2)}) collective-permute-start(bf16[1,80,576]{2,1,0:T(8,128)(2,1)S(1)} %get-tuple-element.15), channel_id=1, source_target_pairs={{0,12},{4,0},{8,4},{12,8},{1,13},{5,1},{9,5},{13,9},{2,14},{6,2},{... | collective-permute-start | bytes 276488 | tf_op jit(solution)/shard_map/ppermute | solution.py:335

commit v7 on v6

--- a/solution.py
+++ b/solution.py
@@ -279,9 +279,7 @@
         columns = pl.ds(head * LAT, LAT)
         return pltpu.make_async_copy(held.at[:, columns], out.at[0, :, columns], signals.at[head])
 
-    def work(pair, odd, seen):
-        values = even_keys[:seen, :LAT]
-        mask = bias[:, :seen]
+    def work(pair, odd, seen, values, mask):
         starts = [(pair + p) * PAIR_W + odd * LAT for p in range(pairs)]
         scores = lax.dot_general(
             jnp.concatenate([queries[0, :, at : at + WIDE] for at in starts], axis=0),
@@ -304,9 +302,11 @@
 
         @pl.when(lax.axis_index("sp") == part)
         def _(part=part):
+            seen = first + (part + 1) * count
+            values, mask = even_keys[:seen, :LAT], bias[:, :seen]
             for pair in range(0, heads // 2, pairs):
                 for odd in (0, 1):
-                    work(pair, odd, first + (part + 1) * count)
+                    work(pair, odd, seen, values, mask)
 
     for head in range(heads):
         leaving(head).wait()

time: 24.2 us -> 24.2 us (level)
  no operation moved by 1% of the time
where the time goes in v7:
time: 24.2 us; the launch traced here: 24.1 us
  starting transfers between devices  12.8 us (53%)
  Pallas kernels  10.4 us (43%)
  between operations  0.8 us (3%)
    ppermute x6, starting transfers between devices, moved(): return lax.ppermute(piece, 'pool', pairs)  9.7 us
    pallas_call x1, Pallas kernels, body(): pl.pallas_call(functools.partial(attend, sources=sources, pre_count=len(p...  6.97 us
    ppermute x3, starting transfers between devices, body(): lax.ppermute(block_latent, ('tp', 'sp'), [(i, i ^ s) for i in range(lanes)])  3.12 us
    pallas_call x1, Pallas kernels, body(): pl.pallas_call(pick_prefix, in_specs=[hbm] * 3, out_specs=[vmem] * pieces...  1.61 us
    pallas_call x1, Pallas kernels, body(): land(functools.partial(land_slots, sources=sources), in_specs=[vmem] * (4...  1.1 us
    pallas_call x1, Pallas kernels, body(): build(functools.partial(build_new, sources=sources), in_specs=[smem] * 4...  0.75 us
  transfers between devices with their start and end apart: 9, of which 0 were waited for; matrix products, arithmetic and copies ran while one was open for 0% of the time, Pallas kernels for 39%

profile of v7, /device:TPU:0, one launch (start us, length us, event | category | flops | bytes accessed | tf_op | source)
XLA Modules:
  0.0 24.1 jit_solution(6201701620426384202)
XLA Ops:
  0.6 0.0 copy-start.4
  0.6 0.0 copy-start
  0.7 0.0 copy-start.3
  0.7 0.0 copy-start.1
  0.7 0.0 copy-start.5
  0.7 0.0 copy-start.2
  0.7 2.4 %collective-permute-start.5 = (bf16[1,64,576]{2,1,0:T(8,128)(2,1)}, bf16[1,64,576]{2,1,0:T(8,128)(2,1)S(1)}, u32[]{:S(2)}, u32[]{:S(2)}) collective-permute-start(bf16[1,64,576]{2,1,0:T(8,128)(2,1)} %refs_0_.1), channel_id=1, source_target_pairs={{0,3},{1,2},{2,1},{3,0},{4,7},{5,6},{6,5},{7,4},{8,11},{9,10},{10,... | collective-permute-start | bytes 221192 | tf_op jit(solution)/shard_map/ppermute | solution.py:360
  3.1 0.6 %collective-permute-start.4 = (bf16[1,64,576]{2,1,0:T(8,128)(2,1)}, bf16[1,64,576]{2,1,0:T(8,128)(2,1)S(1)}, u32[]{:S(2)}, u32[]{:S(2)}) collective-permute-start(bf16[1,64,576]{2,1,0:T(8,128)(2,1)} %refs_0_.1), channel_id=1, source_target_pairs={{0,2},{1,3},{2,0},{3,1},{4,6},{5,7},{6,4},{7,5},{8,10},{9,11},{10,... | collective-permute-start | bytes 221192 | tf_op jit(solution)/shard_map/ppermute | solution.py:360
  3.8 0.0 collective-permute-start.3
  3.8 1.6 %pick_prefix.1 = (bf16[1,48,576]{2,1,0:T(8,128)(2,1)}, bf16[1,48,576]{2,1,0:T(8,128)(2,1)}, bf16[1,48,576]{2,1,0:T(8,128)(2,1)}) custom-call(s32[4]{0:T(128)} %queue.3, s32[4]{0:T(128)} %dest.3, bf16[4,32,576]{2,1,0:T(8,128)(2,1)} %cache.7), custom_call_target="tpu_custom_call" | custom-call | flops 4000000000 | bytes 10000000 | tf_op jit(solution)/shard_map/pick_prefix/pallas_call | solution.py:341
  5.4 1.9 %collective-permute-start = (bf16[1,48,576]{2,1,0:T(8,128)(2,1)}, bf16[1,48,576]{2,1,0:T(8,128)(2,1)S(1)}, u32[]{:S(2)}, u32[]{:S(2)}) collective-permute-start(bf16[1,48,576]{2,1,0:T(8,128)(2,1)} %get-tuple-element.9), channel_id=1, source_target_pairs={{0,4},{4,8},{8,12},{12,0},{1,5},{5,9},{9,13},{13,1},{2,6},{6,10},{... | collective-permute-start | bytes 165896 | tf_op jit(solution)/shard_map/ppermute | solution.py:335
  7.3 2.6 %collective-permute-start.1 = (bf16[1,48,576]{2,1,0:T(8,128)(2,1)}, bf16[1,48,576]{2,1,0:T(8,128)(2,1)S(1)}, u32[]{:S(2)}, u32[]{:S(2)}) collective-permute-start(bf16[1,48,576]{2,1,0:T(8,128)(2,1)} %get-tuple-element.10), channel_id=1, source_target_pairs={{0,8},{4,12},{8,0},{12,4},{1,9},{5,13},{9,1},{13,5},{2,10},{6,14},... | collective-permute-start | bytes 165896 | tf_op jit(solution)/shard_map/ppermute | solution.py:335
  9.9 0.0 collective-permute-done.5.refs_6_.refs_3_
  9.9 0.0 slice-start
  9.9 0.0 slice-start.1
  9.9 1.3 %collective-permute-start.2 = (bf16[1,48,576]{2,1,0:T(8,128)(2,1)}, bf16[1,48,576]{2,1,0:T(8,128)(2,1)S(1)}, u32[]{:S(2)}, u32[]{:S(2)}) collective-permute-start(bf16[1,48,576]{2,1,0:T(8,128)(2,1)} %get-tuple-element.11), channel_id=1, source_target_pairs={{0,12},{4,0},{8,4},{12,8},{1,13},{5,1},{9,5},{13,9},{2,14},{6,2},{... | collective-permute-start | bytes 165896 | tf_op jit(solution)/shard_map/ppermute | solution.py:335
  11.3 0.0 collective-permute-done.4.refs_5_.refs_2_
  11.3 0.0 collective-permute-done.3.refs_4_.refs_1_
  11.3 0.0 copy-done.4
  11.3 0.0 copy-done
  11.3 0.0 copy-done.3
  11.3 0.0 copy-done.1
  11.3 0.0 copy-done.5
  11.3 0.0 copy-done.2
  11.3 0.7 %build_new.1 = (bf16[1,64,576]{2,1,0:T(8,128)(2,1)S(1)}, bf16[1,80,576]{2,1,0:T(8,128)(2,1)S(1)}, bf16[1,80,576]{2,1,0:T(8,128)(2,1)S(1)}, bf16[1,80,576]{2,1,0:T(8,128)(2,1)S(1)}) custom-call(s32[4]{0:T(128)S(1)} %copy-done.1, s32[4]{0:T(128)S(1)} %copy-done.2, s32[4]{0:T(128)S(1)} %copy-done.5, s32[4]{0:T(128)S(1)} %copy-done.3, ...), custom_call_target="tpu_custom_call" | custom-call | flops 4000000000 | bytes 10000000 | tf_op jit(solution)/shard_map/build_new/pallas_call | solution.py:375
  12.1 0.7 %collective-permute-start.6 = (bf16[1,80,576]{2,1,0:T(8,128)(2,1)S(1)}, bf16[1,80,576]{2,1,0:T(8,128)(2,1)S(1)}, u32[]{:S(2)}, u32[]{:S(2)}) collective-permute-start(bf16[1,80,576]{2,1,0:T(8,128)(2,1)S(1)} %get-tuple-element.13), channel_id=1, source_target_pairs={{0,4},{4,8},{8,12},{12,0},{1,5},{5,9},{9,13},{13,1},{2,6},{6,10},{... | collective-permute-start | bytes 276488 | tf_op jit(solution)/shard_map/ppermute | solution.py:335
  12.8 1.1 %collective-permute-start.7 = (bf16[1,80,576]{2,1,0:T(8,128)(2,1)S(1)}, bf16[1,80,576]{2,1,0:T(8,128)(2,1)S(1)}, u32[]{:S(2)}, u32[]{:S(2)}) collective-permute-start(bf16[1,80,576]{2,1,0:T(8,128)(2,1)S(1)} %get-tuple-element.14), channel_id=1, source_target_pairs={{0,8},{4,12},{8,0},{12,4},{1,9},{5,13},{9,1},{13,5},{2,10},{6,14},... | collective-permute-start | bytes 276488 | tf_op jit(solution)/shard_map/ppermute | solution.py:335
  13.9 0.0 collective-permute-done.refs_0_
  13.9 2.0 %collective-permute-start.8 = (bf16[1,80,576]{2,1,0:T(8,128)(2,1)S(1)}, bf16[1,80,576]{2,1,0:T(8,128)(2,1)S(1)}, u32[]{:S(2)}, u32[]{:S(2)}) collective-permute-start(bf16[1,80,576]{2,1,0:T(8,128)(2,1)S(1)} %get-tuple-element.15), channel_id=1, source_target_pairs={{0,12},{4,0},{8,4},{12,8},{1,13},{5,1},{9,5},{13,9},{2,14},{6,2},{... | collective-permute-start | bytes 276488 | tf_op jit(solution)/shard_map/ppermute | solution.py:335
  16.0 0.0 collective-permute-done.1.refs_1_
  16.0 0.0 collective-permute-done.2.refs_2_
  16.0 0.0 slice-done
  16.0 0.0 slice-done.1
  16.0 7.0 %attend.1 = bf16[1,128,16384]{2,1,0:T(8,128)(2,1)} custom-call(s32[1,4]{1,0:T(1,128)S(1)} %bitcast.5, s32[1,4]{1,0:T(1,128)S(1)} %bitcast.7, s32[1,4]{1,0:T(1,128)S(1)} %bitcast.12, bf16[1,128,18432]{2,1,0:T(8,128)(2,1)S(1)} %bitcast.11, bf16[4,32,576]{2,1,0:T(8,128)(2,1)S(1)} %copy-done, bf16[1,48,576]{2,1,0:T(8,128)(2,1)S(1)} %collective-permute-done.refs_0_, ...), custom_call_target="tpu_custom_call" | custom-call | flops 3422552064 | bytes 8912896 | tf_op jit(solution)/shard_map/attend/pallas_call | solution.py:396
  23.0 0.0 collective-permute-done.6.refs_4_
  23.0 0.0 collective-permute-done.7.refs_5_
  23.0 0.0 collective-permute-done.8.refs_6_
  23.0 1.1 %land_slots.1 = bf16[1,2,96,576]{3,2,1,0:T(8,128)(2,1)} custom-call(s32[1,4]{1,0:T(1,128)S(1)} %bitcast.6, s32[1,4]{1,0:T(1,128)S(1)} %bitcast.8, s32[1,4]{1,0:T(1,128)S(1)} %bitcast.9, bf16[4,32,576]{2,1,0:T(8,128)(2,1)S(1)} %copy-done, bf16[1,48,576]{2,1,0:T(8,128)(2,1)S(1)} %collective-permute-done.refs_0_, ...), custom_call_target="tpu_custom_call" | custom-call | tf_op jit(solution)/shard_map/land_slots/pallas_call | solution.py:423
  (1 shorter events, 0.0 us)
Async XLA Ops:
  0.6 10.6 %copy-start.4 = (bf16[1,64,576]{2,1,0:T(8,128)(2,1)S(1)}, bf16[1,64,576]{2,1,0:T(8,128)(2,1)}, u32[]{:S(2)}) copy-start(bf16[1,64,576]{2,1,0:T(8,128)(2,1)} %refs_0_.1) | copy-start | bytes 221188
  0.6 10.6 %copy-start = (bf16[4,32,576]{2,1,0:T(8,128)(2,1)S(1)}, bf16[4,32,576]{2,1,0:T(8,128)(2,1)}, u32[]{:S(2)}) copy-start(bf16[4,32,576]{2,1,0:T(8,128)(2,1)} %cache.7) | copy-start | bytes 442372
  0.7 10.6 %copy-start.3 = (s32[4]{0:T(128)S(1)}, s32[4]{0:T(128)}, u32[]{:S(2)}) copy-start(s32[4]{0:T(128)} %dest.3) | copy-start | bytes 52
  0.7 10.6 %copy-start.1 = (s32[4]{0:T(128)S(1)}, s32[4]{0:T(128)}, u32[]{:S(2)}) copy-start(s32[4]{0:T(128)} %queue.3) | copy-start | bytes 52
  0.7 10.6 %copy-start.5 = (s32[4]{0:T(128)S(1)}, s32[4]{0:T(128)}, u32[]{:S(2)}) copy-start(s32[4]{0:T(128)} %blk_len.1) | copy-start | bytes 52
  0.7 10.6 %copy-start.2 = (s32[4]{0:T(128)S(1)}, s32[4]{0:T(128)}, u32[]{:S(2)}) copy-start(s32[4]{0:T(128)} %pre_len.1) | copy-start | bytes 52
  0.7 9.2 %collective-permute-start.5 = (bf16[1,64,576]{2,1,0:T(8,128)(2,1)}, bf16[1,64,576]{2,1,0:T(8,128)(2,1)S(1)}, u32[]{:S(2)}, u32[]{:S(2)}) collective-permute-start(bf16[1,64,576]{2,1,0:T(8,128)(2,1)} %refs_0_.1), channel_id=1, source_target_pairs={{0,3},{1,2},{2,1},{3,0},{4,7},{5,6},{6,5},{7,4},{8,11},{9,10},{10,... | collective-permute-start | bytes 221192 | tf_op jit(solution)/shard_map/ppermute | solution.py:360
  3.1 8.1 %collective-permute-start.4 = (bf16[1,64,576]{2,1,0:T(8,128)(2,1)}, bf16[1,64,576]{2,1,0:T(8,128)(2,1)S(1)}, u32[]{:S(2)}, u32[]{:S(2)}) collective-permute-start(bf16[1,64,576]{2,1,0:T(8,128)(2,1)} %refs_0_.1), channel_id=1, source_target_pairs={{0,2},{1,3},{2,0},{3,1},{4,6},{5,7},{6,4},{7,5},{8,10},{9,11},{10,... | collective-permute-start | bytes 221192 | tf_op jit(solution)/shard_map/ppermute | solution.py:360
  3.8 7.5 %collective-permute-start.3 = (bf16[1,64,576]{2,1,0:T(8,128)(2,1)}, bf16[1,64,576]{2,1,0:T(8,128)(2,1)S(1)}, u32[]{:S(2)}, u32[]{:S(2)}) collective-permute-start(bf16[1,64,576]{2,1,0:T(8,128)(2,1)} %refs_0_.1), channel_id=1, source_target_pairs={{0,1},{1,0},{2,3},{3,2},{4,5},{5,4},{6,7},{7,6},{8,9},{9,8},{10,11... | collective-permute-start | bytes 221192 | tf_op jit(solution)/shard_map/ppermute | solution.py:360
  5.4 8.5 %collective-permute-start = (bf16[1,48,576]{2,1,0:T(8,128)(2,1)}, bf16[1,48,576]{2,1,0:T(8,128)(2,1)S(1)}, u32[]{:S(2)}, u32[]{:S(2)}) collective-permute-start(bf16[1,48,576]{2,1,0:T(8,128)(2,1)} %get-tuple-element.9), channel_id=1, source_target_pairs={{0,4},{4,8},{8,12},{12,0},{1,5},{5,9},{9,13},{13,1},{2,6},{6,10},{... | collective-permute-start | bytes 165896 | tf_op jit(solution)/shard_map/ppermute | solution.py:335
  7.3 8.6 %collective-permute-start.1 = (bf16[1,48,576]{2,1,0:T(8,128)(2,1)}, bf16[1,48,576]{2,1,0:T(8,128)(2,1)S(1)}, u32[]{:S(2)}, u32[]{:S(2)}) collective-permute-start(bf16[1,48,576]{2,1,0:T(8,128)(2,1)} %get-tuple-element.10), channel_id=1, source_target_pairs={{0,8},{4,12},{8,0},{12,4},{1,9},{5,13},{9,1},{13,5},{2,10},{6,14},... | collective-permute-start | bytes 165896 | tf_op jit(solution)/shard_map/ppermute | solution.py:335
  9.9 6.1 %slice-start = ((s8[4718592]{0:T(1024)(128)(4,1)}), s8[4194304]{0:T(1024)(128)(4,1)S(1)}, s32[]{:S(2)}) async-start(s8[4718592]{0:T(1024)(128)(4,1)} %bitcast.10), calls=%async_computation | async-start | bytes 8388608
  9.9 6.1 %slice-start.1 = ((s8[4718592]{0:T(1024)(128)(4,1)}), s8[524288]{0:T(1024)(128)(4,1)S(1)}, s32[]{:S(2)}) async-start(s8[4718592]{0:T(1024)(128)(4,1)} %bitcast.10), calls=%async_computation.1 | async-start | bytes 1048576
  9.9 6.1 %collective-permute-start.2 = (bf16[1,48,576]{2,1,0:T(8,128)(2,1)}, bf16[1,48,576]{2,1,0:T(8,128)(2,1)S(1)}, u32[]{:S(2)}, u32[]{:S(2)}) collective-permute-start(bf16[1,48,576]{2,1,0:T(8,128)(2,1)} %get-tuple-element.11), channel_id=1, source_target_pairs={{0,12},{4,0},{8,4},{12,8},{1,13},{5,1},{9,5},{13,9},{2,14},{6,2},{... | collective-permute-start | bytes 165896 | tf_op jit(solution)/shard_map/ppermute | solution.py:335
  12.1 10.9 %collective-permute-start.6 = (bf16[1,80,576]{2,1,0:T(8,128)(2,1)S(1)}, bf16[1,80,576]{2,1,0:T(8,128)(2,1)S(1)}, u32[]{:S(2)}, u32[]{:S(2)}) collective-permute-start(bf16[1,80,576]{2,1,0:T(8,128)(2,1)S(1)} %get-tuple-element.13), channel_id=1, source_target_pairs={{0,4},{4,8},{8,12},{12,0},{1,5},{5,9},{9,13},{13,1},{2,6},{6,10},{... | collective-permute-start | bytes 276488 | tf_op jit(solution)/shard_map/ppermute | solution.py:335
  12.8 10.2 %collective-permute-start.7 = (bf16[1,80,576]{2,1,0:T(8,128)(2,1)S(1)}, bf16[1,80,576]{2,1,0:T(8,128)(2,1)S(1)}, u32[]{:S(2)}, u32[]{:S(2)}) collective-permute-start(bf16[1,80,576]{2,1,0:T(8,128)(2,1)S(1)} %get-tuple-element.14), channel_id=1, source_target_pairs={{0,8},{4,12},{8,0},{12,4},{1,9},{5,13},{9,1},{13,5},{2,10},{6,14},... | collective-permute-start | bytes 276488 | tf_op jit(solution)/shard_map/ppermute | solution.py:335
  13.9 9.0 %collective-permute-start.8 = (bf16[1,80,576]{2,1,0:T(8,128)(2,1)S(1)}, bf16[1,80,576]{2,1,0:T(8,128)(2,1)S(1)}, u32[]{:S(2)}, u32[]{:S(2)}) collective-permute-start(bf16[1,80,576]{2,1,0:T(8,128)(2,1)S(1)} %get-tuple-element.15), channel_id=1, source_target_pairs={{0,12},{4,0},{8,4},{12,8},{1,13},{5,1},{9,5},{13,9},{2,14},{6,2},{... | collective-permute-start | bytes 276488 | tf_op jit(solution)/shard_map/ppermute | solution.py:335
